TPU v7x, 32 devices: a whole 2x2x4 slice. The times are simulated.
32 devices in a mesh: fsdp: 16 (over z, y, x), tp: 2 (over core).
Axes of the slice: x: 2, y: 2, z: 4, core: 2. Of those that a mesh axis runs over, the one named last changes fastest.
Arguments:
- inputs: bfloat16 [2, 16, 256, 2048], P(None, 'fsdp', 'tp'), may hold values from -6 to 6
- cotangent: bfloat16 [2, 16, 256, 2048], P(None, 'fsdp', 'tp'), may hold values from -14 to 14
- joined_master: float32 [3, 2048, 2048], P(None, 'fsdp', 'tp'), may hold values from -0.125 to 0.125
- joined_first: float32 [3, 2048, 2048], P(None, 'fsdp', 'tp'), may hold values from -0.001953125 to 0.001953125
- joined_second: float32 [3, 2048, 2048], P(None, 'fsdp', 'tp'), may hold values from 1.9458863e-08 to 7.783545e-08
- outward_master: float32 [2048, 2048], P('fsdp', 'tp'), may hold values from -0.75 to 0.75
- outward_first: float32 [2048, 2048], P('fsdp', 'tp'), may hold values from -0.001953125 to 0.001953125
- outward_second: float32 [2048, 2048], P('fsdp', 'tp'), may hold values from 1.9458863e-08 to 7.783545e-08
- gated_master: float32 [2, 2048, 5632], P(None, 'fsdp', 'tp'), may hold values from -0.125 to 0.125
- gated_first: float32 [2, 2048, 5632], P(None, 'fsdp', 'tp'), may hold values from -0.001953125 to 0.001953125
- gated_second: float32 [2, 2048, 5632], P(None, 'fsdp', 'tp'), may hold values from 1.9458863e-08 to 7.783545e-08
- downward_master: float32 [2048, 5632], P('fsdp', 'tp'), may hold values from -2 to 2
- downward_first: float32 [2048, 5632], P('fsdp', 'tp'), may hold values from -0.001953125 to 0.001953125
- downward_second: float32 [2048, 5632], P('fsdp', 'tp'), may hold values from 1.9458863e-08 to 7.783545e-08
- vectors_master: float32 [5, 2048], P(None, 'fsdp'), may hold values from -1.5 to 3
- vectors_first: float32 [5, 2048], P(None, 'fsdp'), may hold values from -0.005859375 to 0.005859375
- vectors_second: float32 [5, 2048], P(None, 'fsdp'), may hold values from 1.7512977e-07 to 7.005191e-07
Outputs:
- outputs: bfloat16 [2, 16, 256, 2048], P(None, 'fsdp', 'tp')
- input_grad: bfloat16 [2, 16, 256, 2048], P(None, 'fsdp', 'tp')
- grad_norm: float32 [], replicated
- joined_updated: float32 [3, 2048, 2048], P(None, 'fsdp', 'tp')
- joined_moment: float32 [3, 2048, 2048], P(None, 'fsdp', 'tp')
- joined_variance: float32 [3, 2048, 2048], P(None, 'fsdp', 'tp')
- joined_copy: bfloat16 [3, 2048, 2048], P(None, 'fsdp', 'tp')
- outward_updated: float32 [2048, 2048], P('fsdp', 'tp')
- outward_moment: float32 [2048, 2048], P('fsdp', 'tp')
- outward_variance: float32 [2048, 2048], P('fsdp', 'tp')
- outward_copy: bfloat16 [2048, 2048], P('fsdp', 'tp')
- gated_updated: float32 [2, 2048, 5632], P(None, 'fsdp', 'tp')
- gated_moment: float32 [2, 2048, 5632], P(None, 'fsdp', 'tp')
- gated_variance: float32 [2, 2048, 5632], P(None, 'fsdp', 'tp')
- gated_copy: bfloat16 [2, 2048, 5632], P(None, 'fsdp', 'tp')
- downward_updated: float32 [2048, 5632], P('fsdp', 'tp')
- downward_moment: float32 [2048, 5632], P('fsdp', 'tp')
- downward_variance: float32 [2048, 5632], P('fsdp', 'tp')
- downward_copy: bfloat16 [2048, 5632], P('fsdp', 'tp')
- vectors_updated: float32 [5, 2048], P(None, 'fsdp')
- vectors_moment: float32 [5, 2048], P(None, 'fsdp')
- vectors_variance: float32 [5, 2048], P(None, 'fsdp')
- vectors_copy: bfloat16 [5, 2048], P(None, 'fsdp')
All inputs are finite; a program needn't handle non-finite values.
Results may differ from a plain program's by a relative error of at most 0.012.
The roundings to bfloat16 on the way count: a program that leaves them out, or rounds other values in their place, can miss the bound.
Values may be sent and summed in bfloat16 or wider, within the bound.
No kernel may reach another device: no remote copies, remote signals or barrier semaphores. Data moves between devices by JAX's collectives and lax.ppermute only.
A program may use at most 256 MiB of HBM per device.

v0:
```python
import jax
import jax.numpy as jnp
from jax import lax
from jax.sharding import PartitionSpec as P

D = 2048
HD = 64
ROT = 16
FF = 5632
MICRO = 2
STEP = 5


EPS_NORM = 1e-05
CLIP = 1.0
BETA_ONE = 0.5
BETA_TWO = 0.5
ADAM_EPS = 1e-08
DECAY = 0.1
SMALL_RATE = 0.2
ROPE_BASE = 10000.0


def normalize(row_block, row_gain, row_shift):
    average = jnp.mean(row_block, axis=-1, keepdims=True)
    centred = row_block - average
    variance = jnp.mean(centred * centred, axis=-1, keepdims=True)
    return centred * lax.rsqrt(variance + EPS_NORM) * row_gain + row_shift


def rotary(head_rows, length, rot_dims):
    half_dims = rot_dims // 2
    frequency = ROPE_BASE ** (-(2.0 * jnp.arange(half_dims, dtype=jnp.float32)) / rot_dims)
    angles = jnp.arange(length, dtype=jnp.float32)[:, None] * frequency[None, :]
    cosine_table = jnp.concatenate([jnp.cos(angles), jnp.cos(angles)], axis=-1)[:, None, :]
    sine_table = jnp.concatenate([jnp.sin(angles), jnp.sin(angles)], axis=-1)[:, None, :]
    rotated_part = head_rows[..., :rot_dims]
    first_half = rotated_part[..., :half_dims]
    second_half = rotated_part[..., half_dims:]
    turned = jnp.concatenate([-second_half, first_half], axis=-1)
    return jnp.concatenate(
        [rotated_part * cosine_table + turned * sine_table, head_rows[..., rot_dims:]], axis=-1
    )


def block_scores(query_block, keys, start, scale):
    block_len = query_block.shape[0]
    scores = (
        jnp.einsum("thd,shd->hts", query_block, keys, preferred_element_type=jnp.float32) * scale
    )
    query_pos = start + jnp.arange(block_len)
    key_pos = jnp.arange(keys.shape[0])
    causal = query_pos[:, None] >= key_pos[None, :]
    return jnp.where(causal[None], scores, -jnp.inf)


def attend(query, keys, values, scale):
    length, heads_here, head_size = query.shape
    block_len = min(length, 512)
    block_count = length // block_len

    def one_block(block_index):
        start = block_index * block_len
        scores = block_scores(query, keys, start, scale)
        peak = jnp.max(scores, axis=-1, keepdims=True)
        log_sum = peak + jnp.log(jnp.sum(jnp.exp(scores - peak), axis=-1, keepdims=True))
        probs = jnp.exp(scores - log_sum).astype(jnp.bfloat16)
        mixed = jnp.einsum("hts,shd->thd", probs, values, preferred_element_type=jnp.float32)
        return (mixed, log_sum[..., 0])

    mixed, log_sums = lax.map(one_block, jnp.arange(block_count))
    return (mixed.reshape(length, heads_here, head_size), log_sums)


def attend_back(query, keys, values, mixed_grad, log_sums, scale):
    length = query.shape[0]
    block_len = min(length, 512)
    block_count = length // block_len

    def one_block(carry, block_index):
        keys_acc, values_acc = carry
        start = block_index * block_len
        scores = block_scores(query, keys, start, scale)
        probs = jnp.exp(scores - log_sums[block_index][..., None])
        prob_grad = jnp.einsum(
            "thd,shd->hts", mixed_grad, values, preferred_element_type=jnp.float32
        )
        inner = jnp.sum(probs * prob_grad, axis=-1, keepdims=True)
        score_grad = (probs * (prob_grad - inner)).astype(jnp.bfloat16)
        query_grad = (
            jnp.einsum("hts,shd->thd", score_grad, keys, preferred_element_type=jnp.float32) * scale
        )
        keys_acc = (
            keys_acc
            + jnp.einsum("hts,thd->shd", score_grad, query, preferred_element_type=jnp.float32)
            * scale
        )
        values_acc = values_acc + jnp.einsum(
            "hts,thd->shd",
            probs.astype(jnp.bfloat16),
            mixed_grad,
            preferred_element_type=jnp.float32,
        )
        return ((keys_acc, values_acc), query_grad)

    zero_init = jnp.zeros(keys.shape, jnp.float32)
    (keys_grad, values_grad), query_grads = lax.scan(
        one_block, (zero_init, zero_init), jnp.arange(block_count)
    )
    return (query_grads.reshape(query.shape), keys_grad, values_grad)


def micro_step(own_rows, own_back, weights, tp_index):
    joined_full, outward_full, gated_full, downward_full, vectors_full = weights
    local_width = joined_full.shape[2]
    heads_here = local_width // HD
    model_width = own_rows.shape[1]
    scale = HD ** (-0.5)
    vectors_float = vectors_full.astype(jnp.float32)
    row_gain = vectors_float[0]
    row_shift = vectors_float[1]
    bias_here = lax.dynamic_slice_in_dim(vectors_float[2:5], tp_index * local_width, local_width, 1)
    rows_float = own_rows.astype(jnp.float32)
    normed_own = normalize(rows_float, row_gain, row_shift).astype(jnp.bfloat16)
    normed, back_full = (
        lax.all_gather(normed_own, "tp", axis=0, tiled=True),
        lax.all_gather(own_back, "tp", axis=0, tiled=True),
    )
    length = normed.shape[0]
    joined_out = (
        jnp.einsum("td,cde->cte", normed, joined_full, preferred_element_type=jnp.float32)
        + bias_here[:, None, :]
    )
    heads_all = joined_out.reshape(3, length, heads_here, HD)
    query = rotary(heads_all[0], length, ROT).astype(jnp.bfloat16)
    keys = rotary(heads_all[1], length, ROT).astype(jnp.bfloat16)
    values = heads_all[2].astype(jnp.bfloat16)
    mixed, log_sums = attend(query, keys, values, scale)
    mixed_low = mixed.reshape(length, local_width).astype(jnp.bfloat16)
    attn_part = lax.dot_general(
        mixed_low, outward_full, (((1,), (1,)), ((), ())), preferred_element_type=jnp.float32
    )
    gate_up = jnp.einsum("td,cdf->ctf", normed, gated_full, preferred_element_type=jnp.float32)
    activated = (jax.nn.silu(gate_up[0]) * gate_up[1]).astype(jnp.bfloat16)
    mlp_part = lax.dot_general(
        activated, downward_full, (((1,), (1,)), ((), ())), preferred_element_type=jnp.float32
    )
    branch = lax.psum_scatter(
        (attn_part + mlp_part).astype(jnp.bfloat16), "tp", scatter_dimension=0, tiled=True
    ).astype(jnp.float32)
    output_rows = (rows_float + branch).astype(jnp.bfloat16)
    mixed_grad = jnp.dot(back_full, outward_full, preferred_element_type=jnp.float32).astype(
        jnp.bfloat16
    )
    outward_term = lax.dot_general(
        back_full, mixed_low, (((0,), (0,)), ((), ())), preferred_element_type=jnp.float32
    )
    act_grad = jnp.dot(back_full, downward_full, preferred_element_type=jnp.float32)
    downward_term = lax.dot_general(
        back_full, activated, (((0,), (0,)), ((), ())), preferred_element_type=jnp.float32
    )
    unused_act, act_pull = jax.vjp(
        lambda gate_in, up_in: jax.nn.silu(gate_in) * up_in, gate_up[0], gate_up[1]
    )
    gate_grad, up_grad = act_pull(act_grad)
    gated_grad = jnp.stack([gate_grad, up_grad]).astype(jnp.bfloat16)
    gated_term = jnp.einsum("td,ctf->dcf", normed, gated_grad, preferred_element_type=jnp.float32)
    normed_grad = jnp.einsum(
        "ctf,cdf->td", gated_grad, gated_full, preferred_element_type=jnp.float32
    )
    query_grad, keys_grad, values_grad = attend_back(
        query, keys, values, mixed_grad.reshape(length, heads_here, HD), log_sums, scale
    )
    unused_rot, rot_pull = jax.vjp(lambda head_rows: rotary(head_rows, length, ROT), heads_all[0])
    joined_grad = (
        jnp.stack([rot_pull(query_grad)[0], rot_pull(keys_grad)[0], values_grad])
        .reshape(3, length, local_width)
        .astype(jnp.bfloat16)
    )
    bias_grad = jnp.sum(joined_grad, axis=1, dtype=jnp.float32)
    joined_term = jnp.einsum("td,cte->dce", normed, joined_grad, preferred_element_type=jnp.float32)
    normed_grad = normed_grad + jnp.einsum(
        "cte,cde->td", joined_grad, joined_full, preferred_element_type=jnp.float32
    )
    own_grad = lax.psum_scatter(
        normed_grad.astype(jnp.bfloat16), "tp", scatter_dimension=0, tiled=True
    ).astype(jnp.float32)
    unused_norm, norm_pull = jax.vjp(normalize, rows_float, row_gain, row_shift)
    rows_grad, gain_grad, shift_grad = norm_pull(own_grad)
    input_rows = (own_back.astype(jnp.float32) + rows_grad).astype(jnp.bfloat16)
    bias_full = lax.dynamic_update_slice(
        jnp.zeros((3, model_width), jnp.float32), bias_grad, (0, tp_index * local_width)
    )
    vectors_term = jnp.concatenate([gain_grad[None, :], shift_grad[None, :], bias_full], axis=0).T
    return (
        output_rows,
        input_rows,
        (joined_term, outward_term, gated_term, downward_term, vectors_term),
    )


def restore_layout(reduced):
    joined_part, outward_part, gated_part, downward_part, vectors_part = reduced
    return (
        jnp.moveaxis(joined_part, 0, 1),
        outward_part,
        jnp.moveaxis(gated_part, 0, 1),
        downward_part,
        vectors_part.T,
    )


def adamw(master, first_old, second_old, gradient, factor, step_rate, weight_decay):
    clipped = gradient * factor
    moment = BETA_ONE * first_old + (1.0 - BETA_ONE) * clipped
    variance = BETA_TWO * second_old + (1.0 - BETA_TWO) * clipped * clipped
    moment_hat = moment / (1.0 - BETA_ONE**STEP)
    variance_hat = variance / (1.0 - BETA_TWO**STEP)
    updated = master - step_rate * (
        moment_hat / (jnp.sqrt(variance_hat) + ADAM_EPS) + weight_decay * master
    )
    return (updated, moment, variance, updated.astype(jnp.bfloat16))


def add_terms(totals, new_terms):
    if totals is None:
        return new_terms
    return tuple((acc + new_term for acc, new_term in zip(totals, new_terms)))


def on_device(
    inputs,
    cotangent,
    joined_master,
    joined_first,
    joined_second,
    outward_master,
    outward_first,
    outward_second,
    gated_master,
    gated_first,
    gated_second,
    downward_master,
    downward_first,
    downward_second,
    vectors_master,
    vectors_first,
    vectors_second,
):
    tp_count = lax.axis_size("tp")
    tp_index = lax.axis_index("tp")
    joined_low = joined_master.astype(jnp.bfloat16)
    outward_low = outward_master.astype(jnp.bfloat16)
    gated_low = gated_master.astype(jnp.bfloat16)
    downward_low = downward_master.astype(jnp.bfloat16)
    vectors_low = vectors_master.astype(jnp.bfloat16)
    totals = None
    output_list = []
    grad_list = []
    for micro_index in range(MICRO):
        whole_weights = (
            lax.all_gather(joined_low, "fsdp", axis=1, tiled=True),
            lax.all_gather(outward_low, "fsdp", axis=0, tiled=True),
            lax.all_gather(gated_low, "fsdp", axis=1, tiled=True),
            lax.all_gather(downward_low, "fsdp", axis=0, tiled=True),
            lax.all_gather(vectors_low, "fsdp", axis=1, tiled=True),
        )
        output_rows, input_rows, terms = micro_step(
            inputs[micro_index, 0], cotangent[micro_index, 0], whole_weights, tp_index
        )
        output_list.append(output_rows)
        grad_list.append(input_rows)
        joined_term, outward_term, gated_term, downward_term, vectors_term = terms
        reduced = (
            lax.psum_scatter(joined_term, "fsdp", scatter_dimension=0, tiled=True),
            lax.psum_scatter(outward_term, "fsdp", scatter_dimension=0, tiled=True),
            lax.psum_scatter(gated_term, "fsdp", scatter_dimension=0, tiled=True),
            lax.psum_scatter(downward_term, "fsdp", scatter_dimension=0, tiled=True),
            lax.psum_scatter(vectors_term, "fsdp", scatter_dimension=0, tiled=True),
        )
        totals = add_terms(totals, restore_layout(reduced))
    joined_grad, outward_grad, gated_grad, downward_grad, vectors_part = totals
    vectors_grad = lax.psum(vectors_part, "tp")
    square_local = (
        jnp.sum(joined_grad * joined_grad)
        + jnp.sum(outward_grad * outward_grad)
        + jnp.sum(gated_grad * gated_grad)
        + jnp.sum(downward_grad * downward_grad)
        + jnp.sum(vectors_grad * vectors_grad) / tp_count
    )
    grad_norm = jnp.sqrt(lax.psum(square_local, ("fsdp", "tp")))
    factor = jnp.minimum(1.0, CLIP / (grad_norm + 1e-06))
    joined_new = adamw(
        joined_master, joined_first, joined_second, joined_grad, factor, D ** (-0.5), DECAY
    )
    outward_new = adamw(
        outward_master,
        outward_first,
        outward_second,
        outward_grad,
        factor,
        (D // 32) ** (-0.5),
        DECAY,
    )
    gated_new = adamw(
        gated_master, gated_first, gated_second, gated_grad, factor, D ** (-0.5), DECAY
    )
    downward_new = adamw(
        downward_master, downward_first, downward_second, downward_grad, factor, FF ** (-0.5), DECAY
    )
    vectors_new = adamw(
        vectors_master, vectors_first, vectors_second, vectors_grad, factor, SMALL_RATE, 0.0
    )
    outputs = jnp.stack(output_list)[:, None]
    input_grad = jnp.stack(grad_list)[:, None]
    return (
        outputs,
        input_grad,
        grad_norm,
        joined_new[0],
        joined_new[1],
        joined_new[2],
        joined_new[3],
        outward_new[0],
        outward_new[1],
        outward_new[2],
        outward_new[3],
        gated_new[0],
        gated_new[1],
        gated_new[2],
        gated_new[3],
        downward_new[0],
        downward_new[1],
        downward_new[2],
        downward_new[3],
        vectors_new[0],
        vectors_new[1],
        vectors_new[2],
        vectors_new[3],
    )


def solution(mesh):
    placed = (
        P(None, "fsdp", "tp", None),
        P(None, "fsdp", "tp", None),
        P(None, "fsdp", "tp"),
        P(None, "fsdp", "tp"),
        P(None, "fsdp", "tp"),
        P("fsdp", "tp"),
        P("fsdp", "tp"),
        P("fsdp", "tp"),
        P(None, "fsdp", "tp"),
        P(None, "fsdp", "tp"),
        P(None, "fsdp", "tp"),
        P("fsdp", "tp"),
        P("fsdp", "tp"),
        P("fsdp", "tp"),
        P(None, "fsdp"),
        P(None, "fsdp"),
        P(None, "fsdp"),
    )
    return jax.shard_map(
        on_device,
        mesh=mesh,
        in_specs=placed,
        out_specs=(
            P(None, "fsdp", "tp", None),
            P(None, "fsdp", "tp", None),
            P(),
            P(None, "fsdp", "tp"),
            P(None, "fsdp", "tp"),
            P(None, "fsdp", "tp"),
            P(None, "fsdp", "tp"),
            P("fsdp", "tp"),
            P("fsdp", "tp"),
            P("fsdp", "tp"),
            P("fsdp", "tp"),
            P(None, "fsdp", "tp"),
            P(None, "fsdp", "tp"),
            P(None, "fsdp", "tp"),
            P(None, "fsdp", "tp"),
            P("fsdp", "tp"),
            P("fsdp", "tp"),
            P("fsdp", "tp"),
            P("fsdp", "tp"),
            P(None, "fsdp"),
            P(None, "fsdp"),
            P(None, "fsdp"),
            P(None, "fsdp"),
        ),
        check_vma=False,
    )
```

profile of v0, /device:TPU:0, one launch (start us, length us, event | category | flops | bytes accessed | tf_op | source)
XLA Modules:
  0.0 3080.2 jit_solution(10853162096243506333)
XLA Ops:
  12.5 42.7 %all_gather.32 = bf16[5,2048]{1,0:T(8,128)(2,1)S(1)} all-gather(bf16[5,128]{1,0:T(8,128)(2,1)S(1)} %convert_element_type.168), channel_id=1, replica_groups=mesh['fsdp'=16,'tp'=2] {'fsdp'}, dimensions={1}, use_global_device_ids=true | all-gather | bytes 21760 | tf_op jit(solution)/shard_map/all_gather | solution.py:266
  65.2 37.3 %all-gather.15.cloned.1.call-done = bf16[2048,1024]{1,0:T(8,128)(2,1)} async-done(((bf16[128,1024]{1,0:T(8,128)(2,1)}), bf16[2048,1024]{1,0:T(8,128)(2,1)}) %all-gather.15.cloned.1.call-update) | async-done | bytes 4194320 | tf_op jit(solution)/shard_map/all_gather | solution.py:263
  124.5 156.2 %all-gather.13.cloned.1.call-done = bf16[3,2048,1024]{2,1,0:T(8,128)(2,1)} async-done(((bf16[3,128,1024]{2,1,0:T(8,128)(2,1)}), bf16[3,2048,1024]{2,1,0:T(8,128)(2,1)}) %all-gather.13.cloned.1.call-update) | async-done | bytes 12582928 | tf_op jit(solution)/shard_map/all_gather | solution.py:262
  365.1 180.7 %all-gather.17.cloned.1.call-done = bf16[2,2048,2816]{2,1,0:T(8,128)(2,1)} async-done(((bf16[2,128,2816]{2,1,0:T(8,128)(2,1)}), bf16[2,2048,2816]{2,1,0:T(8,128)(2,1)}) %all-gather.17.cloned.1.call-update) | async-done | bytes 23068688 | tf_op jit(solution)/shard_map/all_gather | solution.py:264
  545.8 13.2 convolution_bitcast_fusion
  559.0 130.5 %all-gather.19.cloned.1.call-done = bf16[2048,2816]{1,0:T(8,128)(2,1)} async-done(((bf16[128,2816]{1,0:T(8,128)(2,1)}), bf16[2048,2816]{1,0:T(8,128)(2,1)}) %all-gather.19.cloned.1.call-update) | async-done | bytes 11534352 | tf_op jit(solution)/shard_map/all_gather | solution.py:265
  689.5 10.8 fusion.24
  700.3 13.0 fusion.13
  713.4 11.6 convolution_bitcast_fusion.1
  735.1 13.0 fusion.14
  780.9 11.7 fusion.77
  797.5 17.4 convolution_add_fusion.1
  815.2 12.8 fusion.65
  828.0 15.2 add_bitcast_fusion
  843.2 19.9 fusion.19
  863.1 30.5 convolution_add_fusion
  907.5 28.8 reduce-scatter.20.cloned.1.call-done
  938.1 11.9 reduce-scatter.12.cloned.1.call-done
  950.0 12.6 reduce-scatter.10.cloned.1.call-done
  966.8 75.6 %reduce-scatter.26.cloned.1.call-done = f32[128,5]{0,1:T(8,128)} async-done(((f32[2048,5]{0,1:T(8,128)}), f32[128,5]{0,1:T(8,128)}) %reduce-scatter.26.cloned.1.call-update) | async-done | bytes 2576 | tf_op jit(solution)/shard_map/reduce_scatter | solution.py:279
  1046.5 511.6 %reduce-scatter.18.cloned.1.call-done = f32[128,3,1024]{2,0,1:T(8,128)} async-done(((f32[2048,3,1024]{2,0,1:T(8,128)}), f32[128,3,1024]{2,0,1:T(8,128)}) %reduce-scatter.18.cloned.1.call-update) | async-done | bytes 1572880 | tf_op jit(solution)/shard_map/reduce_scatter | solution.py:275
  1561.8 477.0 %reduce-scatter.24.cloned.1.call-done = f32[128,2816]{0,1:T(8,128)} async-done(((f32[2048,2816]{0,1:T(8,128)}), f32[128,2816]{0,1:T(8,128)}) %reduce-scatter.24.cloned.1.call-update) | async-done | bytes 1441808 | tf_op jit(solution)/shard_map/reduce_scatter | solution.py:278
  2041.2 944.8 %reduce-scatter.22.cloned.1.call-done = f32[128,2,2816]{2,0,1:T(8,128)} async-done(((f32[2048,2,2816]{2,0,1:T(8,128)}), f32[128,2,2816]{2,0,1:T(8,128)}) %reduce-scatter.22.cloned.1.call-update) | async-done | bytes 2883600 | tf_op jit(solution)/shard_map/reduce_scatter | solution.py:277
  2992.6 43.9 %psum.15 = f32[]{:T(128)} all-reduce(f32[]{:T(128)S(6)} %add.378), channel_id=1, replica_groups=mesh['fsdp'=16,'tp'=2] {'fsdp','tp'}, use_global_device_ids=true, to_apply=%region_40.41 | all-reduce | flops 1 | bytes 8 | tf_op jit(solution)/shard_map/psum | solution.py:291
  (346 shorter events, 237.1 us)
Async XLA Ops:
  7.2 57.9 %all-gather.23.cloned.1.call-start = ((), (), s32[]{:S(2)}) async-start(), calls=%async_computation.19 | async-start | bytes 1572864 | tf_op jit(solution)/shard_map/all_gather | solution.py:127
  9.7 92.8 %all-gather.15.cloned.1.call-start = ((), (), s32[]{:S(2)}) async-start(), calls=%async_computation.11 | async-start | bytes 4456448 | tf_op jit(solution)/shard_map/all_gather | solution.py:263
  10.5 101.7 %all-gather.25.cloned.1.call-start = ((), (), s32[]{:S(2)}) async-start(), calls=%async_computation.20 | async-start | bytes 1572864 | tf_op jit(solution)/shard_map/all_gather | solution.py:127
  11.2 113.2 %all-gather.11.cloned.1.call-start = ((), (), s32[]{:S(2)}) async-start(), calls=%async_computation.9 | async-start | bytes 1572864 | tf_op jit(solution)/shard_map/all_gather | solution.py:126
  56.7 224.0 %all-gather.13.cloned.1.call-start = ((), (), s32[]{:S(2)}) async-start(), calls=%async_computation.10 | async-start | bytes 13369344 | tf_op jit(solution)/shard_map/all_gather | solution.py:262
  59.4 231.0 %all-gather.21.cloned.1.call-start = ((), (), s32[]{:S(2)}) async-start(), calls=%async_computation.15 | async-start | bytes 1572864 | tf_op jit(solution)/shard_map/all_gather | solution.py:126
  60.0 485.9 %all-gather.17.cloned.1.call-start = ((), (), s32[]{:S(2)}) async-start(), calls=%async_computation.12 | async-start | bytes 24510464 | tf_op jit(solution)/shard_map/all_gather | solution.py:264
  61.3 628.3 %all-gather.19.cloned.1.call-start = ((), (), s32[]{:S(2)}) async-start(), calls=%async_computation.13 | async-start | bytes 12255232 | tf_op jit(solution)/shard_map/all_gather | solution.py:265
  63.7 728.9 %reduce-scatter.16.cloned.1.call-start = ((), (), s32[]{:S(2)}) async-start(), calls=%async_computation.18 | async-start | bytes 1572864 | tf_op jit(solution)/shard_map/reduce_scatter | solution.py:185
  64.5 246.5 %copy-start.65 = (f32[256,16]{0,1:T(8,128)}, f32[256,16]{0,1:T(8,128)S(1)}, u32[]{:S(2)}) copy-start(f32[256,16]{0,1:T(8,128)S(1)} %get-tuple-element.254) | copy-start | bytes 49156
  355.4 190.5 %copy-start.5 = (bf16[256,2048]{1,0:T(8,128)(2,1)S(1)}, bf16[256,2048]{1,0:T(8,128)(2,1)}, u32[]{:S(2)}) copy-start(bf16[256,2048]{1,0:T(8,128)(2,1)} %all-gather.21.cloned.1.call-done) | copy-start | bytes 3145732
  365.1 324.5 %copy-start.29 = (bf16[1,1,256,2048]{3,2,1,0:T(8,128)(2,1)S(1)}, bf16[1,1,256,2048]{3,2,1,0:T(8,128)(2,1)}, u32[]{:S(2)}) copy-start(bf16[1,1,256,2048]{3,2,1,0:T(8,128)(2,1)} %all-gather.25.cloned.1.call-done) | copy-start | bytes 3145732
  713.3 79.3 %reduce-scatter.14.cloned.1.call-start = ((), (), s32[]{:S(2)}) async-start(), calls=%async_computation.17 | async-start | bytes 1572864 | tf_op jit(solution)/shard_map/reduce_scatter | solution.py:185
  748.1 188.2 %reduce-scatter.20.cloned.1.call-start = ((), (), s32[]{:S(2)}) async-start(), calls=%async_computation.22 | async-start | bytes 8912896 | tf_op jit(solution)/shard_map/reduce_scatter | solution.py:276
  759.2 190.7 %reduce-scatter.12.cloned.1.call-start = ((), (), s32[]{:S(2)}) async-start(), calls=%async_computation.16 | async-start | bytes 1572864 | tf_op jit(solution)/shard_map/reduce_scatter | solution.py:148
  768.9 193.8 %reduce-scatter.10.cloned.1.call-start = ((), (), s32[]{:S(2)}) async-start(), calls=%async_computation.14 | async-start | bytes 1572864 | tf_op jit(solution)/shard_map/reduce_scatter | solution.py:148
  780.8 261.6 %reduce-scatter.26.cloned.1.call-start = ((), (), s32[]{:S(2)}) async-start(), calls=%async_computation.25 | async-start | bytes 69632 | tf_op jit(solution)/shard_map/reduce_scatter | solution.py:279
  797.5 760.6 %reduce-scatter.18.cloned.1.call-start = ((), (), s32[]{:S(2)}) async-start(), calls=%async_computation.21 | async-start | bytes 26738688 | tf_op jit(solution)/shard_map/reduce_scatter | solution.py:275
  815.0 1223.8 %reduce-scatter.24.cloned.1.call-start = ((), (), s32[]{:S(2)}) async-start(), calls=%async_computation.24 | async-start | bytes 24510464 | tf_op jit(solution)/shard_map/reduce_scatter | solution.py:278
  843.2 2142.9 %reduce-scatter.22.cloned.1.call-start = ((), (), s32[]{:S(2)}) async-start(), calls=%async_computation.23 | async-start | bytes 49020928 | tf_op jit(solution)/shard_map/reduce_scatter | solution.py:277
  900.4 62.2 %copy-start.33 = (bf16[2,1,128,2048]{3,2,1,0:T(8,128)(2,1)S(1)}, bf16[2,1,128,2048]{3,2,1,0:T(8,128)(2,1)}, u32[]{:S(2)}) copy-start(bf16[2,1,128,2048]{3,2,1,0:T(8,128)(2,1)} %param.18) | copy-start | bytes 3145732
  1046.5 1944.0 %copy-start.48 = (bf16[1,128,2048]{2,1,0:T(8,128)(2,1)S(1)}, bf16[1,128,2048]{2,1,0:T(8,128)(2,1)}, u32[]{:S(2)}) copy-start(bf16[1,128,2048]{2,1,0:T(8,128)(2,1)} %get-tuple-element.209) | copy-start | bytes 1572868
  1561.8 1475.5 %copy-start.13 = (f32[128,2816]{0,1:T(8,128)S(1)}, f32[128,2816]{0,1:T(8,128)}, u32[]{:S(2)}) copy-start(f32[128,2816]{0,1:T(8,128)} %copy.133) | copy-start | bytes 4325380
  2038.8 998.5 %copy-start.12 = (f32[128,2816]{0,1:T(8,128)S(1)}, f32[128,2816]{0,1:T(8,128)}, u32[]{:S(2)}) copy-start(f32[128,2816]{0,1:T(8,128)} %reduce-scatter.24.cloned.1.call-done) | copy-start | bytes 4325380
  (82 other events, 757.4 us)
Sparse Core Ops, SparseCore 0:
  10.2 11.7 all-gather.22
  25.3 77.1 all-gather.14
  104.6 7.6 all-gather.24
  114.2 10.1 all-gather.10
  127.6 153.0 all-gather.12
  282.7 7.2 all-gather.20
  293.3 252.4 all-gather.16
  549.1 140.3 all-gather.18
  713.4 6.7 reduce-scatter.15
  748.3 6.6 reduce-scatter.13
  759.4 176.9 reduce-scatter.19
  939.0 10.9 reduce-scatter.11
  952.9 9.6 reduce-scatter.9
  965.3 77.1 reduce-scatter.25
  1044.7 513.3 reduce-scatter.17
  1560.3 478.3 reduce-scatter.23
  2041.1 944.9 reduce-scatter.21
where the time goes:
time: 3090 us; the launch traced here: 3080 us
  waiting for transfers between devices  2580 us (83%)
  matrix products  263 us (9%)
  blocking collectives  89.3 us (3%)
  other arithmetic  67 us (2%)
  local copies, waits for them, and re-layouts  58.5 us (2%)
    reduce_scatter x1, waiting for transfers between devices, on_device(): lax.psum_scatter(gated_term, 'fsdp', scatter_dimension=0, tiled=True)  945 us
    reduce_scatter x1, waiting for transfers between devices, on_device(): lax.psum_scatter(joined_term, 'fsdp', scatter_dimension=0, tiled=True)  512 us
    reduce_scatter x1, waiting for transfers between devices, on_device(): lax.psum_scatter(downward_term, 'fsdp', scatter_dimension=0, tiled=True)  477 us
    all_gather x1, waiting for transfers between devices, on_device(): lax.all_gather(gated_low, 'fsdp', axis=1, tiled=True)  181 us
    all_gather x1, waiting for transfers between devices, on_device(): lax.all_gather(joined_low, 'fsdp', axis=1, tiled=True)  156 us
    all_gather x1, waiting for transfers between devices, on_device(): lax.all_gather(downward_low, 'fsdp', axis=0, tiled=True)  131 us
    reduce_scatter x1, waiting for transfers between devices, on_device(): lax.psum_scatter(vectors_term, 'fsdp', scatter_dimension=0, tiled=True)  75.6 us
  transfers between devices with their start and end apart: 17, of which 13 were waited for; matrix products, arithmetic and copies ran while one was open for 10% of the time, Pallas kernels for 0%

commit v1 on v0

v1 whole, which is shorter than its diff:
```python
import functools
import jax
import jax.numpy as jnp
from jax import lax
from jax.experimental import pallas as pl
from jax.experimental.pallas import tpu as pltpu
from jax.sharding import Mesh
from jax.sharding import PartitionSpec as P

HD = 64
ROT = 16
MICRO = 2
STEP = 5
QUAD = 4

EPS_NORM = 1e-05
CLIP = 1.0
BETA_ONE = 0.5
BETA_TWO = 0.5
ADAM_EPS = 1e-08
DECAY = 0.1
SMALL_RATE = 0.2
ROPE_BASE = 10000.0
LOW = jnp.bfloat16
F32 = jnp.float32
SWAP = [(0, 1), (1, 0)]


def nn(left, right):
    return lax.dot_general(left, right, (((1,), (0,)), ((), ())), preferred_element_type=F32)


def nt(left, right):
    return lax.dot_general(left, right, (((1,), (1,)), ((), ())), preferred_element_type=F32)


def tn(left, right):
    return lax.dot_general(left, right, (((0,), (0,)), ((), ())), preferred_element_type=F32)


def swap(value, axis):
    return lax.ppermute(value, axis, SWAP)


def gate_kernel(*refs):
    pass


def after(value, *others):
    anywhere = pl.BlockSpec(memory_space=pl.ANY)
    return pl.pallas_call(
        gate_kernel,
        in_specs=[anywhere] * (1 + len(others)),
        out_specs=anywhere,
        out_shape=jax.ShapeDtypeStruct(value.shape, value.dtype),
        input_output_aliases={0: 0},
        name="after",
    )(value, *others)


def gather_line(block, place):
    ups, downs = [block], [block]
    for step in range(1, QUAD):
        ups.append(lax.ppermute(ups[-1], "a", [(i, i + 1) for i in range(step - 1, QUAD - 1)]))
        downs.append(lax.ppermute(downs[-1], "a", [(i, i - 1) for i in range(1, QUAD - step + 1)]))
    whole = jnp.zeros((QUAD,) + block.shape, block.dtype)
    whole = lax.dynamic_update_index_in_dim(whole, block, 0, 0)
    for k in range(1, QUAD):
        picked = jnp.where(place + k < QUAD, downs[k], ups[QUAD - k])
        whole = lax.dynamic_update_index_in_dim(whole, picked, k, 0)
    return whole, downs[-1]


def add_low(left, right):
    return (left.astype(F32) + right.astype(F32)).astype(LOW)


def scatter_line(parts):
    up = down = None
    for step in range(1, QUAD):
        to_up, to_down = parts[QUAD - step], parts[step]
        if step > 1:
            to_up, to_down = add_low(to_up, up), add_low(to_down, down)
        up = lax.ppermute(to_up, "a", [(i, i + 1) for i in range(0, step)])
        down = lax.ppermute(to_down, "a", [(i, i - 1) for i in range(QUAD - step, QUAD)])
    return parts[0].astype(F32) + up.astype(F32) + down.astype(F32)


def bits(axis):
    found, bit = [], 1
    count, at = lax.axis_size(axis), lax.axis_index(axis)
    while bit < count:
        found.append((axis, [(i, i ^ bit) for i in range(count)], (at // bit) % 2))
        bit *= 2
    return found


def gather_small(value):
    for axis, pairs, bit in bits("p") + bits("a"):
        other = lax.ppermute(value, axis, pairs)
        value = jnp.where(
            bit == 0,
            jnp.concatenate([value, other], axis=-1),
            jnp.concatenate([other, value], axis=-1),
        )
    return value


def sum_small(value):
    for axis, pairs, bit in bits("tp") + bits("p") + bits("a"):
        value = value + lax.ppermute(value, axis, pairs)
    return value


def attention_kernel(
    mask_ref, cos_ref, left_ref, right_ref, bias_ref, joined_ref, back_ref, mixed_ref, grad_ref, bias_grad_ref
):
    rows, width = cos_ref.shape
    heads = width // HD
    scale = HD ** (-0.5)
    joined = joined_ref[...].reshape(rows, 3 * width) + bias_ref[0:1, :]
    cos, left, right = cos_ref[...], left_ref[...], right_ref[...]

    def turn(v):
        return v * cos + pltpu.roll(v, width - ROT // 2, 1) * left + pltpu.roll(v, ROT // 2, 1) * right

    def turn_back(g):
        return g * cos - (pltpu.roll(g, width - ROT // 2, 1) * left + pltpu.roll(g, ROT // 2, 1) * right)

    query = turn(joined[:, :width]).astype(LOW)
    keys = turn(joined[:, width : 2 * width]).astype(LOW)
    values = joined[:, 2 * width :].astype(LOW)
    back = back_ref[...].reshape(rows, width)
    mask = mask_ref[...]
    mixed, d_query, d_keys, d_values = [], [], [], []
    for head in range(heads):
        cut = slice(head * HD, (head + 1) * HD)
        q, k, v, g = query[:, cut], keys[:, cut], values[:, cut], back[:, cut]
        scores = nt(q, k) * scale + mask
        peak = jnp.max(scores, axis=-1, keepdims=True)
        raised = jnp.exp(scores - peak)
        full = raised / jnp.sum(raised, axis=-1, keepdims=True)
        probs = full.astype(LOW)
        mixed.append(nn(probs, v))
        prob_grad = nt(g, v)
        weighted = full * prob_grad
        inner = jnp.sum(weighted, axis=-1, keepdims=True)
        score_grad = (weighted - full * inner).astype(LOW)
        d_query.append(nn(score_grad, k) * scale)
        d_keys.append(tn(score_grad, q) * scale)
        d_values.append(tn(probs, g))
    mixed_ref[...] = jnp.concatenate(mixed, axis=-1).astype(LOW).reshape(mixed_ref.shape)
    out = jnp.concatenate(
        [
            turn_back(jnp.concatenate(d_query, axis=-1)),
            turn_back(jnp.concatenate(d_keys, axis=-1)),
            jnp.concatenate(d_values, axis=-1),
        ],
        axis=-1,
    ).astype(LOW)
    grad_ref[...] = out.reshape(grad_ref.shape)

    @pl.when(pl.program_id(0) == 0)
    def _():
        bias_grad_ref[...] = jnp.zeros_like(bias_grad_ref)

    sums = jnp.sum(out.astype(F32).reshape(rows // 8, 8, 3 * width), axis=0)
    bias_grad_ref[...] += sums


def attention(joined, back, bias, tp_index):
    tokens, width = back.shape
    half = 128
    seqs = tokens // (2 * half)
    length = 2 * half
    position = lax.rem(jnp.arange(length) + tp_index * half, length)
    mask = jnp.where(position[:, None] >= position[None, :], 0.0, -jnp.inf).astype(F32)
    frequency = ROPE_BASE ** (-(2.0 * jnp.arange(ROT // 2, dtype=F32)) / ROT)
    angles = position.astype(F32)[:, None] * frequency[None, :]
    cosine, sine = jnp.cos(angles), jnp.sin(angles)
    rest = jnp.ones((length, HD - ROT), F32)
    nothing = jnp.zeros((length, ROT // 2), F32)
    heads = width // HD
    cos = jnp.tile(jnp.concatenate([cosine, cosine, rest], 1), (1, heads))
    left = jnp.tile(jnp.concatenate([-sine, nothing, 0.0 * rest], 1), (1, heads))
    right = jnp.tile(jnp.concatenate([nothing, sine, 0.0 * rest], 1), (1, heads))
    fixed = lambda i: (0, 0)
    rows = lambda i: (0, i, 0, 0)
    shape = lambda w: (2, seqs, half, w)
    mixed, grad, bias_grad = pl.pallas_call(
        attention_kernel,
        grid=(seqs,),
        in_specs=[
            pl.BlockSpec((length, length), fixed),
            pl.BlockSpec((length, width), fixed),
            pl.BlockSpec((length, width), fixed),
            pl.BlockSpec((length, width), fixed),
            pl.BlockSpec((1, 3 * width), fixed),
            pl.BlockSpec((2, 1, half, 3 * width), rows),
            pl.BlockSpec((2, 1, half, width), rows),
        ],
        out_specs=[
            pl.BlockSpec((2, 1, half, width), rows),
            pl.BlockSpec((2, 1, half, 3 * width), rows),
            pl.BlockSpec((8, 3 * width), fixed),
        ],
        out_shape=[
            jax.ShapeDtypeStruct(shape(width), LOW),
            jax.ShapeDtypeStruct(shape(3 * width), LOW),
            jax.ShapeDtypeStruct((8, 3 * width), F32),
        ],
        cost_estimate=pl.CostEstimate(
            flops=seqs * heads * 7 * 2 * length * length * HD * 4,
            bytes_accessed=tokens * width * 30,
            transcendentals=seqs * heads * length * length,
        ),
        compiler_params=pltpu.CompilerParams(vmem_limit_bytes=32 * 1024 * 1024),
        name="attention_both_ways",
    )(mask, cos, left, right, bias, joined.reshape(shape(3 * width)), back.reshape(shape(width)))
    return (
        mixed.reshape(tokens, width),
        grad.reshape(tokens, 3 * width),
        jnp.sum(bias_grad, axis=0),
    )


def product_kernel(terms, *refs):
    out_ref = refs[2 * terms]
    total = nt(refs[0][...], refs[terms][...])
    for term in range(1, terms):
        total += nt(refs[term][...], refs[terms + term][...])
    out_ref[...] = total.astype(out_ref.dtype)


def product_grad_kernel(terms, *refs):
    xhat_ref, out_ref, sums_ref = refs[2 * terms :]
    total = nt(refs[0][...], refs[terms][...])
    for term in range(1, terms):
        total += nt(refs[term][...], refs[terms + term][...])
    out_ref[...] = total.astype(out_ref.dtype)
    xhat = xhat_ref[...].astype(F32)

    @pl.when(pl.program_id(1) == 0)
    def _():
        sums_ref[...] = jnp.zeros_like(sums_ref)

    tall = total.shape[0] // 8
    sums_ref[0:8, :] += jnp.sum((total * xhat).reshape(tall, 8, -1), axis=0)
    sums_ref[8:16, :] += jnp.sum(total.reshape(tall, 8, -1), axis=0)


def product_sum(pairs, tokens, depth, extra=None):
    tall, broad = 512, 512
    terms = len(pairs)
    lefts = [pl.BlockSpec((tall, left.shape[1]), lambda j, i: (i, 0)) for left, _, _ in pairs]
    rights = [
        pl.BlockSpec((broad, left.shape[1]), functools.partial(lambda at, j, i: (j, at), at))
        for left, _, at in pairs
    ]
    deep = sum(left.shape[1] for left, _, _ in pairs)
    in_specs, operands = lefts + rights, [p[0] for p in pairs] + [p[1] for p in pairs]
    out_specs = pl.BlockSpec((tall, broad), lambda j, i: (i, j))
    out_shape = jax.ShapeDtypeStruct((tokens, depth), LOW)
    kernel = product_kernel
    if extra is not None:
        kernel = product_grad_kernel
        in_specs = in_specs + [
            pl.BlockSpec((tall, broad), lambda j, i: (i, j)),
        ]
        operands = operands + list(extra)
        out_specs = [out_specs, pl.BlockSpec((16, broad), lambda j, i: (0, j))]
        out_shape = [out_shape, jax.ShapeDtypeStruct((16, depth), F32)]
    return pl.pallas_call(
        functools.partial(kernel, terms),
        grid=(depth // broad, tokens // tall),
        in_specs=in_specs,
        out_specs=out_specs,
        out_shape=out_shape,
        cost_estimate=pl.CostEstimate(
            flops=2 * tokens * depth * deep,
            bytes_accessed=2 * (depth + tokens) * deep + 2 * tokens * depth,
            transcendentals=0,
        ),
        compiler_params=pltpu.CompilerParams(vmem_limit_bytes=48 * 1024 * 1024),
        name="product_sum",
    )(*operands)


def norm_kernel(gain_ref, shift_ref, own_ref, other_ref, normed_ref, xhat_ref):
    def run(ref):
        rows = ref[...].astype(F32)
        average = jnp.mean(rows, axis=-1, keepdims=True)
        centred = rows - average
        variance = jnp.mean(centred * centred, axis=-1, keepdims=True)
        xhat = centred * lax.rsqrt(variance + EPS_NORM)
        xhat_ref[...] = xhat.astype(LOW)
        normed_ref[...] = (xhat * gain_ref[...] + shift_ref[...]).astype(LOW)

    half = pl.num_programs(0) // 2

    @pl.when(pl.program_id(0) < half)
    def _():
        run(own_ref)

    @pl.when(pl.program_id(0) >= half)
    def _():
        run(other_ref)


def norm_rows(own, other, gain, shift):
    rows, depth = own.shape
    tall = 256
    half = rows // tall
    fixed = lambda i: (0, 0)
    return pl.pallas_call(
        norm_kernel,
        grid=(2 * half,),
        in_specs=[
            pl.BlockSpec((1, depth), fixed),
            pl.BlockSpec((1, depth), fixed),
            pl.BlockSpec((tall, depth), lambda i: (jnp.minimum(i, half - 1), 0)),
            pl.BlockSpec((tall, depth), lambda i: (jnp.maximum(i - half, 0), 0)),
        ],
        out_specs=[pl.BlockSpec((tall, depth), lambda i: (i, 0))] * 2,
        out_shape=[jax.ShapeDtypeStruct((2 * rows, depth), LOW)] * 2,
        cost_estimate=pl.CostEstimate(
            flops=20 * rows * depth, bytes_accessed=12 * rows * depth, transcendentals=0
        ),
        compiler_params=pltpu.CompilerParams(vmem_limit_bytes=32 * 1024 * 1024),
        name="norm_rows",
    )(gain, shift, own, other)


def adamw(master, first_old, second_old, gradient, factor, step_rate, weight_decay):
    clipped = gradient * factor
    moment = BETA_ONE * first_old + (1.0 - BETA_ONE) * clipped
    variance = BETA_TWO * second_old + (1.0 - BETA_TWO) * clipped * clipped
    moment_hat = moment / (1.0 - BETA_ONE**STEP)
    variance_hat = variance / (1.0 - BETA_TWO**STEP)
    updated = master - step_rate * (
        moment_hat / (jnp.sqrt(variance_hat) + ADAM_EPS) + weight_decay * master
    )
    return (updated, moment, variance, updated.astype(LOW))


def on_device(
    inputs,
    cotangent,
    joined_master,
    joined_first,
    joined_second,
    outward_master,
    outward_first,
    outward_second,
    gated_master,
    gated_first,
    gated_second,
    downward_master,
    downward_first,
    downward_second,
    vectors_master,
    vectors_first,
    vectors_second,
):
    tp_count = lax.axis_size("tp")
    quads = lax.axis_size("p")
    place = lax.axis_index("a")
    at_p = lax.axis_index("p")
    tp_index = lax.axis_index("tp")
    depth = inputs.shape[-1]
    rows_here = joined_master.shape[1]
    att_width = joined_master.shape[2] // QUAD
    ff_here = gated_master.shape[2]
    tiles = ff_here // 128
    wide = -(-tiles // QUAD)
    ff_width = wide * 128
    shortage = wide * QUAD - tiles
    parts = 2
    ff_part = ff_width // parts

    starts, lengths = [], []
    for index in range(QUAD):
        lacks = max(0, index - (QUAD - shortage))
        starts.append((index * wide - lacks) * 128)
        lengths.append((wide - (1 if index >= QUAD - shortage else 0)) * 128)

    def reorder(value):
        shape = value.shape[:-1]
        split = value.reshape(shape + (QUAD, quads, rows_here))
        return jnp.swapaxes(split, -3, -2).reshape(shape + (depth,))

    def restore(value):
        shape = value.shape[:-1]
        split = value.reshape(shape + (quads, QUAD, rows_here))
        return jnp.swapaxes(split, -3, -2).reshape(shape + (depth,))

    def attention_piece(index):
        cut = slice(index * att_width, (index + 1) * att_width)
        return jnp.concatenate(
            [joined_master[c][:, cut] for c in range(3)] + [outward_master[:, cut]], axis=1
        ).astype(LOW)

    def hidden_piece(part, index):
        low, high = part * ff_part, min((part + 1) * ff_part, lengths[index])
        first, last = starts[index] + low, starts[index] + high

        def cut(w):
            return jnp.pad(w[:, first:last], ((0, 0), (0, ff_part - (last - first))))

        return jnp.concatenate(
            [cut(gated_master[0]), cut(gated_master[1]), cut(downward_master)], axis=1
        ).astype(LOW)

    def gather_weight(make):
        pieces = jnp.stack([make(index) for index in range(QUAD)])
        mine = lax.all_to_all(pieces, "a", 0, 0, tiled=True)
        return lax.all_gather(mine, "p", axis=0).reshape(depth, pieces.shape[-1])

    attention_weight = gather_weight(attention_piece)

    vectors_full = gather_small(vectors_master.astype(LOW)).astype(F32)
    row_gain, row_shift = reorder(vectors_full[0:1]), reorder(vectors_full[1:2])
    bias_at = (tp_index * QUAD + place) * att_width
    bias_here = lax.dynamic_slice_in_dim(vectors_full[2:5], bias_at, att_width, 1).reshape(1, 3 * att_width)

    own_rows, own_back = reorder(inputs[:, 0]), reorder(cotangent[:, 0])
    rows_quad, last = gather_line(own_rows, place)
    rows_quad = rows_quad.reshape(-1, depth)
    rows_other = swap(rows_quad, "tp")
    hidden_weights = [gather_weight(functools.partial(hidden_piece, part)) for part in range(parts)]
    back_quad, last = gather_line(after(own_back, last), place)
    back_quad = back_quad.reshape(-1, depth)
    back_all = jnp.concatenate([back_quad, swap(back_quad, "tp")], axis=0)
    normed, xhat_all = norm_rows(rows_quad, rows_other, row_gain, row_shift)
    tokens = normed.shape[0]

    def hidden(weight):
        gate_up = nn(normed, weight[:, : 2 * ff_part])
        act_grad = nn(back_all, weight[:, 2 * ff_part :])
        gate, up = gate_up[:, :ff_part], gate_up[:, ff_part:]
        sigma = 1.0 / (1.0 + jnp.exp(-gate))
        silu = gate * sigma
        activated = (silu * up).astype(LOW)
        gate_grad = (act_grad * up * sigma * (1.0 + gate * (1.0 - sigma))).astype(LOW)
        up_grad = (act_grad * silu).astype(LOW)
        gated_grad = jnp.concatenate([gate_grad, up_grad], axis=1)
        term = jnp.concatenate(
            [tn(normed, gated_grad).astype(LOW), tn(back_all, activated).astype(LOW)], axis=1
        )
        return activated, gated_grad, term

    joined_out = nn(normed, attention_weight[:, : 3 * att_width])
    mixed_grad = nn(back_all, attention_weight[:, 3 * att_width :]).astype(LOW)
    mixed, joined_grad, bias_grad = attention(joined_out, mixed_grad, bias_here, tp_index)
    attention_term = jnp.concatenate(
        [tn(normed, joined_grad).astype(LOW), tn(back_all, mixed).astype(LOW)], axis=1
    )
    done = [hidden(weight) for weight in hidden_weights]

    out_part = product_sum(
        [(mixed, attention_weight, 3)]
        + [(item[0], weight, 2) for item, weight in zip(done, hidden_weights)],
        tokens,
        depth,
    )
    normed_grad_part, sums = product_sum(
        [(joined_grad, attention_weight, 0)]
        + [(item[1], weight, 0) for item, weight in zip(done, hidden_weights)],
        tokens,
        depth,
        (xhat_all,),
    )

    def collect(term):
        folded = after(term).reshape(quads, QUAD, rows_here, term.shape[1])
        mine = lax.psum_scatter(folded, "p", scatter_dimension=0)
        return lax.all_to_all(mine, "a", 0, 0, tiled=True).astype(F32)

    attention_own = collect(attention_term)
    hidden_own = [collect(item[2]) for item in done]

    def scatter_rows(part):
        halves = part.reshape(2, QUAD, MICRO, 128, depth)
        quad = add_low(halves[0], swap(halves[1], "tp"))
        return scatter_line([quad[k] for k in range(QUAD)])

    branch = scatter_rows(out_part)
    own_grad = scatter_rows(normed_grad_part)
    own_float = own_rows.astype(F32)
    outputs = restore((own_float + branch).astype(LOW))[:, None]

    average = jnp.mean(own_float, axis=-1, keepdims=True)
    centred_own = own_float - average
    inverse_own = lax.rsqrt(jnp.mean(centred_own * centred_own, axis=-1, keepdims=True) + EPS_NORM)
    xhat = centred_own * inverse_own
    scaled = own_grad * row_gain
    rows_grad = inverse_own * (
        scaled
        - jnp.mean(scaled, axis=-1, keepdims=True)
        - xhat * jnp.mean(scaled * xhat, axis=-1, keepdims=True)
    )
    input_grad = restore((own_back.astype(F32) + rows_grad).astype(LOW))[:, None]

    bias_wide = lax.dynamic_update_slice(
        jnp.zeros((3, depth), F32), bias_grad.reshape(3, att_width), (0, bias_at)
    )
    vectors_term = jnp.concatenate(
        [restore(jnp.sum(sums.reshape(2, 8, depth), axis=1)), bias_wide], axis=0
    )
    vectors_grad = lax.dynamic_slice_in_dim(
        sum_small(vectors_term), (place * quads + at_p) * rows_here, rows_here, 1
    )

    def columns(piece, c):
        return piece[:, :, c * att_width : (c + 1) * att_width]

    def widen(cut):
        return jnp.concatenate([cut[index] for index in range(QUAD)], axis=1)

    joined_grads = jnp.stack([widen(columns(attention_own, c)) for c in range(3)])
    outward_grads = widen(columns(attention_own, 3))

    def hidden_columns(c):
        found = []
        for index in range(QUAD):
            for part in range(parts):
                size = min(lengths[index] - part * ff_part, ff_part)
                found.append(hidden_own[part][index][:, c * ff_part : c * ff_part + size])
        return jnp.concatenate(found, axis=1)

    gated_grads = jnp.stack([hidden_columns(0), hidden_columns(1)])
    downward_grads = hidden_columns(2)

    square = (
        sum(jnp.sum(own * own) for own in hidden_own)
        + jnp.sum(attention_own * attention_own)
        + jnp.sum(vectors_grad * vectors_grad) / tp_count
    )
    grad_norm = jnp.sqrt(sum_small(jnp.full((8, 128), square))[0, 0])
    factor = jnp.minimum(1.0, CLIP / (grad_norm + 1e-06))
    ff_total = ff_here * tp_count
    return (
        outputs,
        input_grad,
        grad_norm,
        *adamw(joined_master, joined_first, joined_second, joined_grads, factor, depth ** (-0.5), DECAY),
        *adamw(outward_master, outward_first, outward_second, outward_grads, factor, (depth // 32) ** (-0.5), DECAY),
        *adamw(gated_master, gated_first, gated_second, gated_grads, factor, depth ** (-0.5), DECAY),
        *adamw(downward_master, downward_first, downward_second, downward_grads, factor, ff_total ** (-0.5), DECAY),
        *adamw(vectors_master, vectors_first, vectors_second, vectors_grad, factor, SMALL_RATE, 0.0),
    )


def solution(mesh):
    fsdp, tp = mesh.shape["fsdp"], mesh.shape["tp"]
    fine = Mesh(mesh.devices.reshape(QUAD, fsdp // QUAD, tp), ("a", "p", "tp"))
    every = ("a", "p")
    rows = P(None, every, "tp", None)
    stacked = P(None, every, "tp")
    flat = P(every, "tp")
    vectors = P(None, every)
    return jax.shard_map(
        on_device,
        mesh=fine,
        in_specs=(rows,) * 2 + (stacked,) * 3 + (flat,) * 3 + (stacked,) * 3 + (flat,) * 3 + (vectors,) * 3,
        out_specs=(rows,) * 2
        + (P(),)
        + (stacked,) * 4
        + (flat,) * 4
        + (stacked,) * 4
        + (flat,) * 4
        + (vectors,) * 4,
        check_vma=False,
    )
```

time: 3090 us -> 786 us (0.25)
  waiting for transfers between devices: 2580 us -> 231 us
  matrix products: 263 us -> 114 us
  starting transfers between devices: 0.87 us -> 131 us
  Pallas kernels: 0 us -> 89.9 us
  blocking collectives: 89.3 us -> 32.1 us
    reduce_scatter x9 -> x0, waiting for transfers between devices: 2060 us -> none  [the longest x1 945 us: on_device(): lax.psum_scatter(gated_term, 'fsdp', scatter_dimension=0, tiled=True)]
    all_gather x8 -> x3, waiting for transfers between devices: 517 us -> 0.02 us  [gather_weight(): return lax.all_gather(mine, 'p', axis=0).reshape(depth, pieces.shape[-1])]
    ppermute x0 -> x42, waiting for transfers between devices: none -> 224 us  [the longest x6 110 us: gather_line(): lax.ppermute(downs[-1], 'a', [(i, i - 1) for i in range(1, QUAD - step +...]
    dot_general x36 -> x12, matrix products: 263 us -> 114 us  [the longest x6 66.3 us: nn(): lax.dot_general(left, right, (((1,), (0,)), ((), ())), preferred_element_...]
    pallas_call x0 -> x8, Pallas kernels: none -> 89.9 us  [the longest x2 50.2 us: product_sum(): pl.pallas_call(functools.partial(kernel, terms), grid=(depth // broad, to...]
    ppermute x0 -> x42, starting transfers between devices: none -> 74.1 us  [the longest x6 25.7 us: scatter_line(): up = lax.ppermute(to_up, 'a', [(i, i + 1) for i in range(0, step)])]
    all_to_all x0 -> x5, starting transfers between devices: none -> 56.9 us  [the longest x2 44.2 us: gather_weight(): mine = lax.all_to_all(pieces, 'a', 0, 0, tiled=True)]
    psum x2 -> x0, blocking collectives: 46.7 us -> none  [the longest x1 43.9 us: on_device(): grad_norm = jnp.sqrt(lax.psum(square_local, ('fsdp', 'tp')))]
  transfers between devices with their start and end apart: 17 -> 53, of which waited for: 13 -> 20; matrix products, arithmetic and copies ran while one was open for 10% -> 31% of each run, Pallas kernels for 0% -> 12%
where the time goes in v1:
time: 786 us; the launch traced here: 776 us
  waiting for transfers between devices  231 us (29%)
  starting transfers between devices  131 us (17%)
  matrix products  114 us (15%)
  other arithmetic  90.2 us (11%)
  Pallas kernels  89.9 us (11%)
  local copies, waits for them, and re-layouts  67.2 us (9%)
  blocking collectives  32.1 us (4%)
  between operations  20.4 us (3%)
    ppermute x6, waiting for transfers between devices, gather_line(): lax.ppermute(downs[-1], 'a', [(i, i - 1) for i in range(1, QUAD - step +...  110 us
    dot_general x6, matrix products, nn(): lax.dot_general(left, right, (((1,), (0,)), ((), ())), preferred_element_...  66.3 us
    ppermute x10, waiting for transfers between devices, sum_small(): value = value + lax.ppermute(value, axis, pairs)  51.3 us
    pallas_call x2, Pallas kernels, product_sum(): pl.pallas_call(functools.partial(kernel, terms), grid=(depth // broad, to...  50.2 us
    dot_general x6, matrix products, tn(): lax.dot_general(left, right, (((0,), (0,)), ((), ())), preferred_element_...  48.2 us
    all_to_all x2, starting transfers between devices, gather_weight(): mine = lax.all_to_all(pieces, 'a', 0, 0, tiled=True)  44.2 us
    ppermute x6, waiting for transfers between devices, scatter_line(): up = lax.ppermute(to_up, 'a', [(i, i + 1) for i in range(0, step)])  43.2 us
    all_to_all x1, blocking collectives, gather_weight(): mine = lax.all_to_all(pieces, 'a', 0, 0, tiled=True)  32.1 us
  transfers between devices with their start and end apart: 53, of which 20 were waited for; matrix products, arithmetic and copies ran while one was open for 31% of the time, Pallas kernels for 12%

profile of v1, /device:TPU:0, one launch (start us, length us, event | category | flops | bytes accessed | tf_op | source)
XLA Modules:
  0.0 776.4 jit_solution(496939284435361122)
XLA Ops:
  10.1 32.1 %all_to_all.30 = bf16[4,128,1024]{2,1,0:T(8,128)(2,1)} all-to-all(bf16[4,128,1024]{2,1,0:T(8,128)(2,1)S(1)} %maximum_maximum_fusion.2), channel_id=1, replica_groups=mesh['a'=4,'p'=4,'tp'=2] {'a'}, dimensions={0} | all-to-all | bytes 2097152 | tf_op jit(solution)/shard_map/all_to_all | solution.py:416
  56.7 22.1 %collective-permute-done.4 = bf16[2,128,2048]{2,1,0:T(8,128)(2,1)} collective-permute-done((bf16[2,128,2048]{2,1,0:T(8,128)(2,1)S(1)}, bf16[2,128,2048]{2,1,0:T(8,128)(2,1)}, u32[]{:S(2)}, u32[]{:S(2)}) %collective-permute-start.4) | collective-permute-done | bytes 1048608 | tf_op jit(solution)/shard_map/ppermute | solution.py:65
  85.6 25.9 %collective-permute-done.8 = bf16[2,128,2048]{2,1,0:T(8,128)(2,1)} collective-permute-done((bf16[2,128,2048]{2,1,0:T(8,128)(2,1)}, bf16[2,128,2048]{2,1,0:T(8,128)(2,1)}, u32[]{:S(2)}, u32[]{:S(2)}) %collective-permute-start.8) | collective-permute-done | bytes 1048608 | tf_op jit(solution)/shard_map/ppermute | solution.py:65
  118.7 21.4 %collective-permute-done.9.refs_1_ = bf16[2,128,2048]{2,1,0:T(8,128)(2,1)} collective-permute-done((bf16[2,128,2048]{2,1,0:T(8,128)(2,1)}, bf16[2,128,2048]{2,1,0:T(8,128)(2,1)}, u32[]{:S(2)}, u32[]{:S(2)}) %collective-permute-start.9) | collective-permute-done | bytes 1048608 | tf_op jit(solution)/shard_map/ppermute | solution.py:65
  150.3 11.0 %collective-permute-done.12 = bf16[2,128,2048]{2,1,0:T(8,128)(2,1)} collective-permute-done((bf16[2,128,2048]{2,1,0:T(8,128)(2,1)}, bf16[2,128,2048]{2,1,0:T(8,128)(2,1)}, u32[]{:S(2)}, u32[]{:S(2)}) %collective-permute-start.12) | collective-permute-done | bytes 1048608 | tf_op jit(solution)/shard_map/ppermute | solution.py:64
  179.1 39.7 %all-to-all-start.1 = ((bf16[4,128,1152]{2,1,0:T(8,128)(2,1)}), bf16[4,128,1152]{2,1,0:T(8,128)(2,1)S(1)}, u32[]{:S(2)}, u32[]{:S(2)}) async-start(bf16[4,128,1152]{2,1,0:T(8,128)(2,1)} %maximum_maximum_fusion), calls=%async_computation.1 | async-start | bytes 2359296 | tf_op jit(solution)/shard_map/all_to_all | solution.py:416
  226.6 36.6 %collective-permute-done.16 = bf16[2,128,2048]{2,1,0:T(8,128)(2,1)S(1)} collective-permute-done((bf16[2,128,2048]{2,1,0:T(8,128)(2,1)}, bf16[2,128,2048]{2,1,0:T(8,128)(2,1)S(1)}, u32[]{:S(2)}, u32[]{:S(2)}) %collective-permute-start.16) | collective-permute-done | bytes 1048608 | tf_op jit(solution)/shard_map/ppermute | solution.py:65
  278.3 11.8 %norm_rows.1 = (bf16[2048,2048]{1,0:T(8,128)(2,1)S(1)}, bf16[2048,2048]{1,0:T(8,128)(2,1)}) custom-call(f32[1,2048]{1,0:T(1,128)S(1)} %bitcast.274, f32[1,2048]{1,0:T(1,128)S(1)} %bitcast.277, bf16[1024,2048]{1,0:T(8,128)(2,1)} %bitcast.13.own_ref, bf16[1024,2048]{1,0:T(8,128)(2,1)} %collective-permute-done.10.other_ref), custom_call_target="tpu_custom_call" | custom-call | flops 41943040 | bytes 25165824 | tf_op jit(solution)/shard_map/norm_rows/pallas_call | solution.py:315
  294.0 10.0 %fusion.6 = f32[2048,768]{1,0:T(8,128)S(1)} fusion(bf16[2048,2048]{1,0:T(8,128)(2,1)} %copy-done.2, bf16[2048,1024]{1,0:T(8,128)(2,1)} %bitcast.321), kind=kOutput, calls=%fused_computation.17 | convolution fusion | flops 6442450944 | bytes 17825792 | tf_op jit(solution)/shard_map/dot_general | solution.py:30
  311.0 27.9 %attention_both_ways.1 = (bf16[2,8,128,256]{3,2,1,0:T(8,128)(2,1)S(1)}, bf16[2,8,128,768]{3,2,1,0:T(8,128)(2,1)S(1)}, f32[8,768]{1,0:T(8,128)S(1)}) custom-call(f32[256,256]{1,0:T(8,128)S(1)} %compare_select_fusion.mask_ref, f32[256,256]{1,0:T(8,128)S(1)} %copy.115.cos_ref, f32[256,256]{1,0:T(8,128)S(1)} %copy.116.left_ref, f32[256,256]{1,0:T(8,128)S(1)} %copy.117.right_ref, ...), custom_call_target="tpu_custom_call" | custom-call | flops 7516192768 | bytes 15728640 | tf_op jit(solution)/shard_map/attention_both_ways/pallas_call | solution.py:190
  356.3 12.1 %fusion.2 = f32[2048,768]{1,0:T(8,128)} fusion(bf16[2048,2048]{1,0:T(8,128)(2,1)} %copy-done.2, bf16[2048,1152]{1,0:T(8,128)(2,1)} %bitcast.313), kind=kOutput, calls=%fused_computation.13 | convolution fusion | flops 6442450944 | bytes 17825792 | tf_op jit(solution)/shard_map/dot_general | solution.py:30
  368.4 12.0 %fusion.4 = f32[2048,768]{1,0:T(8,128)} fusion(bf16[2048,2048]{1,0:T(8,128)(2,1)} %copy-done.2, bf16[2048,1152]{1,0:T(8,128)(2,1)} %bitcast.317), kind=kOutput, calls=%fused_computation.15 | convolution fusion | flops 6442450944 | bytes 17825792 | tf_op jit(solution)/shard_map/dot_general | solution.py:30
  380.4 13.0 %multiply_convert_fusion.1 = (bf16[2048,384]{1,0:T(8,128)(2,1)S(1)}, bf16[2048,384]{1,0:T(8,128)(2,1)}, bf16[2048,384]{1,0:T(8,128)(2,1)S(1)}) fusion(f32[2048,768]{1,0:T(8,128)} %fusion.2, bf16[2048,1152]{1,0:T(8,128)(2,1)} %bitcast.314, bf16[1024,2048]{1,0:T(8,128)(2,1)} %collective-permute-done.17, bf16[1024,2048]{1,0:T(8,128)(2,1)} %bitcast.40), kind=kOutput, calls=%fused_computation.22 | convolution fusion | flops 3249799168 | bytes 20971520 | tf_op jit(solution)/shard_map/dot_general | solution.py:30
  393.5 9.9 %convolution_convert_fusion.1 = bf16[2048,768]{1,0:T(8,128)(2,1)S(1)} fusion(bf16[2048,2048]{1,0:T(8,128)(2,1)S(1)} %bitcast.282, bf16[2048,384]{1,0:T(8,128)(2,1)} %get-tuple-element.62, bf16[2048,384]{1,0:T(8,128)(2,1)S(1)} %get-tuple-element.61), kind=kOutput, calls=%fused_computation.11 | convolution fusion | flops 6450315264 | bytes 14680064 | tf_op jit(solution)/shard_map/dot_general | solution.py:38
  403.4 8.2 %convolution_convert_fusion.3 = bf16[2048,384]{1,0:T(8,128)(2,1)S(1)} fusion(bf16[2048,384]{1,0:T(8,128)(2,1)S(1)} %get-tuple-element.69.refs_2_, bf16[1024,2048]{1,0:T(8,128)(2,1)} %collective-permute-done.17, bf16[1024,2048]{1,0:T(8,128)(2,1)} %bitcast.40), kind=kOutput, calls=%fused_computation.34 | convolution fusion | flops 3238789120 | bytes 11534336 | tf_op jit(solution)/shard_map/dot_general | solution.py:38
  414.1 12.1 %multiply_convert_fusion.3 = (bf16[2048,384]{1,0:T(8,128)(2,1)S(1)}, bf16[2048,384]{1,0:T(8,128)(2,1)S(1)}, bf16[2048,384]{1,0:T(8,128)(2,1)S(1)}) fusion(f32[2048,768]{1,0:T(8,128)} %fusion.4, bf16[2048,1152]{1,0:T(8,128)(2,1)} %bitcast.318, bf16[1024,2048]{1,0:T(8,128)(2,1)} %collective-permute-done.17, bf16[1024,2048]{1,0:T(8,128)(2,1)} %bitcast.40), kind=kOutput, calls=%fused_computation.24 | convolution fusion | flops 3249799168 | bytes 20971520 | tf_op jit(solution)/shard_map/dot_general | solution.py:30
  426.3 18.7 %product_sum.2 = bf16[2048,2048]{1,0:T(8,128)(2,1)} custom-call(bf16[2048,256]{1,0:T(8,128)(2,1)S(1)} %bitcast.289, bf16[2048,384]{1,0:T(8,128)(2,1)S(1)} %get-tuple-element.70.refs_1_, bf16[2048,384]{1,0:T(8,128)(2,1)S(1)} %copy-done.6, bf16[2048,1024]{1,0:T(8,128)(2,1)} %bitcast.323, bf16[2048,1152]{1,0:T(8,128)(2,1)} %bitcast.319, ...), custom_call_target="tpu_custom_call" | custom-call | flops 8589934592 | bytes 16777216 | tf_op jit(solution)/shard_map/product_sum/pallas_call | solution.py:273
  456.4 31.5 %product_sum.3 = (bf16[2048,2048]{1,0:T(8,128)(2,1)}, f32[16,2048]{1,0:T(8,128)S(1)}) custom-call(bf16[2048,768]{1,0:T(8,128)(2,1)S(1)} %bitcast.287, bf16[2048,768]{1,0:T(8,128)(2,1)} %pad_maximum_fusion.4.refs_1_, bf16[2048,768]{1,0:T(8,128)(2,1)} %pad_maximum_fusion.5.refs_2_, bf16[2048,1024]{1,0:T(8,128)(2,1)} %bitcast.324, ...), custom_call_target="tpu_custom_call" | custom-call | flops 19327352832 | bytes 27262976 | tf_op jit(solution)/shard_map/product_sum/pallas_call | solution.py:273
  494.5 8.3 %convolution_convert_fusion.4 = bf16[2048,384]{1,0:T(8,128)(2,1)S(1)} fusion(bf16[2048,384]{1,0:T(8,128)(2,1)S(1)} %get-tuple-element.70.refs_1_, bf16[1024,2048]{1,0:T(8,128)(2,1)} %collective-permute-done.17, bf16[1024,2048]{1,0:T(8,128)(2,1)} %bitcast.40), kind=kOutput, calls=%fused_computation.35 | convolution fusion | flops 3238789120 | bytes 11534336 | tf_op jit(solution)/shard_map/dot_general | solution.py:38
  533.0 12.1 %collective-permute-done.26 = bf16[2,128,2048]{2,1,0:T(8,128)(2,1)S(1)} collective-permute-done((bf16[2,128,2048]{2,1,0:T(8,128)(2,1)S(1)}, bf16[2,128,2048]{2,1,0:T(8,128)(2,1)S(1)}, u32[]{:S(2)}, u32[]{:S(2)}) %collective-permute-start.26) | collective-permute-done | bytes 1048608 | tf_op jit(solution)/shard_map/ppermute | solution.py:84
  578.8 11.3 %collective-permute-done.27 = bf16[2,128,2048]{2,1,0:T(8,128)(2,1)} collective-permute-done((bf16[2,128,2048]{2,1,0:T(8,128)(2,1)}, bf16[2,128,2048]{2,1,0:T(8,128)(2,1)}, u32[]{:S(2)}, u32[]{:S(2)}) %collective-permute-start.27) | collective-permute-done | bytes 1048608 | tf_op jit(solution)/shard_map/ppermute | solution.py:84
  616.1 14.7 %collective-permute-done.35 = f32[5,2048]{1,0:T(8,128)S(1)} collective-permute-done((f32[5,2048]{1,0:T(8,128)S(1)}, f32[5,2048]{1,0:T(8,128)S(1)}, u32[]{:S(2)}, u32[]{:S(2)}) %collective-permute-start.35) | collective-permute-done | bytes 40992 | tf_op jit(solution)/shard_map/ppermute | solution.py:111
  642.3 31.4 %collective-permute-done.36 = f32[5,2048]{1,0:T(8,128)S(1)} collective-permute-done((f32[5,2048]{1,0:T(8,128)S(1)}, f32[5,2048]{1,0:T(8,128)S(1)}, u32[]{:S(2)}, u32[]{:S(2)}) %collective-permute-start.36) | collective-permute-done | bytes 40992 | tf_op jit(solution)/shard_map/ppermute | solution.py:111
  682.5 13.8 %collective-permute-done.21 = bf16[2,128,2048]{2,1,0:T(8,128)(2,1)} collective-permute-done((bf16[2,128,2048]{2,1,0:T(8,128)(2,1)}, bf16[2,128,2048]{2,1,0:T(8,128)(2,1)}, u32[]{:S(2)}, u32[]{:S(2)}) %collective-permute-start.21) | collective-permute-done | bytes 1048608 | tf_op jit(solution)/shard_map/ppermute | solution.py:84
  (385 shorter events, 308.4 us)
Async XLA Ops:
  7.2 286.8 %all-gather.7.cloned.1.call-start = ((), (), s32[]{:S(2)}) async-start(), calls=%async_computation.9 | async-start | bytes 5242880 | tf_op jit(solution)/shard_map/all_gather | solution.py:417
  52.2 62.3 %all-to-all-start.2 = ((bf16[4,128,1152]{2,1,0:T(8,128)(2,1)}), bf16[4,128,1152]{2,1,0:T(8,128)(2,1)}, u32[]{:S(2)}, u32[]{:S(2)}) async-start(bf16[4,128,1152]{2,1,0:T(8,128)(2,1)} %maximum_maximum_fusion.1), calls=%async_computation.2 | async-start | bytes 2359296 | tf_op jit(solution)/shard_map/all_to_all | solution.py:416
  56.7 299.5 %all-gather.11.cloned.1.call-start = ((), (), s32[]{:S(2)}) async-start(), calls=%async_computation.11 | async-start | bytes 5898240 | tf_op jit(solution)/shard_map/all_gather | solution.py:417
  144.2 120.6 %collective-permute-start = (bf16[5,128]{1,0:T(8,128)(2,1)S(1)}, bf16[5,128]{1,0:T(8,128)(2,1)S(1)}, u32[]{:S(2)}, u32[]{:S(2)}) collective-permute-start(bf16[5,128]{1,0:T(8,128)(2,1)S(1)} %convert_element_type.319), channel_id=1, source_target_pairs={{0,2},{2,0},{4,6},{6,4},{1,3},{3,1},{5,7},{7,5},{8,10},{10,8},{12,... | collective-permute-start | bytes 3848 | tf_op jit(solution)/shard_map/ppermute | solution.py:100
  172.3 49.0 %collective-permute-start.15 = (bf16[2,128,2048]{2,1,0:T(8,128)(2,1)S(1)}, bf16[2,128,2048]{2,1,0:T(8,128)(2,1)}, u32[]{:S(2)}, u32[]{:S(2)}) collective-permute-start(bf16[2,128,2048]{2,1,0:T(8,128)(2,1)S(1)} %collective-permute-done.11), channel_id=1, source_target_pairs={{8,0},{16,8},{9,1},{17,9},{10,2},{18,10},{11,3},{19,11},{12,4},{20... | collective-permute-start | bytes 3145736 | tf_op jit(solution)/shard_map/ppermute | solution.py:65
  173.6 49.0 %collective-permute-start.14 = (bf16[2,128,2048]{2,1,0:T(8,128)(2,1)}, bf16[2,128,2048]{2,1,0:T(8,128)(2,1)}, u32[]{:S(2)}, u32[]{:S(2)}) collective-permute-start(bf16[2,128,2048]{2,1,0:T(8,128)(2,1)} %collective-permute-done.13), channel_id=1, source_target_pairs={{16,24},{17,25},{18,26},{19,27},{20,28},{21,29},{22,30},{23,31}} | collective-permute-start | bytes 3145736 | tf_op jit(solution)/shard_map/ppermute | solution.py:64
  177.9 100.4 %collective-permute-start.10 = (bf16[1024,2048]{1,0:T(8,128)(2,1)}, bf16[1024,2048]{1,0:T(8,128)(2,1)}, u32[]{:S(2)}, u32[]{:S(2)}) collective-permute-start(bf16[1024,2048]{1,0:T(8,128)(2,1)} %bitcast.13.own_ref), channel_id=1, source_target_pairs={{0,1},{1,0},{2,3},{3,2},{4,5},{5,4},{6,7},{7,6},{8,9},{9,8},{10,11... | collective-permute-start | bytes 12582920 | tf_op jit(solution)/shard_map/ppermute | solution.py:42
  179.1 97.9 %all-to-all-start.1 = ((bf16[4,128,1152]{2,1,0:T(8,128)(2,1)}), bf16[4,128,1152]{2,1,0:T(8,128)(2,1)S(1)}, u32[]{:S(2)}, u32[]{:S(2)}) async-start(bf16[4,128,1152]{2,1,0:T(8,128)(2,1)} %maximum_maximum_fusion), calls=%async_computation.1 | async-start | bytes 2359296 | tf_op jit(solution)/shard_map/all_to_all | solution.py:416
  218.8 149.6 %all-gather.9.cloned.1.call-start = ((), (), s32[]{:S(2)}) async-start(), calls=%async_computation.10 | async-start | bytes 5898240 | tf_op jit(solution)/shard_map/all_gather | solution.py:417
  278.0 277.6 %reduce-scatter.14.cloned.1.call-start = ((), (), s32[]{:S(2)}) async-start(), calls=%async_computation.14 | async-start | bytes 5242880
  356.2 244.3 %reduce-scatter.12.cloned.1.call-start = ((), (), s32[]{:S(2)}) async-start(), calls=%async_computation.13 | async-start | bytes 5898240
  414.1 263.7 %reduce-scatter.10.cloned.1.call-start = ((), (), s32[]{:S(2)}) async-start(), calls=%async_computation.12 | async-start | bytes 5898240
  451.3 71.2 %collective-permute-start.18 = (bf16[4,2,128,2048]{3,2,1,0:T(8,128)(2,1)}, bf16[4,2,128,2048]{3,2,1,0:T(8,128)(2,1)}, u32[]{:S(2)}, u32[]{:S(2)}) collective-permute-start(bf16[4,2,128,2048]{3,2,1,0:T(8,128)(2,1)} %bitcast.72), channel_id=1, source_target_pairs={{0,1},{1,0},{2,3},{3,2},{4,5},{5,4},{6,7},{7,6},{8,9},{9,8},{10,11... | collective-permute-start | bytes 12582920 | tf_op jit(solution)/shard_map/ppermute | solution.py:42
  546.8 43.4 %collective-permute-start.27 = (bf16[2,128,2048]{2,1,0:T(8,128)(2,1)}, bf16[2,128,2048]{2,1,0:T(8,128)(2,1)}, u32[]{:S(2)}, u32[]{:S(2)}) collective-permute-start(bf16[2,128,2048]{2,1,0:T(8,128)(2,1)} %get-tuple-element.73), channel_id=1, source_target_pairs={{0,8},{8,16},{1,9},{9,17},{2,10},{10,18},{3,11},{11,19},{4,12},{12... | collective-permute-start | bytes 3145736 | tf_op jit(solution)/shard_map/ppermute | solution.py:84
  555.6 51.4 %all-to-all-start.5 = ((bf16[4,128,1024]{2,1,0:T(8,128)(2,1)}), bf16[4,128,1024]{2,1,0:T(8,128)(2,1)S(1)}, u32[]{:S(2)}, u32[]{:S(2)}) async-start(bf16[4,128,1024]{2,1,0:T(8,128)(2,1)} %bitcast.309), calls=%async_computation.5 | async-start | bytes 2097152 | tf_op jit(solution)/shard_map/all_to_all | solution.py:477
  571.6 61.5 %collective-permute-start.20 = (bf16[2,128,2048]{2,1,0:T(8,128)(2,1)}, bf16[2,128,2048]{2,1,0:T(8,128)(2,1)}, u32[]{:S(2)}, u32[]{:S(2)}) collective-permute-start(bf16[2,128,2048]{2,1,0:T(8,128)(2,1)} %get-tuple-element.79), channel_id=1, source_target_pairs={{0,8},{8,16},{1,9},{9,17},{2,10},{10,18},{3,11},{11,19},{4,12},{12... | collective-permute-start | bytes 3145736 | tf_op jit(solution)/shard_map/ppermute | solution.py:84
  577.1 56.1 %collective-permute-start.23 = (bf16[2,128,2048]{2,1,0:T(8,128)(2,1)}, bf16[2,128,2048]{2,1,0:T(8,128)(2,1)}, u32[]{:S(2)}, u32[]{:S(2)}) collective-permute-start(bf16[2,128,2048]{2,1,0:T(8,128)(2,1)} %get-tuple-element.80), channel_id=1, source_target_pairs={{16,8},{24,16},{17,9},{25,17},{18,10},{26,18},{19,11},{27,19},{20,... | collective-permute-start | bytes 3145736 | tf_op jit(solution)/shard_map/ppermute | solution.py:85
  578.7 52.1 %collective-permute-start.35 = (f32[5,2048]{1,0:T(8,128)S(1)}, f32[5,2048]{1,0:T(8,128)S(1)}, u32[]{:S(2)}, u32[]{:S(2)}) collective-permute-start(f32[5,2048]{1,0:T(8,128)S(1)} %add.315), channel_id=1, source_target_pairs={{0,8},{8,0},{16,24},{24,16},{1,9},{9,1},{17,25},{25,17},{2,10},{10... | collective-permute-start | bytes 122888 | tf_op jit(solution)/shard_map/ppermute | solution.py:111
  593.8 81.2 %collective-permute-start.28 = (bf16[2,128,2048]{2,1,0:T(8,128)(2,1)}, bf16[2,128,2048]{2,1,0:T(8,128)(2,1)}, u32[]{:S(2)}, u32[]{:S(2)}) collective-permute-start(bf16[2,128,2048]{2,1,0:T(8,128)(2,1)} %get-tuple-element.71), channel_id=1, source_target_pairs={{0,8},{8,16},{16,24},{1,9},{9,17},{17,25},{2,10},{10,18},{18,26},{... | collective-permute-start | bytes 3145736 | tf_op jit(solution)/shard_map/ppermute | solution.py:84
  599.2 75.8 %collective-permute-start.31 = (bf16[2,128,2048]{2,1,0:T(8,128)(2,1)}, bf16[2,128,2048]{2,1,0:T(8,128)(2,1)}, u32[]{:S(2)}, u32[]{:S(2)}) collective-permute-start(bf16[2,128,2048]{2,1,0:T(8,128)(2,1)} %get-tuple-element.72), channel_id=1, source_target_pairs={{8,0},{16,8},{24,16},{9,1},{17,9},{25,17},{10,2},{18,10},{26,18},{... | collective-permute-start | bytes 3145736 | tf_op jit(solution)/shard_map/ppermute | solution.py:85
  608.0 69.8 %all-to-all-start.4 = ((bf16[4,128,1152]{2,1,0:T(8,128)(2,1)}), bf16[4,128,1152]{2,1,0:T(8,128)(2,1)S(1)}, u32[]{:S(2)}, u32[]{:S(2)}) async-start(bf16[4,128,1152]{2,1,0:T(8,128)(2,1)} %bitcast.305), calls=%async_computation.4 | async-start | bytes 2359296 | tf_op jit(solution)/shard_map/all_to_all | solution.py:477
  637.5 58.7 %collective-permute-start.21 = (bf16[2,128,2048]{2,1,0:T(8,128)(2,1)}, bf16[2,128,2048]{2,1,0:T(8,128)(2,1)}, u32[]{:S(2)}, u32[]{:S(2)}) collective-permute-start(bf16[2,128,2048]{2,1,0:T(8,128)(2,1)} %get-tuple-element.77), channel_id=1, source_target_pairs={{0,8},{8,16},{16,24},{1,9},{9,17},{17,25},{2,10},{10,18},{18,26},{... | collective-permute-start | bytes 3145736 | tf_op jit(solution)/shard_map/ppermute | solution.py:84
  640.8 55.5 %collective-permute-start.24 = (bf16[2,128,2048]{2,1,0:T(8,128)(2,1)}, bf16[2,128,2048]{2,1,0:T(8,128)(2,1)}, u32[]{:S(2)}, u32[]{:S(2)}) collective-permute-start(bf16[2,128,2048]{2,1,0:T(8,128)(2,1)} %get-tuple-element.78), channel_id=1, source_target_pairs={{8,0},{16,8},{24,16},{9,1},{17,9},{25,17},{10,2},{18,10},{26,18},{... | collective-permute-start | bytes 3145736 | tf_op jit(solution)/shard_map/ppermute | solution.py:85
  677.8 43.0 %all-to-all-start.3 = ((bf16[4,128,1152]{2,1,0:T(8,128)(2,1)}), bf16[4,128,1152]{2,1,0:T(8,128)(2,1)S(1)}, u32[]{:S(2)}, u32[]{:S(2)}) async-start(bf16[4,128,1152]{2,1,0:T(8,128)(2,1)} %bitcast.304), calls=%async_computation.3 | async-start | bytes 2359296 | tf_op jit(solution)/shard_map/all_to_all | solution.py:477
  (97 other events, 1492.5 us)
Sparse Core Ops, SparseCore 0:
  42.3 51.8 all-gather.6
  114.7 62.5 all-gather.10
  278.2 55.5 all-gather.8
  356.3 51.2 reduce-scatter.13
  414.2 55.7 reduce-scatter.11
  513.0 56.5 reduce-scatter.9

commit v2 on v1

v2 whole, which is shorter than its diff:
```python
import functools
import jax
import jax.numpy as jnp
from jax import lax
from jax.experimental import pallas as pl
from jax.experimental.pallas import tpu as pltpu
from jax.sharding import Mesh
from jax.sharding import PartitionSpec as P

HD = 64
ROT = 16
MICRO = 2
STEP = 5
QUAD = 4

EPS_NORM = 1e-05
CLIP = 1.0
BETA_ONE = 0.5
BETA_TWO = 0.5
ADAM_EPS = 1e-08
DECAY = 0.1
SMALL_RATE = 0.2
ROPE_BASE = 10000.0
LOW = jnp.bfloat16
F32 = jnp.float32
SWAP = [(0, 1), (1, 0)]


def nn(left, right):
    return lax.dot_general(left, right, (((1,), (0,)), ((), ())), preferred_element_type=F32)


def nt(left, right):
    return lax.dot_general(left, right, (((1,), (1,)), ((), ())), preferred_element_type=F32)


def tn(left, right):
    return lax.dot_general(left, right, (((0,), (0,)), ((), ())), preferred_element_type=F32)


def swap(value, axis):
    return lax.ppermute(value, axis, SWAP)


ANYWHERE = pl.BlockSpec(memory_space=pl.ANY)
BIG = 56 * 1024 * 1024


def launch(kernel, name, grid, operands, in_specs, out_specs, out_shape, flops, deps=(), lead=(), aliases=None):
    count, extra, ahead = len(operands), len(deps), len(lead)

    def run(*refs):
        refs = refs[ahead:]
        kernel(*refs[:count], *refs[count + extra :])

    shapes = out_shape if isinstance(out_shape, list) else [out_shape]
    moved = sum(v.size * v.dtype.itemsize for v in operands)
    moved += sum(s.size * s.dtype.itemsize for s in shapes)
    return pl.pallas_call(
        run,
        grid_spec=pltpu.PrefetchScalarGridSpec(
            num_scalar_prefetch=ahead,
            grid=grid,
            in_specs=list(in_specs) + [ANYWHERE] * extra,
            out_specs=out_specs,
        ),
        out_shape=out_shape,
        input_output_aliases={len(lead) + k: v for k, v in (aliases or {}).items()},
        cost_estimate=pl.CostEstimate(flops=flops, bytes_accessed=moved, transcendentals=0),
        compiler_params=pltpu.CompilerParams(vmem_limit_bytes=BIG),
        name=name,
    )(*lead, *operands, *deps)


def gate_kernel(*refs):
    pass


def after(value, *others):
    if not others:
        return value
    return pl.pallas_call(
        gate_kernel,
        in_specs=[ANYWHERE] * (1 + len(others)),
        out_specs=ANYWHERE,
        out_shape=jax.ShapeDtypeStruct(value.shape, value.dtype),
        input_output_aliases={0: 0},
        name="after",
    )(value, *others)


def blank(shape, dtype):
    return pl.pallas_call(
        gate_kernel,
        out_specs=ANYWHERE,
        out_shape=jax.ShapeDtypeStruct(shape, dtype),
        name="blank",
    )()


def held(values, gate):
    return [after(value, *gate) for value in values]


def exchange(blocks, gate):
    out = held(blocks[1:], gate)
    return [blocks[0]] + [
        lax.ppermute(block, "a", [(i, i ^ bit) for i in range(QUAD)])
        for bit, block in enumerate(out, 1)
    ]


class Plane:
    def __init__(self):
        self.square = lax.axis_size("x") == 2
        self.count = lax.axis_size("x") * lax.axis_size("y")
        self.at = lax.axis_index(("y", "x"))

    def gather_first(self, mine, gate):
        if not self.square:
            return (mine,)
        to_x, to_y = held([mine, mine], gate)
        return (mine, swap(to_x, "x"), swap(to_y, "y"))

    def gather_second(self, known, gate):
        mine = known[0]
        if not self.square:
            return lax.all_gather(mine, ("y", "x"), axis=1, tiled=True), ()
        half = QUAD // 2
        upper, lower = held([known[1][:half], known[2][half:]], gate)
        last = (swap(upper, "y"), swap(lower, "x"))
        rows = mine.shape[1]
        whole = blank((QUAD, self.count * rows, mine.shape[2]), mine.dtype)
        for bits, block, first in (
            (0, mine, 0),
            (1, known[1], 0),
            (2, known[2], 0),
            (3, last[0], 0),
            (3, last[1], half),
        ):
            at = jnp.bitwise_xor(self.at, bits) * rows
            whole = lax.dynamic_update_slice(whole, block, (first, at, 0))
        return whole, last

    def part(self, term, bits):
        rows = term.shape[1] // self.count
        return lax.dynamic_slice_in_dim(term, jnp.bitwise_xor(self.at, bits) * rows, rows, 1)

    def sum_first(self, term, gate):
        if not self.square:
            return (term,)
        half = QUAD // 2
        across = self.part(term, 3)
        upper, lower = held([across[:half], across[half:]], gate)
        return (term, swap(upper, "y"), swap(lower, "x"))

    def sum_second(self, known, gate):
        term = known[0]
        if not self.square:
            return lax.psum_scatter(term, ("y", "x"), scatter_dimension=1, tiled=True), ()
        half = QUAD // 2
        to_x, to_y = self.part(term, 1), self.part(term, 2)
        to_x = jnp.concatenate([add_low(to_x[:half], known[1]), to_x[half:]])
        to_y = jnp.concatenate([to_y[:half], add_low(to_y[half:], known[2])])
        to_x, to_y = held([to_x, to_y], gate)
        last = (swap(to_x, "x"), swap(to_y, "y"))
        total = self.part(term, 0).astype(F32) + last[0].astype(F32) + last[1].astype(F32)
        return total, last


def add_low(left, right):
    return (left.astype(F32) + right.astype(F32)).astype(LOW)


def bits(axis):
    found, bit = [], 1
    count, at = lax.axis_size(axis), lax.axis_index(axis)
    while bit < count:
        found.append((axis, [(i, i ^ bit) for i in range(count)], (at // bit) % 2))
        bit *= 2
    return found


def gather_small(value):
    for axis, pairs, bit in bits("x") + bits("y") + bits("a"):
        other = lax.ppermute(value, axis, pairs)
        value = jnp.where(
            bit == 0,
            jnp.concatenate([value, other], axis=-1),
            jnp.concatenate([other, value], axis=-1),
        )
    return value


def sum_small(value):
    for axis, pairs, bit in bits("tp") + bits("x") + bits("y") + bits("a"):
        value = value + lax.ppermute(value, axis, pairs)
    return value


def attention_kernel(
    mask_ref, cos_ref, left_ref, right_ref, bias_ref, joined_ref, back_ref, mixed_ref, grad_ref, bias_grad_ref
):
    rows, width = cos_ref.shape
    heads = width // HD
    scale = HD ** (-0.5)
    joined = joined_ref[...].reshape(rows, 3 * width) + bias_ref[0:1, :]
    cos, left, right = cos_ref[...], left_ref[...], right_ref[...]

    def turn(v):
        return v * cos + pltpu.roll(v, width - ROT // 2, 1) * left + pltpu.roll(v, ROT // 2, 1) * right

    def turn_back(g):
        return g * cos - (pltpu.roll(g, width - ROT // 2, 1) * left + pltpu.roll(g, ROT // 2, 1) * right)

    query = turn(joined[:, :width]).astype(LOW)
    keys = turn(joined[:, width : 2 * width]).astype(LOW)
    values = joined[:, 2 * width :].astype(LOW)
    back = back_ref[...].reshape(rows, width)
    mask = mask_ref[...]
    mixed, d_query, d_keys, d_values = [], [], [], []
    for head in range(heads):
        cut = slice(head * HD, (head + 1) * HD)
        q, k, v, g = query[:, cut], keys[:, cut], values[:, cut], back[:, cut]
        scores = nt(q, k) * scale + mask
        peak = jnp.max(scores, axis=-1, keepdims=True)
        raised = jnp.exp(scores - peak)
        full = raised / jnp.sum(raised, axis=-1, keepdims=True)
        probs = full.astype(LOW)
        mixed.append(nn(probs, v))
        prob_grad = nt(g, v)
        weighted = full * prob_grad
        inner = jnp.sum(weighted, axis=-1, keepdims=True)
        score_grad = (weighted - full * inner).astype(LOW)
        d_query.append(nn(score_grad, k) * scale)
        d_keys.append(tn(score_grad, q) * scale)
        d_values.append(tn(probs, g))
    mixed_ref[...] = jnp.concatenate(mixed, axis=-1).astype(LOW).reshape(mixed_ref.shape)
    out = jnp.concatenate(
        [
            turn_back(jnp.concatenate(d_query, axis=-1)),
            turn_back(jnp.concatenate(d_keys, axis=-1)),
            jnp.concatenate(d_values, axis=-1),
        ],
        axis=-1,
    ).astype(LOW)
    grad_ref[...] = out.reshape(grad_ref.shape)

    @pl.when(pl.program_id(0) == 0)
    def _():
        bias_grad_ref[...] = jnp.zeros_like(bias_grad_ref)

    sums = jnp.sum(out.astype(F32).reshape(rows // 8, 8, 3 * width), axis=0)
    bias_grad_ref[...] += sums


def attention(joined, back, bias):
    tokens, width = back.shape
    half = 128
    seqs = tokens // (2 * half)
    length = 2 * half
    position = jnp.arange(length)
    mask = jnp.where(position[:, None] >= position[None, :], 0.0, -jnp.inf).astype(F32)
    frequency = ROPE_BASE ** (-(2.0 * jnp.arange(ROT // 2, dtype=F32)) / ROT)
    angles = position.astype(F32)[:, None] * frequency[None, :]
    cosine, sine = jnp.cos(angles), jnp.sin(angles)
    rest = jnp.ones((length, HD - ROT), F32)
    nothing = jnp.zeros((length, ROT // 2), F32)
    heads = width // HD
    cos = jnp.tile(jnp.concatenate([cosine, cosine, rest], 1), (1, heads))
    left = jnp.tile(jnp.concatenate([-sine, nothing, 0.0 * rest], 1), (1, heads))
    right = jnp.tile(jnp.concatenate([nothing, sine, 0.0 * rest], 1), (1, heads))
    fixed = lambda i: (0, 0)
    rows = lambda i: (i // MICRO, 0, i % MICRO, 0, 0)
    shape = lambda w: (seqs // MICRO, 2, MICRO, half, w)
    mixed, grad, bias_grad = pl.pallas_call(
        attention_kernel,
        grid=(seqs,),
        in_specs=[
            pl.BlockSpec((length, length), fixed),
            pl.BlockSpec((length, width), fixed),
            pl.BlockSpec((length, width), fixed),
            pl.BlockSpec((length, width), fixed),
            pl.BlockSpec((1, 3 * width), fixed),
            pl.BlockSpec((1, 2, 1, half, 3 * width), rows),
            pl.BlockSpec((1, 2, 1, half, width), rows),
        ],
        out_specs=[
            pl.BlockSpec((1, 2, 1, half, width), rows),
            pl.BlockSpec((1, 2, 1, half, 3 * width), rows),
            pl.BlockSpec((8, 3 * width), fixed),
        ],
        out_shape=[
            jax.ShapeDtypeStruct(shape(width), LOW),
            jax.ShapeDtypeStruct(shape(3 * width), LOW),
            jax.ShapeDtypeStruct((8, 3 * width), F32),
        ],
        cost_estimate=pl.CostEstimate(
            flops=seqs * heads * 7 * 2 * length * length * HD * 4,
            bytes_accessed=tokens * width * 30,
            transcendentals=seqs * heads * length * length,
        ),
        compiler_params=pltpu.CompilerParams(vmem_limit_bytes=32 * 1024 * 1024),
        name="attention_both_ways",
    )(mask, cos, left, right, bias, joined.reshape(shape(3 * width)), back.reshape(shape(width)))
    return (
        mixed.reshape(tokens, width),
        grad.reshape(tokens, 3 * width),
        jnp.sum(bias_grad, axis=0),
    )


def norm_kernel(gain_ref, shift_ref, rows_ref, normed_ref, xhat_ref):
    rows = rows_ref[...].astype(F32)
    average = jnp.mean(rows, axis=-1, keepdims=True)
    centred = rows - average
    variance = jnp.mean(centred * centred, axis=-1, keepdims=True)
    xhat = centred * lax.rsqrt(variance + EPS_NORM)
    xhat_ref[...] = xhat.astype(LOW)
    normed_ref[...] = (xhat * gain_ref[...] + shift_ref[...]).astype(LOW)


def by_row(i):
    return (i, 0)


def fixed(*grid):
    return (0, 0)


def norm_rows(rows, gain, shift, deps=()):
    tokens, depth = rows.shape
    tall = 256
    return launch(
        norm_kernel,
        "norm_rows",
        (tokens // tall,),
        [gain, shift, rows],
        [pl.BlockSpec((1, depth), fixed)] * 2 + [pl.BlockSpec((tall, depth), by_row)],
        [pl.BlockSpec((tall, depth), by_row)] * 2,
        [jax.ShapeDtypeStruct((tokens, depth), LOW)] * 2,
        20 * tokens * depth,
        deps,
    )


def columns_of(weight, at, width):
    return pl.BlockSpec((weight.shape[0], width), lambda i: (0, at))


def times_kernel(rows_ref, weight_ref, out_ref):
    out_ref[...] = nn(rows_ref[...], weight_ref[...]).astype(out_ref.dtype)


def times(rows, weight, at, width, dtype, deps=()):
    tokens, depth = rows.shape
    tall = 512
    return launch(
        times_kernel,
        "times",
        (tokens // tall,),
        [rows, weight],
        [pl.BlockSpec((tall, depth), by_row), columns_of(weight, at, width)],
        pl.BlockSpec((tall, width), by_row),
        jax.ShapeDtypeStruct((tokens, width), dtype),
        2 * tokens * depth * width,
        deps,
    )


def gate_up_kernel(rows_ref, weight_ref, act_ref, silu_ref, slope_ref):
    width = silu_ref.shape[1]
    both = nn(rows_ref[...], weight_ref[...])
    gate, up = both[:, :width], both[:, width:]
    sigma = 1.0 / (1.0 + jnp.exp(-gate))
    silu = gate * sigma
    act_ref[...] = (silu * up).astype(LOW)
    silu_ref[...] = silu
    slope_ref[...] = up * sigma * (1.0 + gate * (1.0 - sigma))


def gate_up(rows, weight, deps=()):
    tokens, depth = rows.shape
    width = weight.shape[1] // 2
    tall = 512
    return launch(
        gate_up_kernel,
        "gate_up",
        (tokens // tall,),
        [rows, weight],
        [pl.BlockSpec((tall, depth), by_row), pl.BlockSpec(weight.shape, fixed)],
        [pl.BlockSpec((tall, width), by_row)] * 3,
        [jax.ShapeDtypeStruct((tokens, width), dtype) for dtype in (LOW, F32, F32)],
        4 * tokens * depth * width,
        deps,
    )


def gate_up_back_kernel(rows_ref, weight_ref, silu_ref, slope_ref, out_ref):
    width = silu_ref.shape[1]
    act_grad = nn(rows_ref[...], weight_ref[...])
    out_ref[:, :width] = (act_grad * slope_ref[...]).astype(LOW)
    out_ref[:, width:] = (act_grad * silu_ref[...]).astype(LOW)


def gate_up_back(rows, weight, silu, slope, deps=()):
    tokens, depth = rows.shape
    width = weight.shape[1]
    tall = 512
    return launch(
        gate_up_back_kernel,
        "gate_up_back",
        (tokens // tall,),
        [rows, weight, silu, slope],
        [pl.BlockSpec((tall, depth), by_row), pl.BlockSpec(weight.shape, fixed)]
        + [pl.BlockSpec((tall, width), by_row)] * 2,
        pl.BlockSpec((tall, 2 * width), by_row),
        jax.ShapeDtypeStruct((tokens, 2 * width), LOW),
        2 * tokens * depth * width,
        deps,
    )


def term_kernel(*refs):
    out_ref = refs[-1]
    at = 0
    for grads_ref, rows_ref in zip(refs[0:-1:2], refs[1:-1:2]):
        width = grads_ref.shape[1]
        out_ref[:, at : at + width] = tn(rows_ref[...], grads_ref[...]).astype(LOW)
        at += width


def weight_term(items, deps=()):
    operands, in_specs = [], []
    broad = 512
    for grads, rows in items:
        operands += [grads, rows]
        in_specs.append(pl.BlockSpec(grads.shape, fixed))
        in_specs.append(pl.BlockSpec((rows.shape[0], broad), lambda j: (0, j)))
    tokens, depth = rows.shape
    width = sum(grads.shape[1] for grads, _ in items)
    return launch(
        term_kernel,
        "weight_term",
        (depth // broad,),
        operands,
        in_specs,
        pl.BlockSpec((broad, width), by_row),
        jax.ShapeDtypeStruct((depth, width), LOW),
        2 * tokens * depth * width,
        deps,
    )


def product_kernel(terms, with_xhat, *refs):
    lefts, rights, rest = refs[:terms], refs[terms : 2 * terms], refs[2 * terms :]
    total = nt(lefts[0][...], rights[0][...])
    for left, right in zip(lefts[1:], rights[1:]):
        total += nt(left[...], right[...])
    if not with_xhat:
        rest[-1][...] = total.astype(LOW)
        return
    xhat_ref, out_ref, sums_ref = rest[0], rest[-2], rest[-1]
    out_ref[...] = total.astype(LOW)
    xhat = xhat_ref[...].astype(F32)

    @pl.when(pl.program_id(0) == 0)
    def _():
        sums_ref[...] = jnp.zeros_like(sums_ref)

    tall = total.shape[0] // 8
    sums_ref[0:8, :] += jnp.sum((total * xhat).reshape(tall, 8, -1), axis=0)
    sums_ref[8:16, :] += jnp.sum(total.reshape(tall, 8, -1), axis=0)


def product_sum(pairs, depth, xhat=None, deps=(), part=None, into=None):
    tall = 512
    terms = len(pairs)
    rows = pairs[0][0].shape[0]
    steps = rows // tall if part is None else rows // tall // 2
    first = steps * (part or 0)
    below = lambda i: (i + first, 0)
    in_specs = [pl.BlockSpec((tall, left.shape[1]), below) for left, _, _ in pairs]
    in_specs += [columns_of(right, at, left.shape[1]) for left, right, at in pairs]
    operands = [p[0] for p in pairs] + [p[1] for p in pairs]
    out_specs = [pl.BlockSpec((tall, depth), below)]
    out_shape = [jax.ShapeDtypeStruct((rows, depth), LOW)]
    if xhat is not None:
        in_specs.append(pl.BlockSpec((tall, depth), below))
        operands.append(xhat)
        out_specs.append(pl.BlockSpec((16, depth), fixed))
        out_shape.append(jax.ShapeDtypeStruct((16, depth), F32))
    aliases = {}
    if into is not None:
        aliases = {len(operands): 0}
        in_specs.append(ANYWHERE)
        operands.append(into)
    deep = sum(left.shape[1] for left, _, _ in pairs)
    found = launch(
        functools.partial(product_kernel, terms, xhat is not None),
        "product_sum",
        (steps,),
        operands,
        in_specs,
        out_specs,
        out_shape,
        2 * steps * tall * depth * deep,
        deps,
        (),
        aliases,
    )
    return found if xhat is not None else (found[0], None)


def adamw(master, first_old, second_old, gradient, factor, step_rate, weight_decay):
    clipped = gradient * factor
    moment = BETA_ONE * first_old + (1.0 - BETA_ONE) * clipped
    variance = BETA_TWO * second_old + (1.0 - BETA_TWO) * clipped * clipped
    moment_hat = moment / (1.0 - BETA_ONE**STEP)
    variance_hat = variance / (1.0 - BETA_TWO**STEP)
    updated = master - step_rate * (
        moment_hat / (jnp.sqrt(variance_hat) + ADAM_EPS) + weight_decay * master
    )
    return (updated, moment, variance, updated.astype(LOW))


def on_device(
    inputs,
    cotangent,
    joined_master,
    joined_first,
    joined_second,
    outward_master,
    outward_first,
    outward_second,
    gated_master,
    gated_first,
    gated_second,
    downward_master,
    downward_first,
    downward_second,
    vectors_master,
    vectors_first,
    vectors_second,
):
    tp_count = lax.axis_size("tp")
    plane = Plane()
    place = lax.axis_index("a")
    tp_index = lax.axis_index("tp")
    depth = inputs.shape[-1]
    rows_here = joined_master.shape[1]
    att_width = joined_master.shape[2] // QUAD
    ff_here = gated_master.shape[2]
    tiles = ff_here // 128
    wide = -(-tiles // QUAD)
    ff_width = wide * 128
    shortage = wide * QUAD - tiles

    lacking = QUAD - shortage
    firsts = [index * wide - max(0, index - lacking) for index in range(QUAD)]
    skips = [(first - min(first, tiles - wide)) * 128 for first in firsts]
    lengths = [(wide - (index >= lacking)) * 128 for index in range(QUAD)]

    def attention_piece(index):
        cut = lambda w: lax.dynamic_slice_in_dim(w, index * att_width, att_width, 1)
        return jnp.concatenate(
            [cut(joined_master[c]) for c in range(3)] + [cut(outward_master)], axis=1
        ).astype(LOW)

    def hidden_cut(w, index):
        first = index * wide - jnp.maximum(0, index - lacking)
        start = jnp.minimum(first, tiles - wide)
        skip = (first - start) * 128
        length = jnp.where(index >= lacking, wide - 1, wide) * 128
        column = lax.broadcasted_iota(jnp.int32, (1, ff_width), 1)
        keep = (column >= skip) & (column < skip + length)
        part = lax.dynamic_slice_in_dim(w, start * 128, ff_width, 1)
        return jnp.where(keep, part, 0.0).astype(LOW)

    def gated_piece(index):
        return jnp.concatenate([hidden_cut(gated_master[c], index) for c in range(2)], axis=1)

    def downward_piece(index):
        return hidden_cut(downward_master, index)

    def other(bit):
        return jnp.bitwise_xor(place, bit)

    def pieces(make):
        return [make(other(bits)) for bits in range(QUAD)]

    def ordered(blocks):
        stacked = jnp.stack(blocks)
        return jnp.stack(
            [lax.dynamic_index_in_dim(stacked, other(j), 0, False) for j in range(QUAD)]
        )

    vectors_low = gather_small(vectors_master.astype(LOW))
    vectors_full = vectors_low.astype(F32)
    row_gain, row_shift = vectors_full[0:1], vectors_full[1:2]
    bias_at = (tp_index * QUAD + place) * att_width
    bias_here = lax.dynamic_slice_in_dim(vectors_full[2:5], bias_at, att_width, 1).reshape(1, 3 * att_width)

    own_rows, own_back = inputs[:, 0], cotangent[:, 0]
    line = ("a", "tp")
    rows_all = lax.all_gather(own_rows, line, axis=0).reshape(-1, depth)
    back_all = lax.all_gather(own_back, line, axis=0).reshape(-1, depth)

    def flat(weight):
        return weight.reshape(depth, weight.shape[-1])

    joined = exchange(pieces(attention_piece), (vectors_low,))
    joined_near = plane.gather_first(ordered(joined), joined[1:])
    gated = exchange(pieces(gated_piece), joined[1:])
    stage = [*joined_near[1:], *gated[1:], rows_all]
    gated_near = plane.gather_first(ordered(gated), stage)
    downward = exchange(pieces(downward_piece), stage)
    normed, xhat_all = norm_rows(rows_all, row_gain, row_shift)
    stage = [*gated_near[1:], *downward[1:], normed]
    gated_weight, last = plane.gather_second(gated_near, stage)
    gated_weight = flat(gated_weight)
    downward_near = plane.gather_first(ordered(downward), stage)
    stage = [*last, *downward_near[1:]]
    attention_weight, joined_last = plane.gather_second(joined_near, stage)
    attention_weight = flat(attention_weight)
    downward_weight, last = plane.gather_second(downward_near, stage)
    downward_weight = flat(downward_weight)
    activated, silu, slope = gate_up(normed, gated_weight)
    joined_out = times(normed, attention_weight, 0, 3 * att_width, F32, (activated, *last))
    downward_term = weight_term([(activated, back_all)], (joined_out,))
    mixed_grad = times(back_all, attention_weight, 3, att_width, LOW, (downward_term,))
    mixed, joined_grad, bias_grad = attention(joined_out, mixed_grad, bias_here)

    def fold(term):
        return term.reshape(QUAD, depth // QUAD, term.shape[1])

    def homeward(total, gate):
        total = total.astype(LOW)
        return exchange(
            [lax.dynamic_index_in_dim(total, other(bits), 0, False) for bits in range(QUAD)], gate
        )

    def scatter_rows(part):
        folded = part.reshape(2 * QUAD, MICRO, 128, depth)
        return lax.psum_scatter(folded, line, scatter_dimension=0)

    downward_total = lax.psum_scatter(
        fold(downward_term), ("y", "x"), scatter_dimension=1, tiled=True
    )
    out_part, _ = product_sum([(mixed, attention_weight, 3), (activated, downward_weight, 0)], depth)
    branch = scatter_rows(out_part)
    attention_term = weight_term([(joined_grad, normed), (mixed, back_all)], (out_part,))
    joined_known = plane.sum_first(fold(attention_term), ())
    gated_grad = gate_up_back(back_all, downward_weight, silu, slope, (attention_term,))
    gated_term = weight_term([(gated_grad, normed)], joined_known[1:])
    joined_total, last = plane.sum_second(joined_known, joined_known[1:])
    downward_home = homeward(downward_total, joined_known[1:])
    grad_pairs = [(joined_grad, attention_weight, 0), (gated_grad, gated_weight, 0)]
    half_done, sums_low = product_sum(grad_pairs, depth, xhat_all, (gated_term, *last), 0)
    joined_home = homeward(joined_total, last)
    gated_known = plane.sum_first(fold(gated_term), last)
    normed_grad_part, sums_high = product_sum(
        grad_pairs, depth, xhat_all, (*downward_home[1:], *gated_known[1:]), 1, half_done
    )
    gated_total, last = plane.sum_second(gated_known, gated_known[1:])
    own_grad = scatter_rows(after(normed_grad_part, branch, *joined_home[1:], *last)).astype(F32)
    gated_home = homeward(gated_total, [*last, *joined_home[1:]])
    sums = sums_low + sums_high
    branch = branch.astype(F32)

    def settled(home):
        return [block.astype(F32) for block in ordered(home)]

    downward_own, attention_own, gated_own = settled(downward_home), settled(joined_home), settled(gated_home)

    own_float = own_rows.astype(F32)
    outputs = (own_float + branch).astype(LOW)[:, None]
    average = jnp.mean(own_float, axis=-1, keepdims=True)
    centred_own = own_float - average
    inverse_own = lax.rsqrt(jnp.mean(centred_own * centred_own, axis=-1, keepdims=True) + EPS_NORM)
    xhat = centred_own * inverse_own
    scaled = own_grad * row_gain
    rows_grad = inverse_own * (
        scaled
        - jnp.mean(scaled, axis=-1, keepdims=True)
        - xhat * jnp.mean(scaled * xhat, axis=-1, keepdims=True)
    )
    input_grad = (own_back.astype(F32) + rows_grad).astype(LOW)[:, None]

    bias_wide = lax.dynamic_update_slice(
        jnp.zeros((3, depth), F32), bias_grad.reshape(3, att_width), (0, bias_at)
    )
    sums = jnp.sum(sums.reshape(2, 8, depth), axis=1)
    vectors_term = after(jnp.concatenate([sums, bias_wide], axis=0), *last)
    vectors_sum = sum_small(vectors_term)
    vectors_grad = lax.dynamic_slice_in_dim(
        vectors_sum, (place * plane.count + plane.at) * rows_here, rows_here, 1
    )

    def attention_columns(c):
        cut = slice(c * att_width, (c + 1) * att_width)
        return jnp.concatenate([piece[:, cut] for piece in attention_own], axis=1)

    joined_grads = jnp.stack([attention_columns(c) for c in range(3)])
    outward_grads = attention_columns(3)

    def hidden_columns(pieces, c):
        return jnp.concatenate(
            [
                piece[:, c * ff_width + skip : c * ff_width + skip + length]
                for piece, skip, length in zip(pieces, skips, lengths)
            ],
            axis=1,
        )

    gated_grads = jnp.stack([hidden_columns(gated_own, c) for c in range(2)])
    downward_grads = hidden_columns(downward_own, 0)

    square = sum(jnp.sum(own * own) for own in downward_own + attention_own + gated_own)
    square = sum_small(jnp.full((8, 128), square))[0, 0] + jnp.sum(vectors_sum * vectors_sum)
    grad_norm = jnp.sqrt(square)
    factor = jnp.minimum(1.0, CLIP / (grad_norm + 1e-06))
    ff_total = ff_here * tp_count
    return (
        outputs,
        input_grad,
        grad_norm,
        *adamw(joined_master, joined_first, joined_second, joined_grads, factor, depth ** (-0.5), DECAY),
        *adamw(outward_master, outward_first, outward_second, outward_grads, factor, (depth // 32) ** (-0.5), DECAY),
        *adamw(gated_master, gated_first, gated_second, gated_grads, factor, depth ** (-0.5), DECAY),
        *adamw(downward_master, downward_first, downward_second, downward_grads, factor, ff_total ** (-0.5), DECAY),
        *adamw(vectors_master, vectors_first, vectors_second, vectors_grad, factor, SMALL_RATE, 0.0),
    )


def solution(mesh):
    fsdp, tp = mesh.shape["fsdp"], mesh.shape["tp"]
    fine = Mesh(mesh.devices.reshape(QUAD, 2, fsdp // QUAD // 2, tp), ("a", "y", "x", "tp"))
    every = ("a", "y", "x")
    rows = P(None, every, "tp", None)
    stacked = P(None, every, "tp")
    flat = P(every, "tp")
    vectors = P(None, every)
    return jax.shard_map(
        on_device,
        mesh=fine,
        in_specs=(rows,) * 2 + (stacked,) * 3 + (flat,) * 3 + (stacked,) * 3 + (flat,) * 3 + (vectors,) * 3,
        out_specs=(rows,) * 2
        + (P(),)
        + (stacked,) * 4
        + (flat,) * 4
        + (stacked,) * 4
        + (flat,) * 4
        + (vectors,) * 4,
        check_vma=False,
    )
```

time: 786 us -> 651 us (0.83)
  matrix products: 114 us -> 0 us
  Pallas kernels: 89.9 us -> 188 us
  waiting for transfers between devices: 231 us -> 179 us
  blocking collectives: 32.1 us -> 0 us
  other arithmetic: 90.2 us -> 66.3 us
  starting transfers between devices: 131 us -> 120 us
    dot_general x12 -> x0, matrix products: 114 us -> none  [the longest x6 66.3 us: nn(): lax.dot_general(left, right, (((1,), (0,)), ((), ())), preferred_element_...]
    pallas_call x7 -> x49, Pallas kernels: 61.9 us -> 160 us  [the longest x11 160 us: launch(): pl.pallas_call(run, grid_spec=pltpu.PrefetchScalarGridSpec(num_scalar_pre...]
    all_to_all x5 -> x0, starting transfers between devices: 56.9 us -> none  [the longest x2 44.2 us: gather_weight(): mine = lax.all_to_all(pieces, 'a', 0, 0, tiled=True)]
    ppermute x10, waiting for transfers between devices: 51.3 us -> 4.82 us  [sum_small(): value = value + lax.ppermute(value, axis, pairs)]
    ppermute x24 -> x18, waiting for transfers between devices: 164 us -> 119 us  [exchange(): lax.ppermute(block, 'a', [(i, i ^ bit) for i in range(QUAD)])]
    ppermute x4 -> x20, waiting for transfers between devices: 0.01 us -> 39.1 us  [swap(): return lax.ppermute(value, axis, SWAP)]
    all_to_all x1 -> x0, blocking collectives: 32.1 us -> none  [gather_weight(): mine = lax.all_to_all(pieces, 'a', 0, 0, tiled=True)]
    ppermute x4 -> x20, starting transfers between devices: 0.56 us -> 22.2 us  [swap(): return lax.ppermute(value, axis, SWAP)]
  transfers between devices with their start and end apart: 53 -> 57, of which waited for: 20 -> 26; matrix products, arithmetic and copies ran while one was open for 31% -> 16% of each run, Pallas kernels for 12% -> 27%
where the time goes in v2:
time: 651 us; the launch traced here: 647 us
  Pallas kernels  188 us (29%)
  waiting for transfers between devices  179 us (27%)
  starting transfers between devices  120 us (18%)
  local copies, waits for them, and re-layouts  67.6 us (10%)
  other arithmetic  66.3 us (10%)
  between operations  25.2 us (4%)
    pallas_call x11, Pallas kernels, launch(): pl.pallas_call(run, grid_spec=pltpu.PrefetchScalarGridSpec(num_scalar_pre...  160 us
    ppermute x18, waiting for transfers between devices, exchange(): lax.ppermute(block, 'a', [(i, i ^ bit) for i in range(QUAD)])  119 us
    ppermute x18, starting transfers between devices, exchange(): lax.ppermute(block, 'a', [(i, i ^ bit) for i in range(QUAD)])  58 us
    ppermute x20, waiting for transfers between devices, swap(): return lax.ppermute(value, axis, SWAP)  39.1 us
    pallas_call x1, Pallas kernels, attention(): pl.pallas_call(attention_kernel, grid=(seqs,), in_specs=[pl.BlockSpec((le...  28 us
    ppermute x20, starting transfers between devices, swap(): return lax.ppermute(value, axis, SWAP)  22.2 us
    unnamed x192, local copies, waits for them, and re-layouts  21.7 us
    ppermute x10, starting transfers between devices, sum_small(): value = value + lax.ppermute(value, axis, pairs)  18.3 us
  transfers between devices with their start and end apart: 57, of which 26 were waited for; matrix products, arithmetic and copies ran while one was open for 16% of the time, Pallas kernels for 27%

profile of v2, /device:TPU:0, one launch (start us, length us, event | category | flops | bytes accessed | tf_op | source)
XLA Modules:
  0.0 646.6 jit_solution(16280564768937347780)
XLA Ops:
  38.2 18.6 %collective-permute-done.4.refs_1_ = bf16[128,1024]{1,0:T(8,128)(2,1)S(1)} collective-permute-done((bf16[128,1024]{1,0:T(8,128)(2,1)}, bf16[128,1024]{1,0:T(8,128)(2,1)S(1)}, u32[]{:S(2)}, u32[]{:S(2)}) %collective-permute-start.4) | collective-permute-done | bytes 262176 | tf_op jit(solution)/shard_map/ppermute | solution.py:108
  56.8 12.3 %collective-permute-done.5.refs_2_ = bf16[128,1024]{1,0:T(8,128)(2,1)S(1)} collective-permute-done((bf16[128,1024]{1,0:T(8,128)(2,1)}, bf16[128,1024]{1,0:T(8,128)(2,1)S(1)}, u32[]{:S(2)}, u32[]{:S(2)}) %collective-permute-start.5) | collective-permute-done | bytes 262176 | tf_op jit(solution)/shard_map/ppermute | solution.py:108
  70.5 19.0 %collective-permute-start.9 = (bf16[128,1536]{1,0:T(8,128)(2,1)}, bf16[128,1536]{1,0:T(8,128)(2,1)S(1)}, u32[]{:S(2)}, u32[]{:S(2)}) collective-permute-start(bf16[128,1536]{1,0:T(8,128)(2,1)} %after.39), channel_id=1, source_target_pairs={{0,8},{8,0},{16,24},{24,16},{1,9},{9,1},{17,25},{25,17},{2,10},{10... | collective-permute-start | bytes 1179656 | tf_op jit(solution)/shard_map/ppermute | solution.py:108
  97.6 16.2 %collective-permute-done.9.refs_3_ = bf16[128,1536]{1,0:T(8,128)(2,1)S(1)} collective-permute-done((bf16[128,1536]{1,0:T(8,128)(2,1)}, bf16[128,1536]{1,0:T(8,128)(2,1)S(1)}, u32[]{:S(2)}, u32[]{:S(2)}) %collective-permute-start.9) | collective-permute-done | bytes 393248 | tf_op jit(solution)/shard_map/ppermute | solution.py:108
  113.8 22.4 %collective-permute-done.10.refs_4_ = bf16[128,1536]{1,0:T(8,128)(2,1)S(1)} collective-permute-done((bf16[128,1536]{1,0:T(8,128)(2,1)}, bf16[128,1536]{1,0:T(8,128)(2,1)S(1)}, u32[]{:S(2)}, u32[]{:S(2)}) %collective-permute-start.10) | collective-permute-done | bytes 393248 | tf_op jit(solution)/shard_map/ppermute | solution.py:108
  139.1 10.8 %all-gather.5.cloned.1.call-done = bf16[16,1,128,2048]{3,2,1,0:T(8,128)(2,1)} async-done(((bf16[2,1,128,2048]{3,2,1,0:T(8,128)(2,1)}), bf16[16,1,128,2048]{3,2,1,0:T(8,128)(2,1)}) %all-gather.5.cloned.1.call-update) | async-done | bytes 8388624 | tf_op jit(solution)/shard_map/all_gather | solution.py:606
  164.3 13.1 %norm_rows.1 = (bf16[2048,2048]{1,0:T(8,128)(2,1)}, bf16[2048,2048]{1,0:T(8,128)(2,1)}) custom-call(f32[1,2048]{1,0:T(1,128)} %get-tuple-element.266.refs_0_, f32[1,2048]{1,0:T(1,128)} %get-tuple-element.265.refs_1_, bf16[2048,2048]{1,0:T(8,128)(2,1)} %bitcast.253), custom_call_target="tpu_custom_call" | custom-call | flops 83886080 | bytes 25182208 | tf_op jit(solution)/shard_map/norm_rows/pallas_call | solution.py:59
  202.4 8.0 %collective-permute-done.19.refs_3_ = bf16[4,128,768]{2,1,0:T(8,128)(2,1)S(1)} collective-permute-done((bf16[4,128,768]{2,1,0:T(8,128)(2,1)}, bf16[4,128,768]{2,1,0:T(8,128)(2,1)S(1)}, u32[]{:S(2)}, u32[]{:S(2)}) %collective-permute-start.19) | collective-permute-done | bytes 786464 | tf_op jit(solution)/shard_map/ppermute | solution.py:42
  211.3 13.5 %collective-permute-done.17.refs_1_ = bf16[2,128,1536]{2,1,0:T(8,128)(2,1)} collective-permute-done((bf16[2,128,1536]{2,1,0:T(8,128)(2,1)}, bf16[2,128,1536]{2,1,0:T(8,128)(2,1)}, u32[]{:S(2)}, u32[]{:S(2)}) %collective-permute-start.17) | collective-permute-done | bytes 786464 | tf_op jit(solution)/shard_map/ppermute | solution.py:42
  236.4 19.0 %gate_up.1 = (bf16[2048,768]{1,0:T(8,128)(2,1)}, f32[2048,768]{1,0:T(8,128)}, f32[2048,768]{1,0:T(8,128)}) custom-call(bf16[2048,2048]{1,0:T(8,128)(2,1)} %get-tuple-element.35.refs_6_.refs_0_.refs_1_, bf16[2048,1536]{1,0:T(8,128)(2,1)} %bitcast.259), custom_call_target="tpu_custom_call" | custom-call | flops 12884901888 | bytes 30408704 | tf_op jit(solution)/shard_map/gate_up/pallas_call | solution.py:59
  258.0 11.3 %times.2.refs_2_ = f32[2048,768]{1,0:T(8,128)} custom-call(bf16[2048,2048]{1,0:T(8,128)(2,1)} %get-tuple-element.35.refs_6_.refs_0_.refs_1_, bf16[2048,1024]{1,0:T(8,128)(2,1)} %bitcast.34.refs_1_.refs_2_, bf16[2048,768]{1,0:T(8,128)(2,1)} %get-tuple-element.36.refs_2_.refs_0_.refs_1_, bf16[2,128,768]{2,1,0:T(8,128)(2,1)} %copy-done.80, ...), custom_call_target="tpu_custom_call" | custom-call | flops 6442450944 | bytes 18874368 | tf_op jit(solution)/shard_map/times/pallas_call | solution.py:59
  269.3 10.9 %weight_term.3.refs_2_ = bf16[2048,768]{1,0:T(8,128)(2,1)} custom-call(bf16[2048,768]{1,0:T(8,128)(2,1)} %get-tuple-element.36.refs_2_.refs_0_.refs_1_, bf16[2048,2048]{1,0:T(8,128)(2,1)} %bitcast.255, f32[2048,768]{1,0:T(8,128)} %times.2.refs_2_), custom_call_target="tpu_custom_call" | custom-call | flops 6442450944 | bytes 14680064 | tf_op jit(solution)/shard_map/weight_term/pallas_call | solution.py:59
  280.2 12.7 %reduce-scatter.4.cloned.1.call-start = ((), (), s32[]{:S(2)}) async-start(), calls=%async_computation.3 | async-start | bytes 9437184 | tf_op jit(solution)/shard_map/reduce_scatter | solution.py:645
  308.3 28.0 %attention_both_ways.1 = (bf16[4,2,2,128,256]{4,3,2,1,0:T(8,128)(2,1)S(1)}, bf16[4,2,2,128,768]{4,3,2,1,0:T(8,128)(2,1)S(1)}, f32[8,768]{1,0:T(8,128)S(1)}) custom-call(f32[256,256]{1,0:T(8,128)S(1)} %fusion.31.mask_ref, f32[256,256]{1,0:T(8,128)S(1)} %copy.88.cos_ref, f32[256,256]{1,0:T(8,128)S(1)} %copy.89.left_ref, f32[256,256]{1,0:T(8,128)S(1)} %copy.90.right_ref, ...), custom_call_target="tpu_custom_call" | custom-call | flops 7516192768 | bytes 15728640 | tf_op jit(solution)/shard_map/attention_both_ways/pallas_call | solution.py:276
  338.9 13.4 %product_sum.3.refs_4_ = bf16[2048,2048]{1,0:T(8,128)(2,1)} custom-call(bf16[2048,256]{1,0:T(8,128)(2,1)} %bitcast.244, bf16[2048,768]{1,0:T(8,128)(2,1)} %get-tuple-element.36.refs_2_.refs_0_.refs_1_, bf16[2048,1024]{1,0:T(8,128)(2,1)} %bitcast.34.refs_1_.refs_2_, bf16[2048,768]{1,0:T(8,128)(2,1)} %bitcast.270), custom_call_target="tpu_custom_call" | custom-call | flops 8589934592 | bytes 19922944 | tf_op jit(solution)/shard_map/product_sum/pallas_call | solution.py:59
  352.4 14.5 %weight_term.4.refs_4_ = bf16[2048,1024]{1,0:T(8,128)(2,1)} custom-call(bf16[2048,768]{1,0:T(8,128)(2,1)} %bitcast.241, bf16[2048,2048]{1,0:T(8,128)(2,1)} %get-tuple-element.35.refs_6_.refs_0_.refs_1_, bf16[2048,256]{1,0:T(8,128)(2,1)} %bitcast.245, bf16[2048,2048]{1,0:T(8,128)(2,1)} %bitcast.257, bf16[2048,2048]{1,0:T(8,128)(2,1)} %product_sum.3.refs_4_), custom_call_target="tpu_custom_call" | custom-call | flops 8589934592 | bytes 25165824 | tf_op jit(solution)/shard_map/weight_term/pallas_call | solution.py:59
  372.5 14.4 %gate_up_back.1.refs_0_.refs_1_ = bf16[2048,1536]{1,0:T(8,128)(2,1)} custom-call(bf16[2048,2048]{1,0:T(8,128)(2,1)} %bitcast.258, bf16[2048,768]{1,0:T(8,128)(2,1)} %bitcast.271, f32[2048,768]{1,0:T(8,128)} %get-tuple-element.39.refs_2_, f32[2048,768]{1,0:T(8,128)} %get-tuple-element.40.refs_3_, bf16[2048,1024]{1,0:T(8,128)(2,1)} %weight_term.4.refs_4_), custom_call_target="tpu_custom_call" | custom-call | flops 6442450944 | bytes 30408704 | tf_op jit(solution)/shard_map/gate_up_back/pallas_call | solution.py:59
  392.8 18.5 %weight_term.5.refs_5_ = bf16[2048,1536]{1,0:T(8,128)(2,1)} custom-call(bf16[2048,1536]{1,0:T(8,128)(2,1)} %gate_up_back.1.refs_0_.refs_1_, bf16[2048,2048]{1,0:T(8,128)(2,1)} %get-tuple-element.35.refs_6_.refs_0_.refs_1_, bf16[2,128,1024]{2,1,0:T(8,128)(2,1)} %copy-done.24, bf16[2,128,1024]{2,1,0:T(8,128)(2,1)} %copy-done.25), custom_call_target="tpu_custom_call" | custom-call | flops 12884901888 | bytes 20971520 | tf_op jit(solution)/shard_map/weight_term/pallas_call | solution.py:59
  418.6 13.4 %collective-permute-done.33.refs_10_.refs_2_ = bf16[2,128,1536]{2,1,0:T(8,128)(2,1)S(1)} collective-permute-done((bf16[2,128,1536]{2,1,0:T(8,128)(2,1)}, bf16[2,128,1536]{2,1,0:T(8,128)(2,1)S(1)}, u32[]{:S(2)}, u32[]{:S(2)}) %collective-permute-start.33) | collective-permute-done | bytes 786464 | tf_op jit(solution)/shard_map/ppermute | solution.py:42
  440.1 19.2 %product_sum.4 = (bf16[2048,2048]{1,0:T(8,128)(2,1)}, f32[16,2048]{1,0:T(8,128)}) custom-call(bf16[2048,768]{1,0:T(8,128)(2,1)} %bitcast.242, bf16[2048,1536]{1,0:T(8,128)(2,1)} %gate_up_back.1.refs_0_.refs_1_, bf16[2048,1024]{1,0:T(8,128)(2,1)} %bitcast.34.refs_1_.refs_2_, bf16[2048,1536]{1,0:T(8,128)(2,1)} %bitcast.260, ...), custom_call_target="tpu_custom_call" | custom-call | flops 9663676416 | bytes 36831232 | tf_op jit(solution)/shard_map/product_sum/pallas_call | solution.py:59
  485.2 18.8 %product_sum.5 = (bf16[2048,2048]{1,0:T(8,128)(2,1)}, f32[16,2048]{1,0:T(8,128)}) custom-call(bf16[2048,768]{1,0:T(8,128)(2,1)} %bitcast.243, bf16[2048,1536]{1,0:T(8,128)(2,1)} %gate_up_back.1.refs_0_.refs_1_, bf16[2048,1024]{1,0:T(8,128)(2,1)} %bitcast.34.refs_1_.refs_2_, bf16[2048,1536]{1,0:T(8,128)(2,1)} %bitcast.261, ...), custom_call_target="tpu_custom_call", output_to_operand_aliasing={{0}: (5, {})} | custom-call | flops 9663676416 | bytes 45219840 | tf_op jit(solution)/shard_map/product_sum/pallas_call | solution.py:59
  514.4 9.8 %collective-permute-start.39 = (bf16[128,1536]{1,0:T(8,128)(2,1)}, bf16[128,1536]{1,0:T(8,128)(2,1)}, u32[]{:S(2)}, u32[]{:S(2)}) collective-permute-start(bf16[128,1536]{1,0:T(8,128)(2,1)} %after.66), channel_id=1, source_target_pairs={{0,8},{8,0},{16,24},{24,16},{1,9},{9,1},{17,25},{25,17},{2,10},{10... | collective-permute-start | bytes 1179656 | tf_op jit(solution)/shard_map/ppermute | solution.py:108
  531.0 14.3 %collective-permute-done.39 = bf16[128,1536]{1,0:T(8,128)(2,1)} collective-permute-done((bf16[128,1536]{1,0:T(8,128)(2,1)}, bf16[128,1536]{1,0:T(8,128)(2,1)}, u32[]{:S(2)}, u32[]{:S(2)}) %collective-permute-start.39) | collective-permute-done | bytes 393248 | tf_op jit(solution)/shard_map/ppermute | solution.py:108
  550.8 14.5 %collective-permute-done.41 = bf16[128,1536]{1,0:T(8,128)(2,1)S(1)} collective-permute-done((bf16[128,1536]{1,0:T(8,128)(2,1)}, bf16[128,1536]{1,0:T(8,128)(2,1)S(1)}, u32[]{:S(2)}, u32[]{:S(2)}) %collective-permute-start.41) | collective-permute-done | bytes 393248 | tf_op jit(solution)/shard_map/ppermute | solution.py:108
  (470 shorter events, 254.8 us)
Async XLA Ops:
  7.2 142.7 %all-gather.5.cloned.1.call-start = ((), (), s32[]{:S(2)}) async-start(), calls=%async_computation.6 | async-start | bytes 9437184 | tf_op jit(solution)/shard_map/all_gather | solution.py:606
  8.0 261.3 %all-gather.7.cloned.1.call-start = ((), (), s32[]{:S(2)}) async-start(), calls=%async_computation.7 | async-start | bytes 9437184 | tf_op jit(solution)/shard_map/all_gather | solution.py:607
  8.7 450.6 %reduce-scatter.6.cloned.1.call-start = ((), (), s32[]{:S(2)}) async-start(), calls=%async_computation.4 | async-start | bytes 3932160 | tf_op jit(solution)/shard_map/reduce_scatter | solution.py:647
  33.5 35.5 %collective-permute-start.5 = (bf16[128,1024]{1,0:T(8,128)(2,1)}, bf16[128,1024]{1,0:T(8,128)(2,1)S(1)}, u32[]{:S(2)}, u32[]{:S(2)}) collective-permute-start(bf16[128,1024]{1,0:T(8,128)(2,1)} %after.36), channel_id=1, source_target_pairs={{0,16},{8,24},{16,0},{24,8},{1,17},{9,25},{17,1},{25,9},{2,18},{10... | collective-permute-start | bytes 786440 | tf_op jit(solution)/shard_map/ppermute | solution.py:108
  36.6 32.9 %collective-permute-start.6 = (bf16[128,1024]{1,0:T(8,128)(2,1)}, bf16[128,1024]{1,0:T(8,128)(2,1)S(1)}, u32[]{:S(2)}, u32[]{:S(2)}) collective-permute-start(bf16[128,1024]{1,0:T(8,128)(2,1)} %after.37), channel_id=1, source_target_pairs={{0,24},{8,16},{16,8},{24,0},{1,25},{9,17},{17,9},{25,1},{2,26},{10... | collective-permute-start | bytes 786440 | tf_op jit(solution)/shard_map/ppermute | solution.py:108
  70.5 43.4 %collective-permute-start.9 = (bf16[128,1536]{1,0:T(8,128)(2,1)}, bf16[128,1536]{1,0:T(8,128)(2,1)S(1)}, u32[]{:S(2)}, u32[]{:S(2)}) collective-permute-start(bf16[128,1536]{1,0:T(8,128)(2,1)} %after.39), channel_id=1, source_target_pairs={{0,8},{8,0},{16,24},{24,16},{1,9},{9,1},{17,25},{25,17},{2,10},{10... | collective-permute-start | bytes 1179656 | tf_op jit(solution)/shard_map/ppermute | solution.py:108
  89.5 46.8 %collective-permute-start.10 = (bf16[128,1536]{1,0:T(8,128)(2,1)}, bf16[128,1536]{1,0:T(8,128)(2,1)S(1)}, u32[]{:S(2)}, u32[]{:S(2)}) collective-permute-start(bf16[128,1536]{1,0:T(8,128)(2,1)} %after.40), channel_id=1, source_target_pairs={{0,16},{8,24},{16,0},{24,8},{1,17},{9,25},{17,1},{25,9},{2,18},{10... | collective-permute-start | bytes 1179656 | tf_op jit(solution)/shard_map/ppermute | solution.py:108
  91.1 45.1 %collective-permute-start.11 = (bf16[128,1536]{1,0:T(8,128)(2,1)}, bf16[128,1536]{1,0:T(8,128)(2,1)S(1)}, u32[]{:S(2)}, u32[]{:S(2)}) collective-permute-start(bf16[128,1536]{1,0:T(8,128)(2,1)} %after.41), channel_id=1, source_target_pairs={{0,24},{8,16},{16,8},{24,0},{1,25},{9,17},{17,9},{25,1},{2,26},{10... | collective-permute-start | bytes 1179656 | tf_op jit(solution)/shard_map/ppermute | solution.py:108
  94.4 44.6 %collective-permute-start.8 = (bf16[4,128,1024]{2,1,0:T(8,128)(2,1)}, bf16[4,128,1024]{2,1,0:T(8,128)(2,1)S(1)}, u32[]{:S(2)}, u32[]{:S(2)}) collective-permute-start(bf16[4,128,1024]{2,1,0:T(8,128)(2,1)} %after.38), channel_id=1, source_target_pairs={{0,4},{4,0},{1,5},{5,1},{2,6},{6,2},{3,7},{7,3},{8,12},{12,8},{9,1... | collective-permute-start | bytes 3145736 | tf_op jit(solution)/shard_map/ppermute | solution.py:42
  96.4 42.7 %collective-permute-start.7 = (bf16[4,128,1024]{2,1,0:T(8,128)(2,1)}, bf16[4,128,1024]{2,1,0:T(8,128)(2,1)S(1)}, u32[]{:S(2)}, u32[]{:S(2)}) collective-permute-start(bf16[4,128,1024]{2,1,0:T(8,128)(2,1)} %after.38), channel_id=1, source_target_pairs={{0,2},{2,0},{1,3},{3,1},{4,6},{6,4},{5,7},{7,5},{8,10},{10,8},{9,1... | collective-permute-start | bytes 3145736 | tf_op jit(solution)/shard_map/ppermute | solution.py:42
  149.9 36.8 %collective-permute-start.13 = (bf16[4,128,1536]{2,1,0:T(8,128)(2,1)}, bf16[4,128,1536]{2,1,0:T(8,128)(2,1)S(1)}, u32[]{:S(2)}, u32[]{:S(2)}) collective-permute-start(bf16[4,128,1536]{2,1,0:T(8,128)(2,1)} %after.42), channel_id=1, source_target_pairs={{0,4},{4,0},{1,5},{5,1},{2,6},{6,2},{3,7},{7,3},{8,12},{12,8},{9,1... | collective-permute-start | bytes 4718600 | tf_op jit(solution)/shard_map/ppermute | solution.py:42
  151.3 36.5 %collective-permute-start.12 = (bf16[4,128,1536]{2,1,0:T(8,128)(2,1)}, bf16[4,128,1536]{2,1,0:T(8,128)(2,1)S(1)}, u32[]{:S(2)}, u32[]{:S(2)}) collective-permute-start(bf16[4,128,1536]{2,1,0:T(8,128)(2,1)} %after.42), channel_id=1, source_target_pairs={{0,2},{2,0},{1,3},{3,1},{4,6},{6,4},{5,7},{7,5},{8,10},{10,8},{9,1... | collective-permute-start | bytes 4718600 | tf_op jit(solution)/shard_map/ppermute | solution.py:42
  156.7 26.8 %collective-permute-start.16 = (bf16[128,768]{1,0:T(8,128)(2,1)}, bf16[128,768]{1,0:T(8,128)(2,1)S(1)}, u32[]{:S(2)}, u32[]{:S(2)}) collective-permute-start(bf16[128,768]{1,0:T(8,128)(2,1)} %after.45), channel_id=1, source_target_pairs={{0,24},{8,16},{16,8},{24,0},{1,25},{9,17},{17,9},{25,1},{2,26},{10... | collective-permute-start | bytes 589832 | tf_op jit(solution)/shard_map/ppermute | solution.py:108
  189.0 36.7 %collective-permute-start.20 = (bf16[4,128,768]{2,1,0:T(8,128)(2,1)}, bf16[4,128,768]{2,1,0:T(8,128)(2,1)S(1)}, u32[]{:S(2)}, u32[]{:S(2)}) collective-permute-start(bf16[4,128,768]{2,1,0:T(8,128)(2,1)} %after.48), channel_id=1, source_target_pairs={{0,4},{4,0},{1,5},{5,1},{2,6},{6,2},{3,7},{7,3},{8,12},{12,8},{9,1... | collective-permute-start | bytes 2359304 | tf_op jit(solution)/shard_map/ppermute | solution.py:42
  193.5 31.3 %collective-permute-start.17 = (bf16[2,128,1536]{2,1,0:T(8,128)(2,1)}, bf16[2,128,1536]{2,1,0:T(8,128)(2,1)}, u32[]{:S(2)}, u32[]{:S(2)}) collective-permute-start(bf16[2,128,1536]{2,1,0:T(8,128)(2,1)} %after.46), channel_id=1, source_target_pairs={{0,4},{4,0},{1,5},{5,1},{2,6},{6,2},{3,7},{7,3},{8,12},{12,8},{9,1... | collective-permute-start | bytes 2359304 | tf_op jit(solution)/shard_map/ppermute | solution.py:42
  195.8 29.8 %collective-permute-start.18 = (bf16[2,128,1536]{2,1,0:T(8,128)(2,1)}, bf16[2,128,1536]{2,1,0:T(8,128)(2,1)}, u32[]{:S(2)}, u32[]{:S(2)}) collective-permute-start(bf16[2,128,1536]{2,1,0:T(8,128)(2,1)} %after.47), channel_id=1, source_target_pairs={{0,2},{2,0},{1,3},{3,1},{4,6},{6,4},{5,7},{7,5},{8,10},{10,8},{9,1... | collective-permute-start | bytes 2359304 | tf_op jit(solution)/shard_map/ppermute | solution.py:42
  226.5 30.6 %collective-permute-start.23 = (bf16[2,128,768]{2,1,0:T(8,128)(2,1)}, bf16[2,128,768]{2,1,0:T(8,128)(2,1)S(1)}, u32[]{:S(2)}, u32[]{:S(2)}) collective-permute-start(bf16[2,128,768]{2,1,0:T(8,128)(2,1)} %after.51), channel_id=1, source_target_pairs={{0,4},{4,0},{1,5},{5,1},{2,6},{6,2},{3,7},{7,3},{8,12},{12,8},{9,1... | collective-permute-start | bytes 1179656 | tf_op jit(solution)/shard_map/ppermute | solution.py:42
  229.2 27.9 %collective-permute-start.24 = (bf16[2,128,768]{2,1,0:T(8,128)(2,1)}, bf16[2,128,768]{2,1,0:T(8,128)(2,1)S(1)}, u32[]{:S(2)}, u32[]{:S(2)}) collective-permute-start(bf16[2,128,768]{2,1,0:T(8,128)(2,1)} %after.52), channel_id=1, source_target_pairs={{0,2},{2,0},{1,3},{3,1},{4,6},{6,4},{5,7},{7,5},{8,10},{10,8},{9,1... | collective-permute-start | bytes 1179656 | tf_op jit(solution)/shard_map/ppermute | solution.py:42
  280.2 224.7 %reduce-scatter.4.cloned.1.call-start = ((), (), s32[]{:S(2)}) async-start(), calls=%async_computation.3 | async-start | bytes 9437184 | tf_op jit(solution)/shard_map/reduce_scatter | solution.py:645
  352.3 280.6 %reduce-scatter.8.cloned.1.call-start = ((), (), s32[]{:S(2)}) async-start(), calls=%async_computation.5 | async-start | bytes 9437184 | tf_op jit(solution)/shard_map/reduce_scatter | solution.py:645
  436.7 67.4 %collective-permute-start.37 = (bf16[4,128,1536]{2,1,0:T(8,128)(2,1)}, bf16[4,128,1536]{2,1,0:T(8,128)(2,1)S(1)}, u32[]{:S(2)}, u32[]{:S(2)}) collective-permute-start(bf16[4,128,1536]{2,1,0:T(8,128)(2,1)} %after.63), channel_id=1, source_target_pairs={{0,2},{2,0},{1,3},{3,1},{4,6},{6,4},{5,7},{7,5},{8,10},{10,8},{9,1... | collective-permute-start | bytes 4718600 | tf_op jit(solution)/shard_map/ppermute | solution.py:42
  439.3 65.5 %collective-permute-start.38 = (bf16[4,128,1536]{2,1,0:T(8,128)(2,1)}, bf16[4,128,1536]{2,1,0:T(8,128)(2,1)S(1)}, u32[]{:S(2)}, u32[]{:S(2)}) collective-permute-start(bf16[4,128,1536]{2,1,0:T(8,128)(2,1)} %after.64), channel_id=1, source_target_pairs={{0,4},{4,0},{1,5},{5,1},{2,6},{6,2},{3,7},{7,3},{8,12},{12,8},{9,1... | collective-permute-start | bytes 4718600 | tf_op jit(solution)/shard_map/ppermute | solution.py:42
  514.4 30.9 %collective-permute-start.39 = (bf16[128,1536]{1,0:T(8,128)(2,1)}, bf16[128,1536]{1,0:T(8,128)(2,1)}, u32[]{:S(2)}, u32[]{:S(2)}) collective-permute-start(bf16[128,1536]{1,0:T(8,128)(2,1)} %after.66), channel_id=1, source_target_pairs={{0,8},{8,0},{16,24},{24,16},{1,9},{9,1},{17,25},{25,17},{2,10},{10... | collective-permute-start | bytes 1179656 | tf_op jit(solution)/shard_map/ppermute | solution.py:108
  524.2 41.1 %collective-permute-start.41 = (bf16[128,1536]{1,0:T(8,128)(2,1)}, bf16[128,1536]{1,0:T(8,128)(2,1)S(1)}, u32[]{:S(2)}, u32[]{:S(2)}) collective-permute-start(bf16[128,1536]{1,0:T(8,128)(2,1)} %after.68), channel_id=1, source_target_pairs={{0,24},{8,16},{16,8},{24,0},{1,25},{9,17},{17,9},{25,1},{2,26},{10... | collective-permute-start | bytes 1179656 | tf_op jit(solution)/shard_map/ppermute | solution.py:108
  (128 other events, 1148.9 us)
Sparse Core Ops, SparseCore 0:
  9.6 140.1 all-gather.4
  151.5 91.3 all-gather.6
  280.3 46.9 reduce-scatter.5
  352.4 92.3 reduce-scatter.3
  506.7 112.5 reduce-scatter.7

commit v3 on v2

--- a/solution.py
+++ b/solution.py
@@ -222,10 +222,11 @@
     for head in range(heads):
         cut = slice(head * HD, (head + 1) * HD)
         q, k, v, g = query[:, cut], keys[:, cut], values[:, cut], back[:, cut]
-        scores = nt(q, k) * scale + mask
+        q = q * jnp.asarray(scale, LOW)
+        scores = nt(q, k) + mask
         peak = jnp.max(scores, axis=-1, keepdims=True)
         raised = jnp.exp(scores - peak)
-        full = raised / jnp.sum(raised, axis=-1, keepdims=True)
+        full = raised * (1.0 / jnp.sum(raised, axis=-1, keepdims=True))
         probs = full.astype(LOW)
         mixed.append(nn(probs, v))
         prob_grad = nt(g, v)
@@ -233,7 +234,7 @@
         inner = jnp.sum(weighted, axis=-1, keepdims=True)
         score_grad = (weighted - full * inner).astype(LOW)
         d_query.append(nn(score_grad, k) * scale)
-        d_keys.append(tn(score_grad, q) * scale)
+        d_keys.append(tn(score_grad, q))
         d_values.append(tn(probs, g))
     mixed_ref[...] = jnp.concatenate(mixed, axis=-1).astype(LOW).reshape(mixed_ref.shape)
     out = jnp.concatenate(
@@ -254,7 +255,7 @@
     bias_grad_ref[...] += sums
 
 
-def attention(joined, back, bias):
+def attention(joined, back, bias, deps=()):
     tokens, width = back.shape
     half = 128
     seqs = tokens // (2 * half)
@@ -270,13 +271,14 @@
     cos = jnp.tile(jnp.concatenate([cosine, cosine, rest], 1), (1, heads))
     left = jnp.tile(jnp.concatenate([-sine, nothing, 0.0 * rest], 1), (1, heads))
     right = jnp.tile(jnp.concatenate([nothing, sine, 0.0 * rest], 1), (1, heads))
-    fixed = lambda i: (0, 0)
     rows = lambda i: (i // MICRO, 0, i % MICRO, 0, 0)
     shape = lambda w: (seqs // MICRO, 2, MICRO, half, w)
-    mixed, grad, bias_grad = pl.pallas_call(
+    mixed, grad, bias_grad = launch(
         attention_kernel,
-        grid=(seqs,),
-        in_specs=[
+        "attention_both_ways",
+        (seqs,),
+        [mask, cos, left, right, bias, joined.reshape(shape(3 * width)), back.reshape(shape(width))],
+        [
             pl.BlockSpec((length, length), fixed),
             pl.BlockSpec((length, width), fixed),
             pl.BlockSpec((length, width), fixed),
@@ -285,24 +287,19 @@
             pl.BlockSpec((1, 2, 1, half, 3 * width), rows),
             pl.BlockSpec((1, 2, 1, half, width), rows),
         ],
-        out_specs=[
+        [
             pl.BlockSpec((1, 2, 1, half, width), rows),
             pl.BlockSpec((1, 2, 1, half, 3 * width), rows),
             pl.BlockSpec((8, 3 * width), fixed),
         ],
-        out_shape=[
+        [
             jax.ShapeDtypeStruct(shape(width), LOW),
             jax.ShapeDtypeStruct(shape(3 * width), LOW),
             jax.ShapeDtypeStruct((8, 3 * width), F32),
         ],
-        cost_estimate=pl.CostEstimate(
-            flops=seqs * heads * 7 * 2 * length * length * HD * 4,
-            bytes_accessed=tokens * width * 30,
-            transcendentals=seqs * heads * length * length,
-        ),
-        compiler_params=pltpu.CompilerParams(vmem_limit_bytes=32 * 1024 * 1024),
-        name="attention_both_ways",
-    )(mask, cos, left, right, bias, joined.reshape(shape(3 * width)), back.reshape(shape(width)))
+        seqs * heads * 7 * 2 * length * length * HD * 4,
+        deps,
+    )
     return (
         mixed.reshape(tokens, width),
         grad.reshape(tokens, 3 * width),
@@ -614,22 +611,22 @@
     gated = exchange(pieces(gated_piece), joined[1:])
     stage = [*joined_near[1:], *gated[1:], rows_all]
     gated_near = plane.gather_first(ordered(gated), stage)
-    downward = exchange(pieces(downward_piece), stage)
     normed, xhat_all = norm_rows(rows_all, row_gain, row_shift)
-    stage = [*gated_near[1:], *downward[1:], normed]
+    stage = [*gated_near[1:], normed]
     gated_weight, last = plane.gather_second(gated_near, stage)
     gated_weight = flat(gated_weight)
-    downward_near = plane.gather_first(ordered(downward), stage)
-    stage = [*last, *downward_near[1:]]
-    attention_weight, joined_last = plane.gather_second(joined_near, stage)
+    downward = exchange(pieces(downward_piece), last)
+    attention_weight, joined_last = plane.gather_second(joined_near, last)
     attention_weight = flat(attention_weight)
-    downward_weight, last = plane.gather_second(downward_near, stage)
+    downward_near = plane.gather_first(ordered(downward), [*downward[1:], *joined_last])
+    downward_weight, last = plane.gather_second(downward_near, downward_near[1:])
     downward_weight = flat(downward_weight)
     activated, silu, slope = gate_up(normed, gated_weight)
-    joined_out = times(normed, attention_weight, 0, 3 * att_width, F32, (activated, *last))
-    downward_term = weight_term([(activated, back_all)], (joined_out,))
-    mixed_grad = times(back_all, attention_weight, 3, att_width, LOW, (downward_term,))
-    mixed, joined_grad, bias_grad = attention(joined_out, mixed_grad, bias_here)
+    joined_out = times(
+        normed, attention_weight, 0, 3 * att_width, F32, (activated, *downward[1:])
+    )
+    mixed_grad = times(back_all, attention_weight, 3, att_width, LOW, (joined_out,))
+    mixed, joined_grad, bias_grad = attention(joined_out, mixed_grad, bias_here, downward_near[1:])
 
     def fold(term):
         return term.reshape(QUAD, depth // QUAD, term.shape[1])
@@ -644,9 +641,6 @@
         folded = part.reshape(2 * QUAD, MICRO, 128, depth)
         return lax.psum_scatter(folded, line, scatter_dimension=0)
 
-    downward_total = lax.psum_scatter(
-        fold(downward_term), ("y", "x"), scatter_dimension=1, tiled=True
-    )
     out_part, _ = product_sum([(mixed, attention_weight, 3), (activated, downward_weight, 0)], depth)
     branch = scatter_rows(out_part)
     attention_term = weight_term([(joined_grad, normed), (mixed, back_all)], (out_part,))
@@ -654,17 +648,24 @@
     gated_grad = gate_up_back(back_all, downward_weight, silu, slope, (attention_term,))
     gated_term = weight_term([(gated_grad, normed)], joined_known[1:])
     joined_total, last = plane.sum_second(joined_known, joined_known[1:])
-    downward_home = homeward(downward_total, joined_known[1:])
+    downward_term = weight_term([(activated, back_all)], (gated_term, *last))
+    gated_known = plane.sum_first(fold(gated_term), last)
+    joined_home = homeward(joined_total, last)
     grad_pairs = [(joined_grad, attention_weight, 0), (gated_grad, gated_weight, 0)]
-    half_done, sums_low = product_sum(grad_pairs, depth, xhat_all, (gated_term, *last), 0)
-    joined_home = homeward(joined_total, last)
-    gated_known = plane.sum_first(fold(gated_term), last)
+    half_done, sums_low = product_sum(
+        grad_pairs, depth, xhat_all, (downward_term, *gated_known[1:]), 0
+    )
+    gated_total, last = plane.sum_second(gated_known, gated_known[1:])
+    downward_known = plane.sum_first(fold(downward_term), gated_known[1:])
     normed_grad_part, sums_high = product_sum(
-        grad_pairs, depth, xhat_all, (*downward_home[1:], *gated_known[1:]), 1, half_done
-    )
-    gated_total, last = plane.sum_second(gated_known, gated_known[1:])
-    own_grad = scatter_rows(after(normed_grad_part, branch, *joined_home[1:], *last)).astype(F32)
-    gated_home = homeward(gated_total, [*last, *joined_home[1:]])
+        grad_pairs, depth, xhat_all, joined_home[1:], 1, half_done
+    )
+    stage = [*last, *downward_known[1:], *joined_home[1:], normed_grad_part]
+    gated_home = homeward(gated_total, stage)
+    downward_total, last = plane.sum_second(downward_known, stage)
+    stage = [*gated_home[1:], *last]
+    own_grad = scatter_rows(after(normed_grad_part, branch, *stage)).astype(F32)
+    downward_home = homeward(downward_total, stage)
     sums = sums_low + sums_high
     branch = branch.astype(F32)
 
@@ -691,8 +692,14 @@
         jnp.zeros((3, depth), F32), bias_grad.reshape(3, att_width), (0, bias_at)
     )
     sums = jnp.sum(sums.reshape(2, 8, depth), axis=1)
-    vectors_term = after(jnp.concatenate([sums, bias_wide], axis=0), *last)
-    vectors_sum = sum_small(vectors_term)
+    squares = jnp.concatenate(
+        [sum(jnp.sum(block * block, axis=0) for block in own) for own in (downward_own, attention_own, gated_own)]
+    )
+    rest = 3 * depth - squares.shape[0]
+    everywhere = sum_small(
+        jnp.concatenate([sums, bias_wide, jnp.pad(squares, (0, rest)).reshape(3, depth)], axis=0)
+    )
+    vectors_sum = everywhere[:5]
     vectors_grad = lax.dynamic_slice_in_dim(
         vectors_sum, (place * plane.count + plane.at) * rows_here, rows_here, 1
     )
@@ -716,9 +723,7 @@
     gated_grads = jnp.stack([hidden_columns(gated_own, c) for c in range(2)])
     downward_grads = hidden_columns(downward_own, 0)
 
-    square = sum(jnp.sum(own * own) for own in downward_own + attention_own + gated_own)
-    square = sum_small(jnp.full((8, 128), square))[0, 0] + jnp.sum(vectors_sum * vectors_sum)
-    grad_norm = jnp.sqrt(square)
+    grad_norm = jnp.sqrt(jnp.sum(everywhere[5:]) + jnp.sum(vectors_sum * vectors_sum))
     factor = jnp.minimum(1.0, CLIP / (grad_norm + 1e-06))
     ff_total = ff_here * tp_count
     return (

time: 651 us -> 626 us (0.962)
  starting transfers between devices: 120 us -> 99.9 us
  between operations: 25.2 us -> 17.9 us
    pallas_call x11 -> x12, Pallas kernels: 160 us -> 190 us  [launch(): pl.pallas_call(run, grid_spec=pltpu.PrefetchScalarGridSpec(num_scalar_pre...]
    pallas_call x1 -> x0, Pallas kernels: 28 us -> none  [attention(): pl.pallas_call(attention_kernel, grid=(seqs,), in_specs=[pl.BlockSpec((le...]
    ppermute x20 -> x24, waiting for transfers between devices: 39.1 us -> 23 us  [swap(): return lax.ppermute(value, axis, SWAP)]
    reduce_scatter x2, starting transfers between devices: 12.8 us -> 0.08 us  [scatter_rows(): return lax.psum_scatter(folded, line, scatter_dimension=0)]
    ppermute x10 -> x5, waiting for transfers between devices: 4.82 us -> 14.9 us  [sum_small(): value = value + lax.ppermute(value, axis, pairs)]
    ppermute x10 -> x5, starting transfers between devices: 18.3 us -> 11.2 us  [sum_small(): value = value + lax.ppermute(value, axis, pairs)]
    unnamed x192 -> x198, local copies, waits for them, and re-layouts: 21.7 us -> 15.2 us
    ppermute x20 -> x24, starting transfers between devices: 22.2 us -> 26.5 us  [swap(): return lax.ppermute(value, axis, SWAP)]
  transfers between devices with their start and end apart: 57 -> 55, of which waited for: 26 -> 26; matrix products, arithmetic and copies ran while one was open for 16% -> 18% of each run, Pallas kernels for 27% -> 28%
where the time goes in v3:
time: 626 us; the launch traced here: 619 us
  Pallas kernels  190 us (30%)
  waiting for transfers between devices  177 us (28%)
  starting transfers between devices  99.9 us (16%)
  other arithmetic  70.2 us (11%)
  local copies, waits for them, and re-layouts  64.3 us (10%)
  between operations  17.9 us (3%)
    pallas_call x12, Pallas kernels, launch(): pl.pallas_call(run, grid_spec=pltpu.PrefetchScalarGridSpec(num_scalar_pre...  190 us
    ppermute x18, waiting for transfers between devices, exchange(): lax.ppermute(block, 'a', [(i, i ^ bit) for i in range(QUAD)])  120 us
    ppermute x18, starting transfers between devices, exchange(): lax.ppermute(block, 'a', [(i, i ^ bit) for i in range(QUAD)])  53.1 us
    ppermute x24, starting transfers between devices, swap(): return lax.ppermute(value, axis, SWAP)  26.5 us
    ppermute x24, waiting for transfers between devices, swap(): return lax.ppermute(value, axis, SWAP)  23 us
    convert_element_type x5, other arithmetic, adamw(): return (updated, moment, variance, updated.astype(LOW))  17.4 us
    unnamed x198, local copies, waits for them, and re-layouts  15.2 us
    ppermute x5, waiting for transfers between devices, sum_small(): value = value + lax.ppermute(value, axis, pairs)  14.9 us
  transfers between devices with their start and end apart: 55, of which 26 were waited for; matrix products, arithmetic and copies ran while one was open for 18% of the time, Pallas kernels for 28%

profile of v3, /device:TPU:0, one launch (start us, length us, event | category | flops | bytes accessed | tf_op | source)
XLA Modules:
  0.0 619.2 jit_solution(10002150969827315353)
XLA Ops:
  38.0 18.7 %collective-permute-done.4.refs_1_ = bf16[128,1024]{1,0:T(8,128)(2,1)S(1)} collective-permute-done((bf16[128,1024]{1,0:T(8,128)(2,1)}, bf16[128,1024]{1,0:T(8,128)(2,1)S(1)}, u32[]{:S(2)}, u32[]{:S(2)}) %collective-permute-start.4) | collective-permute-done | bytes 262176 | tf_op jit(solution)/shard_map/ppermute | solution.py:108
  56.7 12.2 %collective-permute-done.5.refs_2_ = bf16[128,1024]{1,0:T(8,128)(2,1)S(1)} collective-permute-done((bf16[128,1024]{1,0:T(8,128)(2,1)}, bf16[128,1024]{1,0:T(8,128)(2,1)S(1)}, u32[]{:S(2)}, u32[]{:S(2)}) %collective-permute-start.5) | collective-permute-done | bytes 262176 | tf_op jit(solution)/shard_map/ppermute | solution.py:108
  70.3 19.1 %collective-permute-start.9 = (bf16[128,1536]{1,0:T(8,128)(2,1)}, bf16[128,1536]{1,0:T(8,128)(2,1)S(1)}, u32[]{:S(2)}, u32[]{:S(2)}) collective-permute-start(bf16[128,1536]{1,0:T(8,128)(2,1)} %after.42), channel_id=1, source_target_pairs={{0,8},{8,0},{16,24},{24,16},{1,9},{9,1},{17,25},{25,17},{2,10},{10... | collective-permute-start | bytes 1179656 | tf_op jit(solution)/shard_map/ppermute | solution.py:108
  97.5 16.4 %collective-permute-done.9.refs_3_ = bf16[128,1536]{1,0:T(8,128)(2,1)S(1)} collective-permute-done((bf16[128,1536]{1,0:T(8,128)(2,1)}, bf16[128,1536]{1,0:T(8,128)(2,1)S(1)}, u32[]{:S(2)}, u32[]{:S(2)}) %collective-permute-start.9) | collective-permute-done | bytes 393248 | tf_op jit(solution)/shard_map/ppermute | solution.py:108
  113.8 22.3 %collective-permute-done.10.refs_4_ = bf16[128,1536]{1,0:T(8,128)(2,1)S(1)} collective-permute-done((bf16[128,1536]{1,0:T(8,128)(2,1)}, bf16[128,1536]{1,0:T(8,128)(2,1)S(1)}, u32[]{:S(2)}, u32[]{:S(2)}) %collective-permute-start.10) | collective-permute-done | bytes 393248 | tf_op jit(solution)/shard_map/ppermute | solution.py:108
  139.0 10.9 %all-gather.5.cloned.1.call-done = bf16[16,1,128,2048]{3,2,1,0:T(8,128)(2,1)} async-done(((bf16[2,1,128,2048]{3,2,1,0:T(8,128)(2,1)}), bf16[16,1,128,2048]{3,2,1,0:T(8,128)(2,1)}) %all-gather.5.cloned.1.call-update) | async-done | bytes 8388624 | tf_op jit(solution)/shard_map/all_gather | solution.py:603
  163.1 13.5 %norm_rows.1 = (bf16[2048,2048]{1,0:T(8,128)(2,1)}, bf16[2048,2048]{1,0:T(8,128)(2,1)}) custom-call(f32[1,2048]{1,0:T(1,128)} %get-tuple-element.272.refs_0_, f32[1,2048]{1,0:T(1,128)} %get-tuple-element.271.refs_1_, bf16[2048,2048]{1,0:T(8,128)(2,1)} %bitcast.249), custom_call_target="tpu_custom_call" | custom-call | flops 83886080 | bytes 25182208 | tf_op jit(solution)/shard_map/norm_rows/pallas_call | solution.py:59
  176.7 10.0 %collective-permute-done.12.refs_1_ = bf16[4,128,1536]{2,1,0:T(8,128)(2,1)S(1)} collective-permute-done((bf16[4,128,1536]{2,1,0:T(8,128)(2,1)}, bf16[4,128,1536]{2,1,0:T(8,128)(2,1)S(1)}, u32[]{:S(2)}, u32[]{:S(2)}) %collective-permute-start.12) | collective-permute-done | bytes 1572896 | tf_op jit(solution)/shard_map/ppermute | solution.py:42
  199.3 8.7 %collective-permute-done.14.refs_1_ = bf16[2,128,1536]{2,1,0:T(8,128)(2,1)S(1)} collective-permute-done((bf16[2,128,1536]{2,1,0:T(8,128)(2,1)}, bf16[2,128,1536]{2,1,0:T(8,128)(2,1)S(1)}, u32[]{:S(2)}, u32[]{:S(2)}) %collective-permute-start.14) | collective-permute-done | bytes 786464 | tf_op jit(solution)/shard_map/ppermute | solution.py:42
  220.5 18.9 %gate_up.1 = (bf16[2048,768]{1,0:T(8,128)(2,1)}, f32[2048,768]{1,0:T(8,128)}, f32[2048,768]{1,0:T(8,128)}) custom-call(bf16[2048,2048]{1,0:T(8,128)(2,1)} %get-tuple-element.35.refs_3_.refs_0_.refs_1_, bf16[2048,1536]{1,0:T(8,128)(2,1)} %bitcast.251), custom_call_target="tpu_custom_call" | custom-call | flops 12884901888 | bytes 30408704 | tf_op jit(solution)/shard_map/gate_up/pallas_call | solution.py:59
  249.9 11.4 %times.2.refs_2_ = f32[2048,768]{1,0:T(8,128)} custom-call(bf16[2048,2048]{1,0:T(8,128)(2,1)} %get-tuple-element.35.refs_3_.refs_0_.refs_1_, bf16[2048,1024]{1,0:T(8,128)(2,1)} %bitcast.30.refs_1_.refs_2_, bf16[2048,768]{1,0:T(8,128)(2,1)} %get-tuple-element.36.refs_2_.refs_1_.refs_0_, bf16[128,768]{1,0:T(8,128)(2,1)} %copy-done.75, ...), custom_call_target="tpu_custom_call" | custom-call | flops 6442450944 | bytes 18874368 | tf_op jit(solution)/shard_map/times/pallas_call | solution.py:59
  272.7 29.3 %attention_both_ways.1 = (bf16[4,2,2,128,256]{4,3,2,1,0:T(8,128)(2,1)}, bf16[4,2,2,128,768]{4,3,2,1,0:T(8,128)(2,1)}, f32[8,768]{1,0:T(8,128)}) custom-call(f32[256,256]{1,0:T(8,128)} %fusion.31.refs_0_, f32[256,256]{1,0:T(8,128)} %copy.91.refs_1_, f32[256,256]{1,0:T(8,128)} %copy.92.refs_2_, f32[256,256]{1,0:T(8,128)} %copy.93.refs_3_, f32[1,768]{1,0:T(1,128)} %bitcast.289, ...), custom_call_target="tpu_custom_call" | custom-call | flops 7516192768 | bytes 12610560 | tf_op jit(solution)/shard_map/attention_both_ways/pallas_call | solution.py:59
  306.1 13.6 %product_sum.3.refs_4_ = bf16[2048,2048]{1,0:T(8,128)(2,1)} custom-call(bf16[2048,256]{1,0:T(8,128)(2,1)} %bitcast.276, bf16[2048,768]{1,0:T(8,128)(2,1)} %get-tuple-element.36.refs_2_.refs_1_.refs_0_, bf16[2048,1024]{1,0:T(8,128)(2,1)} %bitcast.30.refs_1_.refs_2_, bf16[2048,768]{1,0:T(8,128)(2,1)} %bitcast.257), custom_call_target="tpu_custom_call" | custom-call | flops 8589934592 | bytes 19922944 | tf_op jit(solution)/shard_map/product_sum/pallas_call | solution.py:59
  319.8 15.0 %weight_term.3.refs_4_ = bf16[2048,1024]{1,0:T(8,128)(2,1)} custom-call(bf16[2048,768]{1,0:T(8,128)(2,1)} %bitcast.254, bf16[2048,2048]{1,0:T(8,128)(2,1)} %get-tuple-element.35.refs_3_.refs_0_.refs_1_, bf16[2048,256]{1,0:T(8,128)(2,1)} %bitcast.277, bf16[2048,2048]{1,0:T(8,128)(2,1)} %bitcast.242, bf16[2048,2048]{1,0:T(8,128)(2,1)} %product_sum.3.refs_4_), custom_call_target="tpu_custom_call" | custom-call | flops 8589934592 | bytes 25165824 | tf_op jit(solution)/shard_map/weight_term/pallas_call | solution.py:59
  339.6 14.3 %gate_up_back.1.refs_0_.refs_1_ = bf16[2048,1536]{1,0:T(8,128)(2,1)} custom-call(bf16[2048,2048]{1,0:T(8,128)(2,1)} %bitcast.243, bf16[2048,768]{1,0:T(8,128)(2,1)} %bitcast.258, f32[2048,768]{1,0:T(8,128)} %get-tuple-element.39.refs_2_, f32[2048,768]{1,0:T(8,128)} %get-tuple-element.40.refs_3_, bf16[2048,1024]{1,0:T(8,128)(2,1)} %weight_term.3.refs_4_), custom_call_target="tpu_custom_call" | custom-call | flops 6442450944 | bytes 30408704 | tf_op jit(solution)/shard_map/gate_up_back/pallas_call | solution.py:59
  360.0 18.5 %weight_term.4.refs_2_ = bf16[2048,1536]{1,0:T(8,128)(2,1)} custom-call(bf16[2048,1536]{1,0:T(8,128)(2,1)} %gate_up_back.1.refs_0_.refs_1_, bf16[2048,2048]{1,0:T(8,128)(2,1)} %get-tuple-element.35.refs_3_.refs_0_.refs_1_, bf16[2,128,1024]{2,1,0:T(8,128)(2,1)} %copy-done.41, bf16[2,128,1024]{2,1,0:T(8,128)(2,1)} %copy-done.42), custom_call_target="tpu_custom_call" | custom-call | flops 12884901888 | bytes 20971520 | tf_op jit(solution)/shard_map/weight_term/pallas_call | solution.py:59
  397.5 10.9 %weight_term.5.refs_5_ = bf16[2048,768]{1,0:T(8,128)(2,1)} custom-call(bf16[2048,768]{1,0:T(8,128)(2,1)} %get-tuple-element.36.refs_2_.refs_1_.refs_0_, bf16[2048,2048]{1,0:T(8,128)(2,1)} %bitcast.244, bf16[2048,1536]{1,0:T(8,128)(2,1)} %weight_term.4.refs_2_, bf16[4,128,1024]{2,1,0:T(8,128)(2,1)} %copy-done.4, bf16[4,128,1024]{2,1,0:T(8,128)(2,1)} %copy-done.6), custom_call_target="tpu_custom_call" | custom-call | flops 6442450944 | bytes 14680064 | tf_op jit(solution)/shard_map/weight_term/pallas_call | solution.py:59
  418.1 18.9 %product_sum.4 = (bf16[2048,2048]{1,0:T(8,128)(2,1)}, f32[16,2048]{1,0:T(8,128)}) custom-call(bf16[2048,768]{1,0:T(8,128)(2,1)} %bitcast.255, bf16[2048,1536]{1,0:T(8,128)(2,1)} %gate_up_back.1.refs_0_.refs_1_, bf16[2048,1024]{1,0:T(8,128)(2,1)} %bitcast.30.refs_1_.refs_2_, bf16[2048,1536]{1,0:T(8,128)(2,1)} %bitcast.252, ...), custom_call_target="tpu_custom_call" | custom-call | flops 9663676416 | bytes 36831232 | tf_op jit(solution)/shard_map/product_sum/pallas_call | solution.py:59
  439.0 18.9 %product_sum.5 = (bf16[2048,2048]{1,0:T(8,128)(2,1)}, f32[16,2048]{1,0:T(8,128)}) custom-call(bf16[2048,768]{1,0:T(8,128)(2,1)} %bitcast.256, bf16[2048,1536]{1,0:T(8,128)(2,1)} %gate_up_back.1.refs_0_.refs_1_, bf16[2048,1024]{1,0:T(8,128)(2,1)} %bitcast.30.refs_1_.refs_2_, bf16[2048,1536]{1,0:T(8,128)(2,1)} %bitcast.253, ...), custom_call_target="tpu_custom_call", output_to_operand_aliasing={{0}: (5, {})} | custom-call | flops 9663676416 | bytes 45219840 | tf_op jit(solution)/shard_map/product_sum/pallas_call | solution.py:59
  473.2 11.2 %collective-permute-done.38.refs_2_.refs_1_ = bf16[128,1536]{1,0:T(8,128)(2,1)S(1)} collective-permute-done((bf16[128,1536]{1,0:T(8,128)(2,1)}, bf16[128,1536]{1,0:T(8,128)(2,1)S(1)}, u32[]{:S(2)}, u32[]{:S(2)}) %collective-permute-start.38) | collective-permute-done | bytes 393248 | tf_op jit(solution)/shard_map/ppermute | solution.py:108
  484.4 13.3 %collective-permute-done.39.refs_3_.refs_2_ = bf16[128,1536]{1,0:T(8,128)(2,1)S(1)} collective-permute-done((bf16[128,1536]{1,0:T(8,128)(2,1)}, bf16[128,1536]{1,0:T(8,128)(2,1)S(1)}, u32[]{:S(2)}, u32[]{:S(2)}) %collective-permute-start.39) | collective-permute-done | bytes 393248 | tf_op jit(solution)/shard_map/ppermute | solution.py:108
  521.2 9.9 %collective-permute-done.43 = bf16[128,768]{1,0:T(8,128)(2,1)S(1)} collective-permute-done((bf16[128,768]{1,0:T(8,128)(2,1)}, bf16[128,768]{1,0:T(8,128)(2,1)S(1)}, u32[]{:S(2)}, u32[]{:S(2)}) %collective-permute-start.43) | collective-permute-done | bytes 196640 | tf_op jit(solution)/shard_map/ppermute | solution.py:108
  531.2 10.7 %collective-permute-done.44 = bf16[128,768]{1,0:T(8,128)(2,1)S(1)} collective-permute-done((bf16[128,768]{1,0:T(8,128)(2,1)}, bf16[128,768]{1,0:T(8,128)(2,1)S(1)}, u32[]{:S(2)}, u32[]{:S(2)}) %collective-permute-start.44) | collective-permute-done | bytes 196640 | tf_op jit(solution)/shard_map/ppermute | solution.py:108
  560.6 7.4 %collective-permute-start.49 = (f32[8,2048]{1,0:T(8,128)S(1)}, f32[8,2048]{1,0:T(8,128)S(1)}, u32[]{:S(2)}, u32[]{:S(2)}) collective-permute-start(f32[8,2048]{1,0:T(8,128)S(1)} %add.425), channel_id=1, source_target_pairs={{0,8},{8,0},{16,24},{24,16},{1,9},{9,1},{17,25},{25,17},{2,10},{10... | collective-permute-start | bytes 196616 | tf_op jit(solution)/shard_map/ppermute | solution.py:197
  (479 shorter events, 247.3 us)
Async XLA Ops:
  7.2 142.7 %all-gather.5.cloned.1.call-start = ((), (), s32[]{:S(2)}) async-start(), calls=%async_computation.4 | async-start | bytes 9437184 | tf_op jit(solution)/shard_map/all_gather | solution.py:603
  8.0 253.3 %all-gather.7.cloned.1.call-start = ((), (), s32[]{:S(2)}) async-start(), calls=%async_computation.5 | async-start | bytes 9437184 | tf_op jit(solution)/shard_map/all_gather | solution.py:604
  8.7 489.0 %reduce-scatter.3.cloned.1.call-start = ((), (), s32[]{:S(2)}) async-start(), calls=%async_computation.2 | async-start | bytes 9437184 | tf_op jit(solution)/shard_map/reduce_scatter | solution.py:642
  33.4 35.5 %collective-permute-start.5 = (bf16[128,1024]{1,0:T(8,128)(2,1)}, bf16[128,1024]{1,0:T(8,128)(2,1)S(1)}, u32[]{:S(2)}, u32[]{:S(2)}) collective-permute-start(bf16[128,1024]{1,0:T(8,128)(2,1)} %after.39), channel_id=1, source_target_pairs={{0,16},{8,24},{16,0},{24,8},{1,17},{9,25},{17,1},{25,9},{2,18},{10... | collective-permute-start | bytes 786440 | tf_op jit(solution)/shard_map/ppermute | solution.py:108
  36.5 33.0 %collective-permute-start.6 = (bf16[128,1024]{1,0:T(8,128)(2,1)}, bf16[128,1024]{1,0:T(8,128)(2,1)S(1)}, u32[]{:S(2)}, u32[]{:S(2)}) collective-permute-start(bf16[128,1024]{1,0:T(8,128)(2,1)} %after.40), channel_id=1, source_target_pairs={{0,24},{8,16},{16,8},{24,0},{1,25},{9,17},{17,9},{25,1},{2,26},{10... | collective-permute-start | bytes 786440 | tf_op jit(solution)/shard_map/ppermute | solution.py:108
  70.3 43.5 %collective-permute-start.9 = (bf16[128,1536]{1,0:T(8,128)(2,1)}, bf16[128,1536]{1,0:T(8,128)(2,1)S(1)}, u32[]{:S(2)}, u32[]{:S(2)}) collective-permute-start(bf16[128,1536]{1,0:T(8,128)(2,1)} %after.42), channel_id=1, source_target_pairs={{0,8},{8,0},{16,24},{24,16},{1,9},{9,1},{17,25},{25,17},{2,10},{10... | collective-permute-start | bytes 1179656 | tf_op jit(solution)/shard_map/ppermute | solution.py:108
  89.4 46.8 %collective-permute-start.10 = (bf16[128,1536]{1,0:T(8,128)(2,1)}, bf16[128,1536]{1,0:T(8,128)(2,1)S(1)}, u32[]{:S(2)}, u32[]{:S(2)}) collective-permute-start(bf16[128,1536]{1,0:T(8,128)(2,1)} %after.43), channel_id=1, source_target_pairs={{0,16},{8,24},{16,0},{24,8},{1,17},{9,25},{17,1},{25,9},{2,18},{10... | collective-permute-start | bytes 1179656 | tf_op jit(solution)/shard_map/ppermute | solution.py:108
  91.0 45.2 %collective-permute-start.11 = (bf16[128,1536]{1,0:T(8,128)(2,1)}, bf16[128,1536]{1,0:T(8,128)(2,1)S(1)}, u32[]{:S(2)}, u32[]{:S(2)}) collective-permute-start(bf16[128,1536]{1,0:T(8,128)(2,1)} %after.44), channel_id=1, source_target_pairs={{0,24},{8,16},{16,8},{24,0},{1,25},{9,17},{17,9},{25,1},{2,26},{10... | collective-permute-start | bytes 1179656 | tf_op jit(solution)/shard_map/ppermute | solution.py:108
  94.3 44.7 %collective-permute-start.8 = (bf16[4,128,1024]{2,1,0:T(8,128)(2,1)}, bf16[4,128,1024]{2,1,0:T(8,128)(2,1)S(1)}, u32[]{:S(2)}, u32[]{:S(2)}) collective-permute-start(bf16[4,128,1024]{2,1,0:T(8,128)(2,1)} %after.41), channel_id=1, source_target_pairs={{0,4},{4,0},{1,5},{5,1},{2,6},{6,2},{3,7},{7,3},{8,12},{12,8},{9,1... | collective-permute-start | bytes 3145736 | tf_op jit(solution)/shard_map/ppermute | solution.py:42
  96.3 42.7 %collective-permute-start.7 = (bf16[4,128,1024]{2,1,0:T(8,128)(2,1)}, bf16[4,128,1024]{2,1,0:T(8,128)(2,1)S(1)}, u32[]{:S(2)}, u32[]{:S(2)}) collective-permute-start(bf16[4,128,1024]{2,1,0:T(8,128)(2,1)} %after.41), channel_id=1, source_target_pairs={{0,2},{2,0},{1,3},{3,1},{4,6},{6,4},{5,7},{7,5},{8,10},{10,8},{9,1... | collective-permute-start | bytes 3145736 | tf_op jit(solution)/shard_map/ppermute | solution.py:42
  149.9 36.8 %collective-permute-start.12 = (bf16[4,128,1536]{2,1,0:T(8,128)(2,1)}, bf16[4,128,1536]{2,1,0:T(8,128)(2,1)S(1)}, u32[]{:S(2)}, u32[]{:S(2)}) collective-permute-start(bf16[4,128,1536]{2,1,0:T(8,128)(2,1)} %after.45), channel_id=1, source_target_pairs={{0,2},{2,0},{1,3},{3,1},{4,6},{6,4},{5,7},{7,5},{8,10},{10,8},{9,1... | collective-permute-start | bytes 4718600 | tf_op jit(solution)/shard_map/ppermute | solution.py:42
  151.4 36.5 %collective-permute-start.13 = (bf16[4,128,1536]{2,1,0:T(8,128)(2,1)}, bf16[4,128,1536]{2,1,0:T(8,128)(2,1)S(1)}, u32[]{:S(2)}, u32[]{:S(2)}) collective-permute-start(bf16[4,128,1536]{2,1,0:T(8,128)(2,1)} %after.45), channel_id=1, source_target_pairs={{0,4},{4,0},{1,5},{5,1},{2,6},{6,2},{3,7},{7,3},{8,12},{12,8},{9,1... | collective-permute-start | bytes 4718600 | tf_op jit(solution)/shard_map/ppermute | solution.py:42
  212.1 28.9 %collective-permute-start.19 = (bf16[128,768]{1,0:T(8,128)(2,1)}, bf16[128,768]{1,0:T(8,128)(2,1)S(1)}, u32[]{:S(2)}, u32[]{:S(2)}) collective-permute-start(bf16[128,768]{1,0:T(8,128)(2,1)} %after.51), channel_id=1, source_target_pairs={{0,16},{8,24},{16,0},{24,8},{1,17},{9,25},{17,1},{25,9},{2,18},{10... | collective-permute-start | bytes 589832 | tf_op jit(solution)/shard_map/ppermute | solution.py:108
  212.9 28.1 %collective-permute-start.20 = (bf16[128,768]{1,0:T(8,128)(2,1)}, bf16[128,768]{1,0:T(8,128)(2,1)}, u32[]{:S(2)}, u32[]{:S(2)}) collective-permute-start(bf16[128,768]{1,0:T(8,128)(2,1)} %after.52), channel_id=1, source_target_pairs={{0,24},{8,16},{16,8},{24,0},{1,25},{9,17},{17,9},{25,1},{2,26},{10... | collective-permute-start | bytes 589832 | tf_op jit(solution)/shard_map/ppermute | solution.py:108
  269.7 34.7 %collective-permute-start.23 = (bf16[2,128,768]{2,1,0:T(8,128)(2,1)}, bf16[2,128,768]{2,1,0:T(8,128)(2,1)S(1)}, u32[]{:S(2)}, u32[]{:S(2)}) collective-permute-start(bf16[2,128,768]{2,1,0:T(8,128)(2,1)} %after.54), channel_id=1, source_target_pairs={{0,4},{4,0},{1,5},{5,1},{2,6},{6,2},{3,7},{7,3},{8,12},{12,8},{9,1... | collective-permute-start | bytes 1179656 | tf_op jit(solution)/shard_map/ppermute | solution.py:42
  272.1 32.4 %collective-permute-start.24 = (bf16[2,128,768]{2,1,0:T(8,128)(2,1)}, bf16[2,128,768]{2,1,0:T(8,128)(2,1)S(1)}, u32[]{:S(2)}, u32[]{:S(2)}) collective-permute-start(bf16[2,128,768]{2,1,0:T(8,128)(2,1)} %after.55), channel_id=1, source_target_pairs={{0,2},{2,0},{1,3},{3,1},{4,6},{6,4},{5,7},{7,5},{8,10},{10,8},{9,1... | collective-permute-start | bytes 1179656 | tf_op jit(solution)/shard_map/ppermute | solution.py:42
  319.7 285.8 %reduce-scatter.5.cloned.1.call-start = ((), (), s32[]{:S(2)}) async-start(), calls=%async_computation.3 | async-start | bytes 9437184 | tf_op jit(solution)/shard_map/reduce_scatter | solution.py:642
  388.5 48.5 %collective-permute-start.31 = (bf16[128,1024]{1,0:T(8,128)(2,1)}, bf16[128,1024]{1,0:T(8,128)(2,1)}, u32[]{:S(2)}, u32[]{:S(2)}) collective-permute-start(bf16[128,1024]{1,0:T(8,128)(2,1)} %after.60), channel_id=1, source_target_pairs={{0,8},{8,0},{16,24},{24,16},{1,9},{9,1},{17,25},{25,17},{2,10},{10... | collective-permute-start | bytes 786440 | tf_op jit(solution)/shard_map/ppermute | solution.py:108
  395.1 43.1 %collective-permute-start.32 = (bf16[128,1024]{1,0:T(8,128)(2,1)}, bf16[128,1024]{1,0:T(8,128)(2,1)}, u32[]{:S(2)}, u32[]{:S(2)}) collective-permute-start(bf16[128,1024]{1,0:T(8,128)(2,1)} %after.61), channel_id=1, source_target_pairs={{0,16},{8,24},{16,0},{24,8},{1,17},{9,25},{17,1},{25,9},{2,18},{10... | collective-permute-start | bytes 786440 | tf_op jit(solution)/shard_map/ppermute | solution.py:108
  395.1 43.8 %collective-permute-start.33 = (bf16[128,1024]{1,0:T(8,128)(2,1)}, bf16[128,1024]{1,0:T(8,128)(2,1)}, u32[]{:S(2)}, u32[]{:S(2)}) collective-permute-start(bf16[128,1024]{1,0:T(8,128)(2,1)} %after.62), channel_id=1, source_target_pairs={{0,24},{8,16},{16,8},{24,0},{1,25},{9,17},{17,9},{25,1},{2,26},{10... | collective-permute-start | bytes 786440 | tf_op jit(solution)/shard_map/ppermute | solution.py:108
  414.5 47.5 %collective-permute-start.35 = (bf16[4,128,1536]{2,1,0:T(8,128)(2,1)}, bf16[4,128,1536]{2,1,0:T(8,128)(2,1)S(1)}, u32[]{:S(2)}, u32[]{:S(2)}) collective-permute-start(bf16[4,128,1536]{2,1,0:T(8,128)(2,1)} %after.64), channel_id=1, source_target_pairs={{0,4},{4,0},{1,5},{5,1},{2,6},{6,2},{3,7},{7,3},{8,12},{12,8},{9,1... | collective-permute-start | bytes 4718600 | tf_op jit(solution)/shard_map/ppermute | solution.py:42
  416.9 45.1 %collective-permute-start.34 = (bf16[4,128,1536]{2,1,0:T(8,128)(2,1)}, bf16[4,128,1536]{2,1,0:T(8,128)(2,1)S(1)}, u32[]{:S(2)}, u32[]{:S(2)}) collective-permute-start(bf16[4,128,1536]{2,1,0:T(8,128)(2,1)} %after.63), channel_id=1, source_target_pairs={{0,2},{2,0},{1,3},{3,1},{4,6},{6,4},{5,7},{7,5},{8,10},{10,8},{9,1... | collective-permute-start | bytes 4718600 | tf_op jit(solution)/shard_map/ppermute | solution.py:42
  463.7 34.0 %collective-permute-start.41 = (bf16[4,128,768]{2,1,0:T(8,128)(2,1)}, bf16[4,128,768]{2,1,0:T(8,128)(2,1)}, u32[]{:S(2)}, u32[]{:S(2)}) collective-permute-start(bf16[4,128,768]{2,1,0:T(8,128)(2,1)} %after.70), channel_id=1, source_target_pairs={{0,2},{2,0},{1,3},{3,1},{4,6},{6,4},{5,7},{7,5},{8,10},{10,8},{9,1... | collective-permute-start | bytes 2359304 | tf_op jit(solution)/shard_map/ppermute | solution.py:42
  464.8 32.9 %collective-permute-start.42 = (bf16[4,128,768]{2,1,0:T(8,128)(2,1)}, bf16[4,128,768]{2,1,0:T(8,128)(2,1)}, u32[]{:S(2)}, u32[]{:S(2)}) collective-permute-start(bf16[4,128,768]{2,1,0:T(8,128)(2,1)} %after.71), channel_id=1, source_target_pairs={{0,4},{4,0},{1,5},{5,1},{2,6},{6,2},{3,7},{7,3},{8,12},{12,8},{9,1... | collective-permute-start | bytes 2359304 | tf_op jit(solution)/shard_map/ppermute | solution.py:42
  (129 other events, 1223.1 us)
Sparse Core Ops, SparseCore 0:
  9.6 140.2 all-gather.4
  151.5 96.0 all-gather.6
  319.9 109.8 reduce-scatter.2
  498.7 106.7 reduce-scatter.4

commit v4 on v3

--- a/solution.py
+++ b/solution.py
@@ -611,21 +611,19 @@
     gated = exchange(pieces(gated_piece), joined[1:])
     stage = [*joined_near[1:], *gated[1:], rows_all]
     gated_near = plane.gather_first(ordered(gated), stage)
+    attention_weight, joined_last = plane.gather_second(joined_near, stage)
+    attention_weight = flat(attention_weight)
     normed, xhat_all = norm_rows(rows_all, row_gain, row_shift)
-    stage = [*gated_near[1:], normed]
+    downward = exchange(pieces(downward_piece), (normed,))
+    stage = [*gated_near[1:], *joined_last, normed]
     gated_weight, last = plane.gather_second(gated_near, stage)
     gated_weight = flat(gated_weight)
-    downward = exchange(pieces(downward_piece), last)
-    attention_weight, joined_last = plane.gather_second(joined_near, last)
-    attention_weight = flat(attention_weight)
-    downward_near = plane.gather_first(ordered(downward), [*downward[1:], *joined_last])
+    joined_out = times(normed, attention_weight, 0, 3 * att_width, F32, downward[1:])
+    activated, silu, slope = gate_up(normed, gated_weight, (joined_out,))
+    downward_near = plane.gather_first(ordered(downward), [*downward[1:], *last])
     downward_weight, last = plane.gather_second(downward_near, downward_near[1:])
     downward_weight = flat(downward_weight)
-    activated, silu, slope = gate_up(normed, gated_weight)
-    joined_out = times(
-        normed, attention_weight, 0, 3 * att_width, F32, (activated, *downward[1:])
-    )
-    mixed_grad = times(back_all, attention_weight, 3, att_width, LOW, (joined_out,))
+    mixed_grad = times(back_all, attention_weight, 3, att_width, LOW, (activated,))
     mixed, joined_grad, bias_grad = attention(joined_out, mixed_grad, bias_here, downward_near[1:])
 
     def fold(term):
@@ -665,7 +663,7 @@
     downward_total, last = plane.sum_second(downward_known, stage)
     stage = [*gated_home[1:], *last]
     own_grad = scatter_rows(after(normed_grad_part, branch, *stage)).astype(F32)
-    downward_home = homeward(downward_total, stage)
+    downward_home = homeward(downward_total, last)
     sums = sums_low + sums_high
     branch = branch.astype(F32)
 

time: 626 us -> 626 us (level)
  waiting for transfers between devices: 177 us -> 170 us
    ppermute x24, waiting for transfers between devices: 23 us -> 4.59 us  [swap(): return lax.ppermute(value, axis, SWAP)]
    ppermute x18, waiting for transfers between devices: 120 us -> 135 us  [exchange(): lax.ppermute(block, 'a', [(i, i ^ bit) for i in range(QUAD)])]
    ppermute x18, starting transfers between devices: 53.1 us -> 60.9 us  [exchange(): lax.ppermute(block, 'a', [(i, i ^ bit) for i in range(QUAD)])]
    unnamed x198 -> x178, local copies, waits for them, and re-layouts: 15.2 us -> 13.9 us
  transfers between devices with their start and end apart: 55 -> 55, of which waited for: 26 -> 23; matrix products, arithmetic and copies ran while one was open for 18% -> 19% of each run, Pallas kernels for 28% -> 28%
where the time goes in v4:
time: 626 us; the launch traced here: 619 us
  Pallas kernels  189 us (30%)
  waiting for transfers between devices  170 us (27%)
  starting transfers between devices  105 us (17%)
  other arithmetic  72.9 us (12%)
  local copies, waits for them, and re-layouts  63.7 us (10%)
  between operations  17.8 us (3%)
    pallas_call x12, Pallas kernels, launch(): pl.pallas_call(run, grid_spec=pltpu.PrefetchScalarGridSpec(num_scalar_pre...  189 us
    ppermute x18, waiting for transfers between devices, exchange(): lax.ppermute(block, 'a', [(i, i ^ bit) for i in range(QUAD)])  135 us
    ppermute x18, starting transfers between devices, exchange(): lax.ppermute(block, 'a', [(i, i ^ bit) for i in range(QUAD)])  60.9 us
    ppermute x24, starting transfers between devices, swap(): return lax.ppermute(value, axis, SWAP)  24.6 us
    convert_element_type x5, other arithmetic, adamw(): return (updated, moment, variance, updated.astype(LOW))  17.4 us
    dynamic_update_slice x12, local copies, waits for them, and re-layouts, gather_second(): whole = lax.dynamic_update_slice(whole, block, (first, at, 0))  16.8 us
    ppermute x5, waiting for transfers between devices, sum_small(): value = value + lax.ppermute(value, axis, pairs)  16 us
    unnamed x178, local copies, waits for them, and re-layouts  13.9 us
  transfers between devices with their start and end apart: 55, of which 23 were waited for; matrix products, arithmetic and copies ran while one was open for 19% of the time, Pallas kernels for 28%

profile of v4, /device:TPU:0, one launch (start us, length us, event | category | flops | bytes accessed | tf_op | source)
XLA Modules:
  0.0 619.0 jit_solution(15028330179409729495)
XLA Ops:
  40.7 16.2 %collective-permute-done.4.refs_1_ = bf16[128,1024]{1,0:T(8,128)(2,1)S(1)} collective-permute-done((bf16[128,1024]{1,0:T(8,128)(2,1)}, bf16[128,1024]{1,0:T(8,128)(2,1)S(1)}, u32[]{:S(2)}, u32[]{:S(2)}) %collective-permute-start.4) | collective-permute-done | bytes 262176 | tf_op jit(solution)/shard_map/ppermute | solution.py:108
  56.9 12.8 %collective-permute-done.5.refs_2_ = bf16[128,1024]{1,0:T(8,128)(2,1)S(1)} collective-permute-done((bf16[128,1024]{1,0:T(8,128)(2,1)}, bf16[128,1024]{1,0:T(8,128)(2,1)S(1)}, u32[]{:S(2)}, u32[]{:S(2)}) %collective-permute-start.5) | collective-permute-done | bytes 262176 | tf_op jit(solution)/shard_map/ppermute | solution.py:108
  71.6 20.2 %collective-permute-start.9 = (bf16[128,1536]{1,0:T(8,128)(2,1)}, bf16[128,1536]{1,0:T(8,128)(2,1)S(1)}, u32[]{:S(2)}, u32[]{:S(2)}) collective-permute-start(bf16[128,1536]{1,0:T(8,128)(2,1)} %after.42), channel_id=1, source_target_pairs={{0,8},{8,0},{16,24},{24,16},{1,9},{9,1},{17,25},{25,17},{2,10},{10... | collective-permute-start | bytes 1179656 | tf_op jit(solution)/shard_map/ppermute | solution.py:108
  99.3 14.7 %collective-permute-done.9.refs_3_ = bf16[128,1536]{1,0:T(8,128)(2,1)S(1)} collective-permute-done((bf16[128,1536]{1,0:T(8,128)(2,1)}, bf16[128,1536]{1,0:T(8,128)(2,1)S(1)}, u32[]{:S(2)}, u32[]{:S(2)}) %collective-permute-start.9) | collective-permute-done | bytes 393248 | tf_op jit(solution)/shard_map/ppermute | solution.py:108
  113.9 24.7 %collective-permute-done.10.refs_4_ = bf16[128,1536]{1,0:T(8,128)(2,1)S(1)} collective-permute-done((bf16[128,1536]{1,0:T(8,128)(2,1)}, bf16[128,1536]{1,0:T(8,128)(2,1)S(1)}, u32[]{:S(2)}, u32[]{:S(2)}) %collective-permute-start.10) | collective-permute-done | bytes 393248 | tf_op jit(solution)/shard_map/ppermute | solution.py:108
  156.9 13.5 %norm_rows.1 = (bf16[2048,2048]{1,0:T(8,128)(2,1)}, bf16[2048,2048]{1,0:T(8,128)(2,1)}) custom-call(f32[1,2048]{1,0:T(1,128)} %get-tuple-element.272.refs_0_, f32[1,2048]{1,0:T(1,128)} %get-tuple-element.271.refs_1_, bf16[2048,2048]{1,0:T(8,128)(2,1)} %bitcast.242), custom_call_target="tpu_custom_call" | custom-call | flops 83886080 | bytes 25182208 | tf_op jit(solution)/shard_map/norm_rows/pallas_call | solution.py:59
  180.6 12.5 %collective-permute-done.14.refs_2_.refs_1_ = bf16[128,768]{1,0:T(8,128)(2,1)S(1)} collective-permute-done((bf16[128,768]{1,0:T(8,128)(2,1)}, bf16[128,768]{1,0:T(8,128)(2,1)S(1)}, u32[]{:S(2)}, u32[]{:S(2)}) %collective-permute-start.14) | collective-permute-done | bytes 196640 | tf_op jit(solution)/shard_map/ppermute | solution.py:108
  194.3 8.5 %collective-permute-done.15.refs_3_.refs_2_ = bf16[128,768]{1,0:T(8,128)(2,1)} collective-permute-done((bf16[128,768]{1,0:T(8,128)(2,1)}, bf16[128,768]{1,0:T(8,128)(2,1)}, u32[]{:S(2)}, u32[]{:S(2)}) %collective-permute-start.15) | collective-permute-done | bytes 196640 | tf_op jit(solution)/shard_map/ppermute | solution.py:108
  219.7 11.4 %times.2.refs_2_ = f32[2048,768]{1,0:T(8,128)} custom-call(bf16[2048,2048]{1,0:T(8,128)(2,1)} %get-tuple-element.35.refs_1_.refs_0_.refs_5_, bf16[2048,1024]{1,0:T(8,128)(2,1)} %bitcast.24.refs_1_.refs_2_, bf16[128,768]{1,0:T(8,128)(2,1)} %copy-done.69, bf16[128,768]{1,0:T(8,128)(2,1)} %collective-permute-done.15.refs_3_.refs_2_, ...), custom_call_target="tpu_custom_call" | custom-call | flops 6442450944 | bytes 18874368 | tf_op jit(solution)/shard_map/times/pallas_call | solution.py:59
  243.0 18.9 %gate_up.1 = (bf16[2048,768]{1,0:T(8,128)(2,1)}, f32[2048,768]{1,0:T(8,128)}, f32[2048,768]{1,0:T(8,128)}) custom-call(bf16[2048,2048]{1,0:T(8,128)(2,1)} %get-tuple-element.35.refs_1_.refs_0_.refs_5_, bf16[2048,1536]{1,0:T(8,128)(2,1)} %bitcast.33.refs_1_.refs_3_, f32[2048,768]{1,0:T(8,128)} %times.2.refs_2_), custom_call_target="tpu_custom_call" | custom-call | flops 12884901888 | bytes 30408704 | tf_op jit(solution)/shard_map/gate_up/pallas_call | solution.py:59
  273.7 29.3 %attention_both_ways.1 = (bf16[4,2,2,128,256]{4,3,2,1,0:T(8,128)(2,1)}, bf16[4,2,2,128,768]{4,3,2,1,0:T(8,128)(2,1)}, f32[8,768]{1,0:T(8,128)}) custom-call(f32[256,256]{1,0:T(8,128)} %fusion.31.refs_0_, f32[256,256]{1,0:T(8,128)} %copy.91.refs_1_, f32[256,256]{1,0:T(8,128)} %copy.92.refs_2_, f32[256,256]{1,0:T(8,128)} %copy.93.refs_3_, f32[1,768]{1,0:T(1,128)} %bitcast.286, ...), custom_call_target="tpu_custom_call" | custom-call | flops 7516192768 | bytes 12610560 | tf_op jit(solution)/shard_map/attention_both_ways/pallas_call | solution.py:59
  307.1 13.6 %product_sum.3.refs_4_ = bf16[2048,2048]{1,0:T(8,128)(2,1)} custom-call(bf16[2048,256]{1,0:T(8,128)(2,1)} %bitcast.274, bf16[2048,768]{1,0:T(8,128)(2,1)} %get-tuple-element.36.refs_2_.refs_1_.refs_0_, bf16[2048,1024]{1,0:T(8,128)(2,1)} %bitcast.24.refs_1_.refs_2_, bf16[2048,768]{1,0:T(8,128)(2,1)} %bitcast.256), custom_call_target="tpu_custom_call" | custom-call | flops 8589934592 | bytes 19922944 | tf_op jit(solution)/shard_map/product_sum/pallas_call | solution.py:59
  320.8 14.3 %weight_term.3.refs_4_ = bf16[2048,1024]{1,0:T(8,128)(2,1)} custom-call(bf16[2048,768]{1,0:T(8,128)(2,1)} %bitcast.253, bf16[2048,2048]{1,0:T(8,128)(2,1)} %get-tuple-element.35.refs_1_.refs_0_.refs_5_, bf16[2048,256]{1,0:T(8,128)(2,1)} %bitcast.275, bf16[2048,2048]{1,0:T(8,128)(2,1)} %bitcast.246, bf16[2048,2048]{1,0:T(8,128)(2,1)} %product_sum.3.refs_4_), custom_call_target="tpu_custom_call" | custom-call | flops 8589934592 | bytes 25165824 | tf_op jit(solution)/shard_map/weight_term/pallas_call | solution.py:59
  340.7 14.3 %gate_up_back.1.refs_0_.refs_1_ = bf16[2048,1536]{1,0:T(8,128)(2,1)} custom-call(bf16[2048,2048]{1,0:T(8,128)(2,1)} %bitcast.247, bf16[2048,768]{1,0:T(8,128)(2,1)} %bitcast.257, f32[2048,768]{1,0:T(8,128)} %get-tuple-element.39.refs_2_, f32[2048,768]{1,0:T(8,128)} %get-tuple-element.40.refs_3_, bf16[2048,1024]{1,0:T(8,128)(2,1)} %weight_term.3.refs_4_), custom_call_target="tpu_custom_call" | custom-call | flops 6442450944 | bytes 30408704 | tf_op jit(solution)/shard_map/gate_up_back/pallas_call | solution.py:59
  360.7 18.5 %weight_term.4.refs_2_ = bf16[2048,1536]{1,0:T(8,128)(2,1)} custom-call(bf16[2048,1536]{1,0:T(8,128)(2,1)} %gate_up_back.1.refs_0_.refs_1_, bf16[2048,2048]{1,0:T(8,128)(2,1)} %get-tuple-element.35.refs_1_.refs_0_.refs_5_, bf16[2,128,1024]{2,1,0:T(8,128)(2,1)} %copy-done.32, bf16[2,128,1024]{2,1,0:T(8,128)(2,1)} %copy-done.33), custom_call_target="tpu_custom_call" | custom-call | flops 12884901888 | bytes 20971520 | tf_op jit(solution)/shard_map/weight_term/pallas_call | solution.py:59
  389.6 10.6 %collective-permute-start.31 = (bf16[128,1024]{1,0:T(8,128)(2,1)}, bf16[128,1024]{1,0:T(8,128)(2,1)}, u32[]{:S(2)}, u32[]{:S(2)}) collective-permute-start(bf16[128,1024]{1,0:T(8,128)(2,1)} %after.60), channel_id=1, source_target_pairs={{0,8},{8,0},{16,24},{24,16},{1,9},{9,1},{17,25},{25,17},{2,10},{10... | collective-permute-start | bytes 786440 | tf_op jit(solution)/shard_map/ppermute | solution.py:108
  402.6 10.9 %weight_term.5.refs_5_ = bf16[2048,768]{1,0:T(8,128)(2,1)} custom-call(bf16[2048,768]{1,0:T(8,128)(2,1)} %get-tuple-element.36.refs_2_.refs_1_.refs_0_, bf16[2048,2048]{1,0:T(8,128)(2,1)} %bitcast.248, bf16[2048,1536]{1,0:T(8,128)(2,1)} %weight_term.4.refs_2_, bf16[4,128,1024]{2,1,0:T(8,128)(2,1)} %copy-done.4, bf16[4,128,1024]{2,1,0:T(8,128)(2,1)} %copy-done.6), custom_call_target="tpu_custom_call" | custom-call | flops 6442450944 | bytes 14680064 | tf_op jit(solution)/shard_map/weight_term/pallas_call | solution.py:59
  423.0 18.9 %product_sum.4 = (bf16[2048,2048]{1,0:T(8,128)(2,1)}, f32[16,2048]{1,0:T(8,128)}) custom-call(bf16[2048,768]{1,0:T(8,128)(2,1)} %bitcast.254, bf16[2048,1536]{1,0:T(8,128)(2,1)} %gate_up_back.1.refs_0_.refs_1_, bf16[2048,1024]{1,0:T(8,128)(2,1)} %bitcast.24.refs_1_.refs_2_, bf16[2048,1536]{1,0:T(8,128)(2,1)} %bitcast.33.refs_1_.refs_3_, ...), custom_call_target="tpu_custom_call" | custom-call | flops 9663676416 | bytes 36831232 | tf_op jit(solution)/shard_map/product_sum/pallas_call | solution.py:59
  444.0 18.9 %product_sum.5 = (bf16[2048,2048]{1,0:T(8,128)(2,1)}, f32[16,2048]{1,0:T(8,128)}) custom-call(bf16[2048,768]{1,0:T(8,128)(2,1)} %bitcast.255, bf16[2048,1536]{1,0:T(8,128)(2,1)} %gate_up_back.1.refs_0_.refs_1_, bf16[2048,1024]{1,0:T(8,128)(2,1)} %bitcast.24.refs_1_.refs_2_, ...), custom_call_target="tpu_custom_call", output_to_operand_aliasing={{0}: (5, {})} | custom-call | flops 9663676416 | bytes 45219840 | tf_op jit(solution)/shard_map/product_sum/pallas_call | solution.py:59
  477.6 9.5 %collective-permute-done.38.refs_2_ = bf16[128,1536]{1,0:T(8,128)(2,1)S(1)} collective-permute-done((bf16[128,1536]{1,0:T(8,128)(2,1)}, bf16[128,1536]{1,0:T(8,128)(2,1)S(1)}, u32[]{:S(2)}, u32[]{:S(2)}) %collective-permute-start.38) | collective-permute-done | bytes 393248 | tf_op jit(solution)/shard_map/ppermute | solution.py:108
  487.1 10.3 %collective-permute-done.39.refs_3_ = bf16[128,1536]{1,0:T(8,128)(2,1)S(1)} collective-permute-done((bf16[128,1536]{1,0:T(8,128)(2,1)}, bf16[128,1536]{1,0:T(8,128)(2,1)S(1)}, u32[]{:S(2)}, u32[]{:S(2)}) %collective-permute-start.39) | collective-permute-done | bytes 393248 | tf_op jit(solution)/shard_map/ppermute | solution.py:108
  521.8 10.2 %collective-permute-done.43 = bf16[128,768]{1,0:T(8,128)(2,1)S(1)} collective-permute-done((bf16[128,768]{1,0:T(8,128)(2,1)}, bf16[128,768]{1,0:T(8,128)(2,1)S(1)}, u32[]{:S(2)}, u32[]{:S(2)}) %collective-permute-start.43) | collective-permute-done | bytes 196640 | tf_op jit(solution)/shard_map/ppermute | solution.py:108
  532.0 10.7 %collective-permute-done.44 = bf16[128,768]{1,0:T(8,128)(2,1)S(1)} collective-permute-done((bf16[128,768]{1,0:T(8,128)(2,1)}, bf16[128,768]{1,0:T(8,128)(2,1)S(1)}, u32[]{:S(2)}, u32[]{:S(2)}) %collective-permute-start.44) | collective-permute-done | bytes 196640 | tf_op jit(solution)/shard_map/ppermute | solution.py:108
  561.0 7.8 %collective-permute-start.49 = (f32[8,2048]{1,0:T(8,128)S(1)}, f32[8,2048]{1,0:T(8,128)S(1)}, u32[]{:S(2)}, u32[]{:S(2)}) collective-permute-start(f32[8,2048]{1,0:T(8,128)S(1)} %add.425), channel_id=1, source_target_pairs={{0,8},{8,0},{16,24},{24,16},{1,9},{9,1},{17,25},{25,17},{2,10},{10... | collective-permute-start | bytes 196616 | tf_op jit(solution)/shard_map/ppermute | solution.py:197
  (459 shorter events, 249.8 us)
Async XLA Ops:
  7.2 141.8 %all-gather.5.cloned.1.call-start = ((), (), s32[]{:S(2)}) async-start(), calls=%async_computation.4 | async-start | bytes 9437184 | tf_op jit(solution)/shard_map/all_gather | solution.py:603
  8.0 254.0 %all-gather.7.cloned.1.call-start = ((), (), s32[]{:S(2)}) async-start(), calls=%async_computation.5 | async-start | bytes 9437184 | tf_op jit(solution)/shard_map/all_gather | solution.py:604
  8.7 488.8 %reduce-scatter.3.cloned.1.call-start = ((), (), s32[]{:S(2)}) async-start(), calls=%async_computation.2 | async-start | bytes 9437184 | tf_op jit(solution)/shard_map/reduce_scatter | solution.py:640
  35.0 34.7 %collective-permute-start.5 = (bf16[128,1024]{1,0:T(8,128)(2,1)}, bf16[128,1024]{1,0:T(8,128)(2,1)S(1)}, u32[]{:S(2)}, u32[]{:S(2)}) collective-permute-start(bf16[128,1024]{1,0:T(8,128)(2,1)} %after.39), channel_id=1, source_target_pairs={{0,16},{8,24},{16,0},{24,8},{1,17},{9,25},{17,1},{25,9},{2,18},{10... | collective-permute-start | bytes 786440 | tf_op jit(solution)/shard_map/ppermute | solution.py:108
  38.0 32.9 %collective-permute-start.6 = (bf16[128,1024]{1,0:T(8,128)(2,1)}, bf16[128,1024]{1,0:T(8,128)(2,1)S(1)}, u32[]{:S(2)}, u32[]{:S(2)}) collective-permute-start(bf16[128,1024]{1,0:T(8,128)(2,1)} %after.40), channel_id=1, source_target_pairs={{0,24},{8,16},{16,8},{24,0},{1,25},{9,17},{17,9},{25,1},{2,26},{10... | collective-permute-start | bytes 786440 | tf_op jit(solution)/shard_map/ppermute | solution.py:108
  71.6 42.3 %collective-permute-start.9 = (bf16[128,1536]{1,0:T(8,128)(2,1)}, bf16[128,1536]{1,0:T(8,128)(2,1)S(1)}, u32[]{:S(2)}, u32[]{:S(2)}) collective-permute-start(bf16[128,1536]{1,0:T(8,128)(2,1)} %after.42), channel_id=1, source_target_pairs={{0,8},{8,0},{16,24},{24,16},{1,9},{9,1},{17,25},{25,17},{2,10},{10... | collective-permute-start | bytes 1179656 | tf_op jit(solution)/shard_map/ppermute | solution.py:108
  91.9 46.8 %collective-permute-start.10 = (bf16[128,1536]{1,0:T(8,128)(2,1)}, bf16[128,1536]{1,0:T(8,128)(2,1)S(1)}, u32[]{:S(2)}, u32[]{:S(2)}) collective-permute-start(bf16[128,1536]{1,0:T(8,128)(2,1)} %after.43), channel_id=1, source_target_pairs={{0,16},{8,24},{16,0},{24,8},{1,17},{9,25},{17,1},{25,9},{2,18},{10... | collective-permute-start | bytes 1179656 | tf_op jit(solution)/shard_map/ppermute | solution.py:108
  91.9 46.8 %collective-permute-start.11 = (bf16[128,1536]{1,0:T(8,128)(2,1)}, bf16[128,1536]{1,0:T(8,128)(2,1)S(1)}, u32[]{:S(2)}, u32[]{:S(2)}) collective-permute-start(bf16[128,1536]{1,0:T(8,128)(2,1)} %after.44), channel_id=1, source_target_pairs={{0,24},{8,16},{16,8},{24,0},{1,25},{9,17},{17,9},{25,1},{2,26},{10... | collective-permute-start | bytes 1179656 | tf_op jit(solution)/shard_map/ppermute | solution.py:108
  96.2 46.0 %collective-permute-start.8 = (bf16[4,128,1024]{2,1,0:T(8,128)(2,1)}, bf16[4,128,1024]{2,1,0:T(8,128)(2,1)S(1)}, u32[]{:S(2)}, u32[]{:S(2)}) collective-permute-start(bf16[4,128,1024]{2,1,0:T(8,128)(2,1)} %after.41), channel_id=1, source_target_pairs={{0,4},{4,0},{1,5},{5,1},{2,6},{6,2},{3,7},{7,3},{8,12},{12,8},{9,1... | collective-permute-start | bytes 3145736 | tf_op jit(solution)/shard_map/ppermute | solution.py:42
  96.7 45.5 %collective-permute-start.7 = (bf16[4,128,1024]{2,1,0:T(8,128)(2,1)}, bf16[4,128,1024]{2,1,0:T(8,128)(2,1)S(1)}, u32[]{:S(2)}, u32[]{:S(2)}) collective-permute-start(bf16[4,128,1024]{2,1,0:T(8,128)(2,1)} %after.41), channel_id=1, source_target_pairs={{0,2},{2,0},{1,3},{3,1},{4,6},{6,4},{5,7},{7,5},{8,10},{10,8},{9,1... | collective-permute-start | bytes 3145736 | tf_op jit(solution)/shard_map/ppermute | solution.py:42
  149.0 66.8 %collective-permute-start.18 = (bf16[4,128,1536]{2,1,0:T(8,128)(2,1)}, bf16[4,128,1536]{2,1,0:T(8,128)(2,1)}, u32[]{:S(2)}, u32[]{:S(2)}) collective-permute-start(bf16[4,128,1536]{2,1,0:T(8,128)(2,1)} %after.50), channel_id=1, source_target_pairs={{0,4},{4,0},{1,5},{5,1},{2,6},{6,2},{3,7},{7,3},{8,12},{12,8},{9,1... | collective-permute-start | bytes 4718600 | tf_op jit(solution)/shard_map/ppermute | solution.py:42
  151.1 62.7 %collective-permute-start.17 = (bf16[4,128,1536]{2,1,0:T(8,128)(2,1)}, bf16[4,128,1536]{2,1,0:T(8,128)(2,1)}, u32[]{:S(2)}, u32[]{:S(2)}) collective-permute-start(bf16[4,128,1536]{2,1,0:T(8,128)(2,1)} %after.50), channel_id=1, source_target_pairs={{0,2},{2,0},{1,3},{3,1},{4,6},{6,4},{5,7},{7,5},{8,10},{10,8},{9,1... | collective-permute-start | bytes 4718600 | tf_op jit(solution)/shard_map/ppermute | solution.py:42
  236.5 33.9 %collective-permute-start.22 = (bf16[4,128,768]{2,1,0:T(8,128)(2,1)}, bf16[4,128,768]{2,1,0:T(8,128)(2,1)}, u32[]{:S(2)}, u32[]{:S(2)}) collective-permute-start(bf16[4,128,768]{2,1,0:T(8,128)(2,1)} %after.53), channel_id=1, source_target_pairs={{0,4},{4,0},{1,5},{5,1},{2,6},{6,2},{3,7},{7,3},{8,12},{12,8},{9,1... | collective-permute-start | bytes 2359304 | tf_op jit(solution)/shard_map/ppermute | solution.py:42
  237.5 31.0 %collective-permute-start.21 = (bf16[4,128,768]{2,1,0:T(8,128)(2,1)}, bf16[4,128,768]{2,1,0:T(8,128)(2,1)}, u32[]{:S(2)}, u32[]{:S(2)}) collective-permute-start(bf16[4,128,768]{2,1,0:T(8,128)(2,1)} %after.53), channel_id=1, source_target_pairs={{0,2},{2,0},{1,3},{3,1},{4,6},{6,4},{5,7},{7,5},{8,10},{10,8},{9,1... | collective-permute-start | bytes 2359304 | tf_op jit(solution)/shard_map/ppermute | solution.py:42
  270.3 35.0 %collective-permute-start.23 = (bf16[2,128,768]{2,1,0:T(8,128)(2,1)}, bf16[2,128,768]{2,1,0:T(8,128)(2,1)S(1)}, u32[]{:S(2)}, u32[]{:S(2)}) collective-permute-start(bf16[2,128,768]{2,1,0:T(8,128)(2,1)} %after.54), channel_id=1, source_target_pairs={{0,4},{4,0},{1,5},{5,1},{2,6},{6,2},{3,7},{7,3},{8,12},{12,8},{9,1... | collective-permute-start | bytes 1179656 | tf_op jit(solution)/shard_map/ppermute | solution.py:42
  272.8 32.6 %collective-permute-start.24 = (bf16[2,128,768]{2,1,0:T(8,128)(2,1)}, bf16[2,128,768]{2,1,0:T(8,128)(2,1)S(1)}, u32[]{:S(2)}, u32[]{:S(2)}) collective-permute-start(bf16[2,128,768]{2,1,0:T(8,128)(2,1)} %after.55), channel_id=1, source_target_pairs={{0,2},{2,0},{1,3},{3,1},{4,6},{6,4},{5,7},{7,5},{8,10},{10,8},{9,1... | collective-permute-start | bytes 1179656 | tf_op jit(solution)/shard_map/ppermute | solution.py:42
  320.8 284.6 %reduce-scatter.5.cloned.1.call-start = ((), (), s32[]{:S(2)}) async-start(), calls=%async_computation.3 | async-start | bytes 9437184 | tf_op jit(solution)/shard_map/reduce_scatter | solution.py:640
  384.1 31.9 %collective-permute-start.30 = (bf16[2,128,1536]{2,1,0:T(8,128)(2,1)}, bf16[2,128,1536]{2,1,0:T(8,128)(2,1)S(1)}, u32[]{:S(2)}, u32[]{:S(2)}) collective-permute-start(bf16[2,128,1536]{2,1,0:T(8,128)(2,1)} %after.59), channel_id=1, source_target_pairs={{0,2},{2,0},{1,3},{3,1},{4,6},{6,4},{5,7},{7,5},{8,10},{10,8},{9,1... | collective-permute-start | bytes 2359304 | tf_op jit(solution)/shard_map/ppermute | solution.py:42
  385.2 30.8 %collective-permute-start.29 = (bf16[2,128,1536]{2,1,0:T(8,128)(2,1)}, bf16[2,128,1536]{2,1,0:T(8,128)(2,1)}, u32[]{:S(2)}, u32[]{:S(2)}) collective-permute-start(bf16[2,128,1536]{2,1,0:T(8,128)(2,1)} %after.58), channel_id=1, source_target_pairs={{0,4},{4,0},{1,5},{5,1},{2,6},{6,2},{3,7},{7,3},{8,12},{12,8},{9,1... | collective-permute-start | bytes 2359304 | tf_op jit(solution)/shard_map/ppermute | solution.py:42
  389.6 52.3 %collective-permute-start.31 = (bf16[128,1024]{1,0:T(8,128)(2,1)}, bf16[128,1024]{1,0:T(8,128)(2,1)}, u32[]{:S(2)}, u32[]{:S(2)}) collective-permute-start(bf16[128,1024]{1,0:T(8,128)(2,1)} %after.60), channel_id=1, source_target_pairs={{0,8},{8,0},{16,24},{24,16},{1,9},{9,1},{17,25},{25,17},{2,10},{10... | collective-permute-start | bytes 786440 | tf_op jit(solution)/shard_map/ppermute | solution.py:108
  400.2 42.8 %collective-permute-start.32 = (bf16[128,1024]{1,0:T(8,128)(2,1)}, bf16[128,1024]{1,0:T(8,128)(2,1)}, u32[]{:S(2)}, u32[]{:S(2)}) collective-permute-start(bf16[128,1024]{1,0:T(8,128)(2,1)} %after.61), channel_id=1, source_target_pairs={{0,16},{8,24},{16,0},{24,8},{1,17},{9,25},{17,1},{25,9},{2,18},{10... | collective-permute-start | bytes 786440 | tf_op jit(solution)/shard_map/ppermute | solution.py:108
  400.2 43.8 %collective-permute-start.33 = (bf16[128,1024]{1,0:T(8,128)(2,1)}, bf16[128,1024]{1,0:T(8,128)(2,1)}, u32[]{:S(2)}, u32[]{:S(2)}) collective-permute-start(bf16[128,1024]{1,0:T(8,128)(2,1)} %after.62), channel_id=1, source_target_pairs={{0,24},{8,16},{16,8},{24,0},{1,25},{9,17},{17,9},{25,1},{2,26},{10... | collective-permute-start | bytes 786440 | tf_op jit(solution)/shard_map/ppermute | solution.py:108
  419.6 47.0 %collective-permute-start.35 = (bf16[4,128,1536]{2,1,0:T(8,128)(2,1)}, bf16[4,128,1536]{2,1,0:T(8,128)(2,1)S(1)}, u32[]{:S(2)}, u32[]{:S(2)}) collective-permute-start(bf16[4,128,1536]{2,1,0:T(8,128)(2,1)} %after.64), channel_id=1, source_target_pairs={{0,4},{4,0},{1,5},{5,1},{2,6},{6,2},{3,7},{7,3},{8,12},{12,8},{9,1... | collective-permute-start | bytes 4718600 | tf_op jit(solution)/shard_map/ppermute | solution.py:42
  422.0 44.6 %collective-permute-start.34 = (bf16[4,128,1536]{2,1,0:T(8,128)(2,1)}, bf16[4,128,1536]{2,1,0:T(8,128)(2,1)S(1)}, u32[]{:S(2)}, u32[]{:S(2)}) collective-permute-start(bf16[4,128,1536]{2,1,0:T(8,128)(2,1)} %after.63), channel_id=1, source_target_pairs={{0,2},{2,0},{1,3},{3,1},{4,6},{6,4},{5,7},{7,5},{8,10},{10,8},{9,1... | collective-permute-start | bytes 4718600 | tf_op jit(solution)/shard_map/ppermute | solution.py:42
  (119 other events, 1032.7 us)
Sparse Core Ops, SparseCore 0:
  9.7 139.2 all-gather.4
  150.6 97.5 all-gather.6
  320.9 114.6 reduce-scatter.2
  498.5 106.8 reduce-scatter.4
